TPU v7x, 256 devices: a whole 4x4x8 slice. The times are simulated.
256 devices in a mesh: dp: 4 (over y_lo, core), lon: 16 (over y_hi, z), lat: 4 (over x).
Axes of the slice: x: 4, y: 4 (y_hi: 2, y_lo: 2; y = y_hi * 2 + y_lo), z: 8, core: 2. Of those that a mesh axis runs over, the one named last changes fastest.
Arguments:
- weather: bfloat16 [4, 8, 24, 384, 192], P('dp', None, 'lat', 'lon'), may hold values from -6 to 6
- cotangent: bfloat16 [4, 8, 24, 384, 192], P('dp', None, 'lat', 'lon'), may hold values from -6 to 6
- norm_gain: float32 [192], replicated, may hold values from 0.1 to 1.9
- qkv_weight: bfloat16 [192, 576], replicated, may hold values from -0.4375 to 0.4375
- proj_weight: bfloat16 [192, 192], replicated, may hold values from -0.4375 to 0.4375
- bias_table: float32 [4, 4, 6, 3312], P(None, 'lat'), may hold values from -3 to 281
Outputs:
- updated: bfloat16 [4, 8, 24, 384, 192], P('dp', None, 'lat', 'lon')
- grad_weather: bfloat16 [4, 8, 24, 384, 192], P('dp', None, 'lat', 'lon')
- grad_qkv: float32 [192, 576], replicated
- grad_proj: float32 [192, 192], replicated
- grad_gain: float32 [192], replicated
- grad_bias: float32 [4, 4, 6, 3312], P(None, 'lat')
All inputs are finite; a program needn't handle non-finite values.
Results may differ from a plain program's by a relative error of at most 0.01.
Values may be sent and summed in bfloat16 or wider, within the bound.
No kernel may reach another device: no remote copies, remote signals or barrier semaphores. Data moves between devices by JAX's collectives and lax.ppermute only.
A program may use at most 192 MiB of HBM per device.

v0:
```python
import jax
import jax.numpy as jnp
from jax import lax
from jax.sharding import PartitionSpec as P

HEADS = 6
WLEV = 2
WLAT = 6
WLON = 12
HD = 32
SHIFT_LEV = 1
SHIFT_LAT = 3
SHIFT_LON = 6


MASKED = -1e30
EPSILON = 1e-05


def passed_along(value, axis, steps):
    count = lax.axis_size(axis)
    pairs = [(source, (source + steps) % count) for source in range(count)]
    return lax.ppermute(value, axis, pairs)


def to_windows(values):
    samples, levels, rows_here, cols_here, channels = values.shape
    shaped = values.reshape(
        samples, levels // WLEV, WLEV, rows_here // WLAT, WLAT, cols_here // WLON, WLON, channels
    )
    shaped = shaped.transpose(1, 0, 3, 5, 2, 4, 6, 7)
    return shaped.reshape(
        levels // WLEV, samples, rows_here // WLAT, cols_here // WLON, WLEV * WLAT * WLON, channels
    )


def from_windows(blocks, samples, levels, rows_here, cols_here):
    channels = blocks.shape[-1]
    shaped = blocks.reshape(
        levels // WLEV, samples, rows_here // WLAT, cols_here // WLON, WLEV, WLAT, WLON, channels
    )
    shaped = shaped.transpose(1, 0, 4, 2, 5, 3, 6, 7)
    return shaped.reshape(samples, levels, rows_here, cols_here, channels)


def make_picker():
    lon_span = 2 * WLON - 1
    offsets = jnp.arange(WLON, dtype=jnp.int32)
    targets = jnp.arange(lon_span, dtype=jnp.int32)
    differ = offsets[None, :, None] - offsets[None, None, :] + WLON - 1
    return (differ == targets[:, None, None]).astype(jnp.float32)


def expand_bias(bias_table, picker):
    lev_windows, lat_windows, head_count, entries = bias_table.shape
    shaped = bias_table.reshape(
        lev_windows, lat_windows, head_count, WLEV, WLEV, WLAT, WLAT, 2 * WLON - 1
    )
    full = jnp.einsum("lahzyuvd,dxw->lahzuxyvw", shaped, picker, precision=lax.Precision.HIGHEST)
    window_size = WLEV * WLAT * WLON
    return full.reshape(lev_windows, lat_windows, head_count, window_size, window_size)


def fold_bias(score_sums, picker):
    lev_windows, lat_windows, head_count, window_size, other_size = score_sums.shape
    shaped = score_sums.reshape(
        lev_windows, lat_windows, head_count, WLEV, WLAT, WLON, WLEV, WLAT, WLON
    )
    folded = jnp.einsum("lahzuxyvw,dxw->lahzyuvd", shaped, picker, precision=lax.Precision.HIGHEST)
    return folded.reshape(
        lev_windows, lat_windows, head_count, WLEV * WLEV * WLAT * WLAT * (2 * WLON - 1)
    )


def attend(operands):
    queries, key_rows, value_rows, grad_rows, bias_full, label_rows = operands
    leading = queries.shape[:-1]
    split_query = queries.reshape(leading + (HEADS, HD))
    split_key = key_rows.reshape(leading + (HEADS, HD))
    split_value = value_rows.reshape(leading + (HEADS, HD))
    split_grad = grad_rows.reshape(leading + (HEADS, HD))
    scores = jnp.einsum(
        "maxihd,maxjhd->maxhij", split_query, split_key, preferred_element_type=jnp.float32
    )
    scores = scores + bias_full[None, :, None]
    allowed = (label_rows[:, :, :, None] == label_rows[:, :, None, :])[None, :, :, None]
    scores = jnp.where(allowed, scores, MASKED)
    highest = jnp.max(scores, axis=-1, keepdims=True)
    exponent = jnp.exp(scores - highest)
    probs = (exponent / jnp.sum(exponent, axis=-1, keepdims=True)).astype(jnp.bfloat16)
    attended = jnp.einsum(
        "maxhij,maxjhd->maxihd", probs, split_value, preferred_element_type=jnp.float32
    ).astype(jnp.bfloat16)
    grad_probs = jnp.einsum(
        "maxihd,maxjhd->maxhij", split_grad, split_value, preferred_element_type=jnp.float32
    )
    grad_value = jnp.einsum(
        "maxhij,maxihd->maxjhd", probs, split_grad, preferred_element_type=jnp.float32
    ).astype(jnp.bfloat16)
    prob_float = probs.astype(jnp.float32)
    grad_scores = prob_float * (
        grad_probs - jnp.sum(prob_float * grad_probs, axis=-1, keepdims=True)
    )
    score_sums = jnp.sum(grad_scores, axis=(0, 2))
    score_round = grad_scores.astype(jnp.bfloat16)
    inv_root = HD ** (-0.5)
    grad_query = (
        jnp.einsum(
            "maxhij,maxjhd->maxihd", score_round, split_key, preferred_element_type=jnp.float32
        )
        * inv_root
    ).astype(jnp.bfloat16)
    grad_key = jnp.einsum(
        "maxhij,maxihd->maxjhd", score_round, split_query, preferred_element_type=jnp.float32
    ).astype(jnp.bfloat16)
    width = HEADS * HD
    return (
        attended.reshape(leading + (width,)),
        grad_query.reshape(leading + (width,)),
        grad_key.reshape(leading + (width,)),
        grad_value.reshape(leading + (width,)),
        score_sums,
    )


def contract(left, right, left_dim, right_dim):
    return lax.dot_general(
        left, right, (((left_dim,), (right_dim,)), ((), ())), preferred_element_type=jnp.float32
    )


def roll_ahead(weather, cotangent):
    lon_parts = passed_along(
        (weather[:, :, :, :SHIFT_LON], cotangent[:, :, :, :SHIFT_LON]), "lon", -1
    )
    weather_lon = jnp.concatenate([weather[:, :, :, SHIFT_LON:], lon_parts[0]], axis=3)
    grad_lon = jnp.concatenate([cotangent[:, :, :, SHIFT_LON:], lon_parts[1]], axis=3)
    lat_parts = passed_along((weather_lon[:, :, :SHIFT_LAT], grad_lon[:, :, :SHIFT_LAT]), "lat", -1)
    weather_lat = jnp.concatenate([weather_lon[:, :, SHIFT_LAT:], lat_parts[0]], axis=2)
    grad_lat = jnp.concatenate([grad_lon[:, :, SHIFT_LAT:], lat_parts[1]], axis=2)
    return (jnp.roll(weather_lat, -SHIFT_LEV, axis=1), jnp.roll(grad_lat, -SHIFT_LEV, axis=1))


def roll_behind(shifted):
    levels_back = jnp.roll(shifted, SHIFT_LEV, axis=1)
    lon_strip = passed_along(levels_back[:, :, :, -SHIFT_LON:], "lon", 1)
    lon_back = jnp.concatenate([lon_strip, levels_back[:, :, :, :-SHIFT_LON]], axis=3)
    lat_strip = passed_along(lon_back[:, :, -SHIFT_LAT:], "lat", 1)
    return jnp.concatenate([lat_strip, lon_back[:, :, :-SHIFT_LAT]], axis=2)


def shards(weather, cotangent, norm_gain, qkv_weight, proj_weight, bias_table):
    samples, levels, rows_here, cols_here, channels = weather.shape
    dims = (samples, levels, rows_here, cols_here, channels)
    shifted, grad_shifted = roll_ahead(weather, cotangent)
    lat_index = lax.axis_index("lat")
    lat_count = lax.axis_size("lat")
    level_region = (jnp.arange(levels, dtype=jnp.int32) >= levels - SHIFT_LEV).astype(jnp.int32)
    row_global = lat_index * rows_here + jnp.arange(rows_here, dtype=jnp.int32)
    row_region = (row_global >= rows_here * lat_count - SHIFT_LAT).astype(jnp.int32)
    groups = level_region[:, None, None] + 2 * row_region[None, :, None]
    groups = jnp.broadcast_to(groups, (levels, rows_here, cols_here))
    group_rows = to_windows(groups[None, :, :, :, None])[:, 0, :, :, :, 0]
    picker = make_picker()
    bias_full = expand_bias(bias_table, picker)
    widened = shifted.astype(jnp.float32)
    centre = jnp.mean(widened, axis=-1, keepdims=True)
    centred = widened - centre
    inv_std = lax.rsqrt(jnp.mean(centred * centred, axis=-1, keepdims=True) + EPSILON)
    normed = (centred * inv_std).reshape(-1, channels)
    inv_std = inv_std.reshape(-1, 1)
    hidden = (normed * norm_gain).astype(jnp.bfloat16)
    mixed = jnp.dot(hidden, qkv_weight, preferred_element_type=jnp.float32)
    inv_root = HD ** (-0.5)
    queries = (mixed[:, :channels] * inv_root).astype(jnp.bfloat16)
    key_flat = mixed[:, channels : 2 * channels].astype(jnp.bfloat16)
    value_flat = mixed[:, 2 * channels :].astype(jnp.bfloat16)
    grad_flat = grad_shifted.reshape(-1, channels)
    grad_attended = contract(grad_flat, proj_weight, 1, 1).astype(jnp.bfloat16)
    query_win = to_windows(queries.reshape(dims))
    key_win = to_windows(key_flat.reshape(dims))
    value_win = to_windows(value_flat.reshape(dims))
    grad_win = to_windows(grad_attended.reshape(dims))
    results = lax.map(attend, (query_win, key_win, value_win, grad_win, bias_full, group_rows))
    attended = from_windows(results[0], samples, levels, rows_here, cols_here).reshape(-1, channels)
    grad_query = from_windows(results[1], samples, levels, rows_here, cols_here).reshape(
        -1, channels
    )
    grad_key = from_windows(results[2], samples, levels, rows_here, cols_here).reshape(-1, channels)
    grad_value = from_windows(results[3], samples, levels, rows_here, cols_here).reshape(
        -1, channels
    )
    grad_mixed = jnp.concatenate([grad_query, grad_key, grad_value], axis=1)
    branch = (
        jnp.dot(attended, proj_weight, preferred_element_type=jnp.float32)
        .astype(jnp.bfloat16)
        .reshape(dims)
    )
    updated = (weather.astype(jnp.float32) + roll_behind(branch).astype(jnp.float32)).astype(
        jnp.bfloat16
    )
    grad_proj = contract(attended, grad_flat, 0, 0)
    grad_qkv = contract(hidden, grad_mixed, 0, 0)
    grad_hidden = contract(grad_mixed, qkv_weight, 1, 1)
    grad_gain = jnp.sum(grad_hidden * normed, axis=0)
    grad_norm = grad_hidden * norm_gain
    grad_input = inv_std * (
        grad_norm
        - jnp.mean(grad_norm, axis=-1, keepdims=True)
        - normed * jnp.mean(grad_norm * normed, axis=-1, keepdims=True)
    )
    grad_input = grad_input.astype(jnp.bfloat16).reshape(dims)
    grad_weather = (
        cotangent.astype(jnp.float32) + roll_behind(grad_input).astype(jnp.float32)
    ).astype(jnp.bfloat16)
    grad_table = fold_bias(results[4], picker)
    token_total = (
        samples
        * levels
        * rows_here
        * cols_here
        * lax.axis_size("dp")
        * lax.axis_size("lon")
        * lat_count
    )
    factor = token_total ** (-0.5)
    lat_windows = grad_table.shape[1]
    padded = jnp.zeros(
        (grad_table.shape[0], lat_windows * lat_count) + grad_table.shape[2:], jnp.float32
    )
    padded = lax.dynamic_update_slice_in_dim(padded, grad_table, lat_index * lat_windows, 1)
    summed_all = lax.psum((grad_qkv, grad_proj, grad_gain, padded), ("dp", "lon", "lat"))
    weight_parts = (summed_all[0], summed_all[1], summed_all[2])
    bias_total = lax.dynamic_slice_in_dim(summed_all[3], lat_index * lat_windows, lat_windows, 1)
    return (
        updated,
        grad_weather,
        weight_parts[0] * factor,
        weight_parts[1] * factor,
        weight_parts[2] * factor,
        bias_total * factor,
    )


def solution(mesh):
    return jax.shard_map(
        shards,
        mesh=mesh,
        in_specs=(
            P("dp", None, "lat", "lon", None),
            P("dp", None, "lat", "lon", None),
            P(),
            P(),
            P(),
            P(None, "lat", None, None),
        ),
        out_specs=(
            P("dp", None, "lat", "lon", None),
            P("dp", None, "lat", "lon", None),
            P(),
            P(),
            P(),
            P(None, "lat", None, None),
        ),
        check_vma=False,
    )
```

profile of v0, /device:TPU:1, one launch (start us, length us, event | category | flops | bytes accessed | tf_op | source)
XLA Modules:
  0.0 622.3 jit_solution(10829592132046241576)
XLA Ops:
  7.2 1.7 slice.88
  8.9 9.0 %collective-permute-start = (bf16[1,8,6,6,192]{4,3,2,1,0:T(8,128)(2,1)}, bf16[1,8,6,6,192]{4,3,2,1,0:T(8,128)(2,1)}, u32[]{:S(2)}, u32[]{:S(2)}) collective-permute-start(bf16[1,8,6,6,192]{4,3,2,1,0:T(8,128)(2,1)} %slice.88), channel_id=1, source_target_pairs={{0,60},{4,0},{8,4},{12,8},{16,12},{20,16},{24,20},{28,24},{32,28},... | collective-permute-start | bytes 331784 | tf_op jit(solution)/shard_map/ppermute | solution.py:23
  19.7 1.3 slice.87
  21.2 1.6 reduce.10
  22.8 2.6 reshape.426
  25.3 14.8 %convolution_bitcast_fusion = f32[4,1,6,2,6,12,2,6,12]{8,7,4,6,3,2,0,5,1:T(8,128)} fusion(f32[4,6,2,2,6,6,23,1]{6,5,4,3,2,1,0,7:T(8,128)S(1)} %reshape.426, pred[23,12,12,1,1,1,1,1]{0,1,2,7,6,5,4,3:T(8,128)(4,1)S(1)} %fusion.30), kind=kOutput, calls=%fused_computation.35 | convolution fusion | flops 137355264 | bytes 2311920 | tf_op jit(solution)/shard_map/lahzyuvd,dxw->lahzuxyvw/dot_general | solution.py:59
  41.4 2.5 collective-permute-start.1
  44.5 39.2 %copy.108 = f32[4,1,6,2,6,12,2,6,12]{5,4,3,8,7,6,2,0,1:T(8,128)} copy(f32[4,1,6,2,6,12,2,6,12]{8,7,4,6,3,2,0,5,1:T(8,128)} %convolution_bitcast_fusion) | data formatting | bytes 3981312 | tf_op jit(solution)/shard_map/while | solution.py:184
  83.7 19.5 %reshape.431 = f32[4,1,6,144,144]{3,4,2,1,0:T(8,128)} reshape(f32[4,1,6,2,6,12,2,6,12]{5,4,3,8,7,6,2,0,1:T(8,128)} %copy.108) | data formatting | bytes 3981312 | tf_op jit(solution)/shard_map/while | solution.py:184
  103.2 1.9 fusion.28
  110.7 1.3 copy.72
  112.5 1.3 copy.70
  117.7 74.0 %while.18 = (s32[]{:T(128)}, bf16[4,1,1,2,144,192]{5,3,4,0,2,1:T(2,128)(2,1)}, bf16[4,1,1,2,144,192]{5,3,4,0,2,1:T(2,128)(2,1)}, bf16[4,1,1,2,144,192]{5,3,4,0,2...) while((s32[]{:T(128)}, ...), condition=%wide.region_7.8_spmd, body=%wide.region_2.7_spmd.sunk | while | flops 99227088 | bytes 23561376 | solution.py:184
  120.3 1.2 dynamic-slice_bitcast_fusion.2
  121.7 2.0 fusion.95
  124.3 2.0 fusion.96
  127.7 1.7 copy.147
  129.5 1.3 convolution_convert_fusion.9
  131.6 1.9 constant_dynamic-update-slice_fusion.7
  140.2 2.0 fusion.95
  142.8 2.0 fusion.96
  146.2 1.7 copy.147
  147.9 1.3 convolution_convert_fusion.9
  150.1 1.9 constant_dynamic-update-slice_fusion.7
  158.6 2.0 fusion.95
  161.3 2.0 fusion.96
  164.7 1.7 copy.147
  166.4 1.3 convolution_convert_fusion.9
  168.5 1.9 constant_dynamic-update-slice_fusion.7
  177.1 2.0 fusion.95
  179.7 2.0 fusion.96
  183.1 1.7 copy.147
  184.9 1.3 convolution_convert_fusion.9
  187.0 1.9 constant_dynamic-update-slice_fusion.7
  191.7 1.3 copy.88
  195.9 2.6 fusion.26
  203.8 18.4 %reshape.432 = f32[4,6,2,6,12,2,6,12]{4,3,2,7,6,5,1,0:T(8,128)} reshape(f32[4,1,6,144,144]{3,4,2,1,0:T(8,128)} %get-tuple-element.76) | data formatting | bytes 3981312 | tf_op jit(solution)/shard_map/reshape.80
  222.2 43.7 %fusion.15 = f32[4,1,6,2,2,6,6,23]{7,6,4,5,3,2,0,1:T(8,128)S(1)} fusion(f32[4,6,2,6,12,2,6,12]{4,3,2,7,6,5,1,0:T(8,128)} %reshape.432, s32[12,12]{0,1:T(8,128)S(1)} %subtract_add_fusion), kind=kOutput, calls=%fused_computation.38 | convolution fusion | flops 137358576 | bytes 2309184 | tf_op jit(solution)/shard_map/lahzuxyvw,dxw->lahzyuvd/dot_general | solution.py:69
  266.2 1.6 reshape.433
  269.6 76.4 %psum.30 = f32[192]{0:T(256)S(1)} all-reduce(f32[192]{0:T(256)S(1)} %get-tuple-element.101), channel_id=1, replica_groups=mesh['dp'=4,'lon'=16,'lat'=4] {'dp','lon','lat'}, use_global_device_ids=true, to_apply=%region_13.14 | all-reduce | flops 192 | bytes 1536 | tf_op jit(solution)/shard_map/psum | solution.py:232
  347.1 2.9 dynamic_update_slice.20
  352.5 3.6 collective-permute-done.4
  357.5 3.8 collective-permute-done.7
  362.2 6.4 %collective-permute-done.5 = bf16[1,8,3,24,192]{4,3,2,1,0:T(8,128)(2,1)S(1)} collective-permute-done((bf16[1,8,3,24,192]{4,3,2,1,0:T(8,128)(2,1)S(1)}, bf16[1,8,3,24,192]{4,3,2,1,0:T(8,128)(2,1)S(1)}, u32[]{:S(2)}, u32[]{:S(2)}) %collective-permute-start.5) | collective-permute-done | bytes 221216 | tf_op jit(solution)/shard_map/ppermute | solution.py:23
  369.6 239.7 %all-reduce.3.cloned.1.call-done = (f32[192,576]{1,0:T(8,128)}, f32[192,192]{1,0:T(8,128)}, f32[4,4,6,3312]{3,1,2,0:T(4,128)}) async-done(((f32[192,576]{1,0:T(8,128)}, f32[192,192]{1,0:T(8,128)}, f32[4,4,6,3312]{3,1,2,0:T(4,128)}), (f32[192,576]{1,0:T(8,128)}, f32[192,192]{1,0:T(8,128)}, f32[4,4,6,3312]{3,1,2,0:T(4,128)})) %all-reduce.3.cloned.1.call-update) | async-done | bytes 1861648 | tf_op jit(solution)/shard_map/psum | solution.py:232
  609.3 1.9 broadcast_multiply_fusion
  611.2 2.5 dynamic-slice_multiply_fusion
  613.6 1.6 broadcast_multiply_fusion.1
  (244 shorter events, 66.7 us)
Async XLA Ops:
  7.2 100.2 %copy-start = (bf16[192,576]{1,0:T(8,128)(2,1)S(1)}, bf16[192,576]{1,0:T(8,128)(2,1)}, u32[]{:S(2)}) copy-start(bf16[192,576]{1,0:T(8,128)(2,1)} %param.11) | copy-start | bytes 663556
  7.2 14.0 %copy-start.24 = (f32[4,1,6,3312]{3,1,2,0:T(1,128)S(1)}, f32[4,1,6,3312]{3,1,2,0:T(1,128)}, u32[]{:S(2)}) copy-start(f32[4,1,6,3312]{3,1,2,0:T(1,128)} %param.13) | copy-start | bytes 953860
  7.2 602.1 %all-reduce.3.cloned.1.call-start = ((), (), s32[]{:S(2)}) async-start(), calls=%async_computation | async-start | bytes 3932160 | tf_op jit(solution)/shard_map/psum | solution.py:232
  8.9 31.2 %collective-permute-start = (bf16[1,8,6,6,192]{4,3,2,1,0:T(8,128)(2,1)}, bf16[1,8,6,6,192]{4,3,2,1,0:T(8,128)(2,1)}, u32[]{:S(2)}, u32[]{:S(2)}) collective-permute-start(bf16[1,8,6,6,192]{4,3,2,1,0:T(8,128)(2,1)} %slice.88), channel_id=1, source_target_pairs={{0,60},{4,0},{8,4},{12,8},{16,12},{20,16},{24,20},{28,24},{32,28},... | collective-permute-start | bytes 331784 | tf_op jit(solution)/shard_map/ppermute | solution.py:23
  18.9 84.3 %collective-permute-start.2 = (bf16[1,8,6,6,192]{4,3,2,1,0:T(8,128)(2,1)S(1)}, bf16[1,8,6,6,192]{4,3,2,1,0:T(8,128)(2,1)}, u32[]{:S(2)}, u32[]{:S(2)}) collective-permute-start(bf16[1,8,6,6,192]{4,3,2,1,0:T(8,128)(2,1)S(1)} %slice.97), channel_id=1, source_target_pairs={{0,60},{4,0},{8,4},{12,8},{16,12},{20,16},{24,20},{28,24},{32,28},... | collective-permute-start | bytes 331784 | tf_op jit(solution)/shard_map/ppermute | solution.py:23
  40.1 3.9 copy-start.8
  41.4 64.5 %collective-permute-start.1 = (bf16[1,8,3,24,192]{4,3,2,1,0:T(8,128)(2,1)S(1)}, bf16[1,8,3,24,192]{4,3,2,1,0:T(8,128)(2,1)S(1)}, u32[]{:S(2)}, u32[]{:S(2)}) collective-permute-start(bf16[1,8,3,24,192]{4,3,2,1,0:T(8,128)(2,1)S(1)} %get-tuple-element.147), channel_id=1, source_target_pairs={{0,3},{1,0},{2,1},{3,2},{4,7},{5,4},{6,5},{7,6},{8,11},{9,8},{10,9... | collective-permute-start | bytes 663560 | tf_op jit(solution)/shard_map/ppermute | solution.py:23
  105.1 8.6 %collective-permute-start.3 = (bf16[1,8,3,24,192]{4,3,2,1,0:T(8,128)(2,1)}, bf16[1,8,3,24,192]{4,3,2,1,0:T(8,128)(2,1)}, u32[]{:S(2)}, u32[]{:S(2)}) collective-permute-start(bf16[1,8,3,24,192]{4,3,2,1,0:T(8,128)(2,1)} %get-tuple-element.145), channel_id=1, source_target_pairs={{0,3},{1,0},{2,1},{3,2},{4,7},{5,4},{6,5},{7,6},{8,11},{9,8},{10,9... | collective-permute-start | bytes 663560 | tf_op jit(solution)/shard_map/ppermute | solution.py:23
  107.6 0.9 copy-start.2
  110.5 1.5 copy-start.15
  112.4 4.0 copy-start.22
  117.8 6.0 copy-start.13
  117.8 6.3 %copy-start.11 = (bf16[4,1,1,2,144,192]{5,3,4,0,2,1:T(2,128)(2,1)}, bf16[4,1,1,2,144,192]{5,3,4,0,2,1:T(2,128)(2,1)S(1)}, u32[]{:S(2)}) copy-start(bf16[4,1,1,2,144,192]{5,3,4,0,2,1:T(2,128)(2,1)S(1)} %get-tuple-element.284) | copy-start | bytes 1327108 | tf_op jit(solution)/shard_map/while
  124.0 2.3 copy-start.1
  134.7 1.5 copy-start.12
  134.7 1.5 copy-start.14
  136.3 6.0 copy-start.13
  136.3 6.2 %copy-start.11 = (bf16[4,1,1,2,144,192]{5,3,4,0,2,1:T(2,128)(2,1)}, bf16[4,1,1,2,144,192]{5,3,4,0,2,1:T(2,128)(2,1)S(1)}, u32[]{:S(2)}) copy-start(bf16[4,1,1,2,144,192]{5,3,4,0,2,1:T(2,128)(2,1)S(1)} %get-tuple-element.284) | copy-start | bytes 1327108 | tf_op jit(solution)/shard_map/while
  142.5 2.3 copy-start.1
  153.2 1.5 copy-start.12
  153.2 1.5 copy-start.14
  154.7 6.0 copy-start.13
  154.7 6.2 %copy-start.11 = (bf16[4,1,1,2,144,192]{5,3,4,0,2,1:T(2,128)(2,1)}, bf16[4,1,1,2,144,192]{5,3,4,0,2,1:T(2,128)(2,1)S(1)}, u32[]{:S(2)}) copy-start(bf16[4,1,1,2,144,192]{5,3,4,0,2,1:T(2,128)(2,1)S(1)} %get-tuple-element.284) | copy-start | bytes 1327108 | tf_op jit(solution)/shard_map/while
  161.0 2.3 copy-start.1
  171.7 1.5 copy-start.12
  171.7 1.5 copy-start.14
  173.2 6.0 copy-start.13
  173.2 6.2 %copy-start.11 = (bf16[4,1,1,2,144,192]{5,3,4,0,2,1:T(2,128)(2,1)}, bf16[4,1,1,2,144,192]{5,3,4,0,2,1:T(2,128)(2,1)S(1)}, u32[]{:S(2)}) copy-start(bf16[4,1,1,2,144,192]{5,3,4,0,2,1:T(2,128)(2,1)S(1)} %get-tuple-element.284) | copy-start | bytes 1327108 | tf_op jit(solution)/shard_map/while
  179.4 2.3 copy-start.1
  190.2 1.5 copy-start.12
  190.2 1.5 copy-start.14
  191.7 2.4 copy-start.18
  193.0 2.4 copy-start.19
  194.3 1.6 copy-start.3
  194.3 1.6 copy-start.20
  195.9 2.7 copy-start.21
  199.6 2.0 copy-start.17
  200.1 1.9 copy-start.5
  201.6 1.5 copy-start.23
  268.8 82.3 %collective-permute-start.6 = (bf16[1,8,6,6,192]{4,3,2,1,0:T(8,128)(2,1)S(1)}, bf16[1,8,6,6,192]{4,3,2,1,0:T(8,128)(2,1)}, u32[]{:S(2)}, u32[]{:S(2)}) collective-permute-start(bf16[1,8,6,6,192]{4,3,2,1,0:T(8,128)(2,1)S(1)} %pad_maximum_fusion.9), channel_id=1, source_target_pairs={{0,4},{4,8},{8,12},{12,16},{16,20},{20,24},{24,28},{28,32},{32,36}... | collective-permute-start | bytes 331784 | tf_op jit(solution)/shard_map/ppermute | solution.py:23
  346.6 4.5 copy-start.7
  346.6 4.5 copy-start.16
  346.6 9.5 %collective-permute-start.4 = (bf16[1,8,6,6,192]{4,3,2,1,0:T(8,128)(2,1)S(1)}, bf16[1,8,6,6,192]{4,3,2,1,0:T(8,128)(2,1)}, u32[]{:S(2)}, u32[]{:S(2)}) collective-permute-start(bf16[1,8,6,6,192]{4,3,2,1,0:T(8,128)(2,1)S(1)} %pad_maximum_fusion.10), channel_id=1, source_target_pairs={{0,4},{4,8},{8,12},{12,16},{16,20},{20,24},{24,28},{28,32},{32,36}... | collective-permute-start | bytes 331784 | tf_op jit(solution)/shard_map/ppermute | solution.py:23
  350.0 1.1 copy-start.6
  352.4 8.9 %copy-start.9 = (bf16[1,8,6,24,192]{4,3,2,1,0:T(8,128)(2,1)S(1)}, bf16[1,8,6,24,192]{4,3,2,1,0:T(8,128)(2,1)}, u32[]{:S(2)}) copy-start(bf16[1,8,6,24,192]{4,3,2,1,0:T(8,128)(2,1)} %param.9) | copy-start | bytes 1327108
  352.4 8.8 %collective-permute-start.7 = (bf16[1,8,3,24,192]{4,3,2,1,0:T(8,128)(2,1)S(1)}, bf16[1,8,3,24,192]{4,3,2,1,0:T(8,128)(2,1)S(1)}, u32[]{:S(2)}, u32[]{:S(2)}) collective-permute-start(bf16[1,8,3,24,192]{4,3,2,1,0:T(8,128)(2,1)S(1)} %get-tuple-element.148), channel_id=1, source_target_pairs={{0,1},{1,2},{2,3},{3,0},{4,5},{5,6},{6,7},{7,4},{8,9},{9,10},{10,1... | collective-permute-start | bytes 663560 | tf_op jit(solution)/shard_map/ppermute | solution.py:23
  357.3 11.3 %copy-start.10 = (bf16[1,8,6,24,192]{4,3,2,1,0:T(8,128)(2,1)S(1)}, bf16[1,8,6,24,192]{4,3,2,1,0:T(8,128)(2,1)}, u32[]{:S(2)}) copy-start(bf16[1,8,6,24,192]{4,3,2,1,0:T(8,128)(2,1)} %param.8) | copy-start | bytes 1327108
  357.4 11.2 %collective-permute-start.5 = (bf16[1,8,3,24,192]{4,3,2,1,0:T(8,128)(2,1)S(1)}, bf16[1,8,3,24,192]{4,3,2,1,0:T(8,128)(2,1)S(1)}, u32[]{:S(2)}, u32[]{:S(2)}) collective-permute-start(bf16[1,8,3,24,192]{4,3,2,1,0:T(8,128)(2,1)S(1)} %get-tuple-element.150), channel_id=1, source_target_pairs={{0,1},{1,2},{2,3},{3,0},{4,5},{5,6},{6,7},{7,4},{8,9},{9,10},{10,1... | collective-permute-start | bytes 663560 | tf_op jit(solution)/shard_map/ppermute | solution.py:23
  (2 other events, 1.5 us)
Sparse Core Ops, SparseCore 0:
  351.2 258.0 all-reduce.2
where the time goes:
time: 631 us; the launch traced here: 622 us
  waiting for transfers between devices  254 us (40%)
  local copies, waits for them, and re-layouts  148 us (23%)
  matrix products  91.9 us (15%)
  blocking collectives  76.4 us (12%)
  other arithmetic  22.6 us (4%)
  between operations  14.9 us (2%)
  starting transfers between devices  14.5 us (2%)
    psum x1, waiting for transfers between devices, shards(): lax.psum((grad_qkv, grad_proj, grad_gain, padded), ('dp', 'lon', 'lat'))  240 us
    psum x1, blocking collectives, shards(): lax.psum((grad_qkv, grad_proj, grad_gain, padded), ('dp', 'lon', 'lat'))  76.4 us
    while x2, local copies, waits for them, and re-layouts, shards(): lax.map(attend, (query_win, key_win, value_win, grad_win, bias_full, grou...  58.7 us
    dot_general x1, matrix products, fold_bias(): jnp.einsum('lahzuxyvw,dxw->lahzyuvd', shaped, picker, precision=lax.Preci...  43.7 us
    dynamic_update_slice x28, local copies, waits for them, and re-layouts, shards(): lax.map(attend, (query_win, key_win, value_win, grad_win, bias_full, grou...  26.8 us
    another operation x2, local copies, waits for them, and re-layouts  21 us
    dot_general x1, matrix products, expand_bias(): jnp.einsum('lahzyuvd,dxw->lahzuxyvw', shaped, picker, precision=lax.Preci...  14.8 us
    ppermute x8, starting transfers between devices, passed_along(): return lax.ppermute(value, axis, pairs)  14.5 us
  transfers between devices with their start and end apart: 9, of which 4 were waited for; matrix products, arithmetic and copies ran while one was open for 16% of the time, Pallas kernels for 0%

commit v1 on v0

v1 whole, which is shorter than its diff:
```python
import functools

import numpy as np
import jax
import jax.numpy as jnp
from jax import lax
from jax.experimental import pallas as pl
from jax.experimental.pallas import tpu as pltpu
from jax.sharding import PartitionSpec as P

HEADS = 6
WLEV = 2
WLAT = 6
WLON = 12
HD = 32
CH = 192
TOK = 144
LANES = 128
SHIFT_LAT = 3
SHIFT_LON = 6
SPAN = 2 * WLON - 1
GROUPS = WLEV * WLAT
MASKED = -1e30
EPSILON = 1e-05
BF = jnp.bfloat16
F32 = jnp.float32
PAY = 2048
WTILES = 6
BIAS_ROWS = 288
BROW = WTILES * CH
GROW = BROW + 3 * BIAS_ROWS
PIECE = 32
VMEM_LIMIT = 56 * 1024 * 1024


def place(rows, cols):
    return np.zeros((rows, cols), np.float32)


def gather_matrices(cols_here):
    windows = cols_here // WLON
    own_cols = cols_here - SHIFT_LON
    own = place(windows * WLAT * WLON, WLAT * cols_here)
    lat = place(windows * WLAT * WLON, SHIFT_LAT * own_cols)
    corner = place(windows * WLAT * WLON, WLAT * SHIFT_LON)
    for n in range(windows):
        for a in range(WLAT):
            for x in range(WLON):
                row = (n * WLAT + a) * WLON + x
                col = n * WLON + x
                if col < own_cols:
                    if a < SHIFT_LAT:
                        own[row, (a + SHIFT_LAT) * cols_here + col + SHIFT_LON] = 1
                    else:
                        lat[row, (a - SHIFT_LAT) * own_cols + col] = 1
                else:
                    corner[row, a * SHIFT_LON + col - own_cols] = 1
    return own, lat, corner


def scatter_matrices(cols_here):
    own_cols = cols_here - SHIFT_LON
    lat = place(WLAT * cols_here, SHIFT_LAT * own_cols)
    corner = place(WLAT * cols_here, WLAT * SHIFT_LON)
    for a in range(WLAT):
        for c in range(cols_here):
            row = a * cols_here + c
            if c >= SHIFT_LON:
                if a < SHIFT_LAT:
                    lat[row, a * own_cols + c - SHIFT_LON] = 1
            elif a >= SHIFT_LAT:
                corner[row, (a - SHIFT_LAT) * SHIFT_LON + c] = 1
            else:
                corner[row, (a + SHIFT_LAT) * SHIFT_LON + c] = 1
    return lat, corner


def lon_selectors():
    out = np.zeros((WLON, 3 * LANES, 2 * LANES), np.float32)
    for xj in range(WLON):
        for g in range(GROUPS):
            for xi in range(WLON):
                out[xj, g * SPAN + xi - xj + WLON - 1, g * WLON + xi] = 1
    return out


def dot(a, b, ca=1, cb=0):
    return lax.dot_general(a, b, (((ca,), (cb,)), ((), ())), preferred_element_type=F32)


def split(value):
    high = value.astype(BF)
    return high, (value - high.astype(F32)).astype(BF)


def prep_kernel(wx_ref, gx_ref, lat_pick, lon_pick, diag_pick, lat_out, lon_out, diag_out):
    def step(level, carry):
        for pick, strip in ((lat_pick, lat_out), (lon_pick, lon_out), (diag_pick, diag_out)):
            strip[level] = jnp.concatenate(
                [dot(pick[...], ref[level]) for ref in (wx_ref, gx_ref)], axis=1
            ).astype(BF)
        return carry

    lax.fori_loop(0, wx_ref.shape[0], step, 0)


def expand_kernel(lat_ref, table_ref, sel_ref, main_ref, rest_ref):
    table = table_ref[...]
    high = table.astype(BF)
    rest = table - high.astype(F32)
    mid = rest.astype(BF)
    low = (rest - mid.astype(F32)).astype(BF)
    rows = table.shape[0]
    last = lat_ref[0] == lat_ref[1]
    row_id = lax.broadcasted_iota(jnp.int32, (rows, 2 * LANES), 0)
    col_id = lax.broadcasted_iota(jnp.int32, (rows, 2 * LANES), 1)
    a_j = row_id % WLAT
    z_j = (row_id // WLAT) % WLEV
    a_i = (col_id // WLON) % WLAT
    z_i = col_id // (WLON * WLAT)
    cross_lev = jnp.logical_and(row_id >= rows * 3 // 4, z_j != z_i)
    cross_lat = jnp.logical_and(last, (a_j >= SHIFT_LAT) != (a_i >= SHIFT_LAT))
    hide = jnp.where(jnp.logical_or(cross_lev, cross_lat), MASKED, 0.0)

    def step(xj, carry):
        sel = sel_ref[xj, : GROUPS * SPAN]
        value = dot(high, sel) + dot(mid, sel) + dot(low, sel) + hide
        main_ref[pl.ds(xj, rows, stride=WLON), :] = value[:, :LANES]
        rest_ref[pl.ds(xj, rows, stride=WLON), :] = value[:, LANES:]
        return carry

    lax.fori_loop(0, WLON, step, 0)


def main_kernel(
    core_ref, wx_ref, gx_ref, lat_in, lon_in, diag_in, gain_ref, wqkv_ref, proj_ref, bias_main, bias_rest, sel_ref,
    pown_ref, plat_ref, plon_ref, pdiag_ref,
    base_ref, gbase_ref, lat_out, lon_out, diag_out, keep_ref, send_ref,
    x_s, g_s, br_s, gi_s, dsum_main, dsum_rest, gw_ref, gproj_ref, ggain_ref, gbias_ref, pay_s,
):
    channel = lax.broadcasted_iota(jnp.int32, (TOK, CH), 1)
    head_mask = [jnp.logical_and(channel >= h * HD, channel < (h + 1) * HD) for h in range(HEADS)]

    def load_level(level, carry):
        k = ((level + 7) % 8) // 2
        z = (level + 7) % 2
        place_own = pown_ref[...]
        strips = ((plat_ref, lat_in), (plon_ref, lon_in), (pdiag_ref, diag_in))
        xw = dot(place_own, wx_ref[level])
        gw = dot(place_own, gx_ref[level])
        for where_ref, strip in strips:
            both = strip[level]
            xw = xw + dot(where_ref[...], both[:, :CH])
            gw = gw + dot(where_ref[...], both[:, CH:])
        half = TOK // 2
        for n in range(2):
            x_s[2 * k + n, pl.ds(pl.multiple_of(z * half, 8), half), :] = xw[n * half : (n + 1) * half]
            g_s[2 * k + n, pl.ds(pl.multiple_of(z * half, 8), half), :] = gw[n * half : (n + 1) * half]
        return carry

    lax.fori_loop(0, 8, load_level, 0)
    dsum_main[...] = jnp.zeros_like(dsum_main)
    dsum_rest[...] = jnp.zeros_like(dsum_rest)
    gw_ref[...] = jnp.zeros_like(gw_ref)
    gproj_ref[...] = jnp.zeros_like(gproj_ref)
    ggain_ref[...] = jnp.zeros_like(ggain_ref)
    gain = gain_ref[...]
    inv_root = HD ** (-0.5)

    def eye(n):
        return (lax.broadcasted_iota(jnp.int32, (n, n), 0) == lax.broadcasted_iota(jnp.int32, (n, n), 1)).astype(F32).astype(BF)

    eye_c = eye(CH)
    eye_t = eye(TOK)

    def window(w, carry):
        k = w // 2
        x = x_s[w]
        centre = jnp.mean(x, axis=-1, keepdims=True)
        centred = x - centre
        inv_std = lax.rsqrt(jnp.mean(centred * centred, axis=-1, keepdims=True) + EPSILON)
        normed = centred * inv_std
        hidden = (normed * gain).astype(BF)
        q = (dot(hidden, wqkv_ref[0]) * inv_root).astype(BF)
        key = dot(hidden, wqkv_ref[1]).astype(BF)
        v = dot(hidden, wqkv_ref[2]).astype(BF)
        g = g_s[w].astype(BF)
        d_att = dot(g, proj_ref[...], 1, 1).astype(BF)
        key_t = dot(eye_c, key, 1, 1).astype(BF)
        v_t = dot(eye_c, v, 1, 1).astype(BF)
        zero = jnp.zeros((TOK, CH), BF)
        att_parts = []
        dq_parts = []
        d_key = jnp.zeros((TOK, CH), F32)
        d_val = jnp.zeros((TOK, CH), F32)
        for h in range(HEADS):
            lo, hi = h * HD, (h + 1) * HD
            s = dot(jnp.where(head_mask[h], key, zero), q, 1, 1)
            rows = pl.ds(pl.multiple_of((k * HEADS + h) * TOK, 8), TOK)
            s = s + jnp.concatenate([bias_main[rows, :], bias_rest[rows, : TOK - LANES]], axis=1)
            s = s - jnp.max(s, axis=0, keepdims=True)
            e = jnp.exp(s)
            probs = (e / jnp.sum(e, axis=0, keepdims=True)).astype(BF)
            dp = dot(jnp.where(head_mask[h], v, zero), d_att, 1, 1)
            att_parts.append(dot(v_t[lo:hi], probs))
            d_val = d_val + dot(probs, jnp.where(head_mask[h], d_att, zero))
            pf = probs.astype(F32)
            t = pf * dp
            ds = t - pf * jnp.sum(t, axis=0, keepdims=True)
            dsum_main[rows, :] += ds[:, :LANES]
            dsum_rest[rows, : TOK - LANES] += ds[:, LANES:]
            dsb = ds.astype(BF)
            dq_parts.append(dot(key_t[lo:hi], dsb))
            d_key = d_key + dot(dsb, jnp.where(head_mask[h], q, zero))
        att_t = jnp.concatenate(att_parts, axis=0).astype(BF)
        dq_t = (jnp.concatenate(dq_parts, axis=0) * inv_root).astype(BF)
        att = dot(eye_t, att_t, 1, 1).astype(BF)
        dq = dot(eye_t, dq_t, 1, 1).astype(BF)
        dk = d_key.astype(BF)
        dv = d_val.astype(BF)
        br_s[w] = dot(att, proj_ref[...])
        gproj_ref[...] += dot(att_t, g)
        hidden_t = dot(eye_c, hidden, 1, 1).astype(BF)
        gw_ref[0] += dot(hidden_t, dq)
        gw_ref[1] += dot(hidden_t, dk)
        gw_ref[2] += dot(hidden_t, dv)
        gh = dot(dq, wqkv_ref[0], 1, 1) + dot(dk, wqkv_ref[1], 1, 1) + dot(dv, wqkv_ref[2], 1, 1)
        ggain_ref[...] += jnp.sum(gh * normed, axis=0, keepdims=True)
        gn = gh * gain
        gi = inv_std * (
            gn
            - jnp.mean(gn, axis=-1, keepdims=True)
            - normed * jnp.mean(gn * normed, axis=-1, keepdims=True)
        )
        gi_s[w] = gi
        return carry

    lax.fori_loop(0, 8, window, 0)

    def store_level(level, carry):
        k = ((level + 7) % 8) // 2
        z = (level + 7) % 2
        half = TOK // 2
        moved = []
        for src, own_in, own_out in ((br_s, wx_ref, base_ref), (gi_s, gx_ref, gbase_ref)):
            rows = jnp.concatenate(
                [src[2 * k + n, pl.ds(pl.multiple_of(z * half, 8), half), :] for n in range(2)], axis=0
            ).astype(BF)
            own_out[level] = (own_in[level].astype(F32) + dot(pown_ref[...], rows, 0, 0)).astype(BF)
            moved.append(rows)
        for where_ref, strip in ((plat_ref, lat_out), (plon_ref, lon_out), (pdiag_ref, diag_out)):
            strip[level] = jnp.concatenate(
                [dot(where_ref[...], rows, 0, 0) for rows in moved], axis=1
            ).astype(BF)
        return carry

    lax.fori_loop(0, 8, store_level, 0)

    gbias_ref[...] = jnp.zeros_like(gbias_ref)
    pairs = dsum_main.shape[0] // TOK

    def fold_step(xj, carry):
        blocks = []
        for m in range(GROUPS):
            rows = pl.ds(m * WLON + xj, pairs, stride=TOK)
            blocks.append(jnp.concatenate([dsum_main[rows, :], dsum_rest[rows, :]], axis=1))
        high, low = split(jnp.concatenate(blocks, axis=0))
        sel = sel_ref[xj]
        gbias_ref[...] += dot(high, sel, 1, 1) + dot(low, sel, 1, 1)
        return carry

    lax.fori_loop(0, WLON, fold_step, 0)
    weights = jnp.concatenate([gw_ref[0], gw_ref[1], gw_ref[2], gproj_ref[...]], axis=1)
    for j in range(WTILES):
        pay_s[j * CH : (j + 1) * CH, :] = weights[:, j * LANES : (j + 1) * LANES]
    for j in range(3):
        pay_s[BROW + j * BIAS_ROWS : BROW + (j + 1) * BIAS_ROWS, :] = gbias_ref[:, j * LANES : (j + 1) * LANES]
    pay_s[GROW:, :] = jnp.zeros((PAY - GROW, LANES), F32)
    pay_s[GROW : GROW + 1, :] = ggain_ref[:, :LANES]
    pay_s[GROW + 1 : GROW + 2, : CH - LANES] = ggain_ref[:, LANES:]
    core = core_ref[0]
    half_rows = PAY // 2
    keep_ref[...] = pay_s[pl.ds(pl.multiple_of(core * half_rows, half_rows), half_rows), :].astype(BF)
    send_ref[...] = pay_s[pl.ds(pl.multiple_of((1 - core) * half_rows, half_rows), half_rows), :].astype(BF)


def finish_kernel(
    factor, core_ref, base_ref, gbase_ref, lat_in, lon_in, diag_in, slat_ref, slon_ref, sdiag_ref, mine_ref, other_ref,
    out_ref, gout_ref, gqkv_ref, gproj_ref, ggain_ref, gbias_ref, full_s, table_s,
):
    core = core_ref[0]
    half_rows = PAY // 2
    full_s[pl.ds(pl.multiple_of(core * half_rows, half_rows), half_rows), :] = mine_ref[...].astype(F32) * factor
    full_s[pl.ds(pl.multiple_of((1 - core) * half_rows, half_rows), half_rows), :] = other_ref[...].astype(F32) * factor
    tiles = [full_s[j * CH : (j + 1) * CH, :] for j in range(WTILES)]
    for j in range(4):
        gqkv_ref[:, j * LANES : (j + 1) * LANES] = tiles[j]
    cut = 3 * CH - 4 * LANES
    gqkv_ref[:, 4 * LANES :] = tiles[4][:, :cut]
    gproj_ref[...] = jnp.concatenate([tiles[4][:, cut:], tiles[5]], axis=1)
    ggain_ref[...] = jnp.concatenate(
        [full_s[GROW : GROW + 1, :], full_s[GROW + 1 : GROW + 2, : CH - LANES]], axis=1
    )
    pairs = BIAS_ROWS // GROUPS
    for m in range(GROUPS):
        z_j, a_j = divmod(m, WLAT)
        block = jnp.concatenate(
            [full_s[BROW + j * BIAS_ROWS + m * pairs : BROW + j * BIAS_ROWS + (m + 1) * pairs, :] for j in range(3)],
            axis=1,
        )
        for g in range(GROUPS):
            z_i, a_i = divmod(g, WLAT)
            to = SPAN * (((z_i * WLEV + z_j) * WLAT + a_i) * WLAT + a_j)
            table_s[:, to : to + SPAN] = block[:, g * SPAN : (g + 1) * SPAN]
    for r in range(pairs):
        gbias_ref[r] = table_s[r : r + 1, : gbias_ref.shape[2]]

    def step(level, carry):
        up = base_ref[level].astype(F32)
        gup = gbase_ref[level].astype(F32)
        for where_ref, strip in ((slat_ref, lat_in), (slon_ref, lon_in), (sdiag_ref, diag_in)):
            both = strip[level]
            up = up + dot(where_ref[...], both[:, :CH])
            gup = gup + dot(where_ref[...], both[:, CH:])
        out_ref[level] = up.astype(BF)
        gout_ref[level] = gup.astype(BF)
        return carry

    lax.fori_loop(0, 8, step, 0)


def passed(value, lat_step, lon_step):
    lats, highs, zs = lax.axis_size("lat"), lax.axis_size("yhi"), lax.axis_size("z")
    lons = highs * zs
    pairs = [
        (b * lats + a, (b + lon_step) % lons * lats + (a + lat_step) % lats)
        for b in range(lons)
        for a in range(lats)
    ]
    return lax.ppermute(value, ("yhi", "z", "lat"), pairs)


def swapped(value):
    return lax.ppermute(value, "core", [(0, 1), (1, 0)])


def total_over_devices(keep, send):
    wide = ("ylo", "yhi", "z")
    peers = lax.axis_size("ylo") * lax.axis_size("yhi") * lax.axis_size("z")
    half = (keep.astype(F32) + swapped(send).astype(F32)).astype(BF)
    pieces = lax.all_to_all(half, wide, 0, 0, tiled=True)
    piece = jnp.sum(pieces.reshape(peers, PIECE, LANES).astype(F32), axis=0)
    lats = lax.axis_size("lat")
    place_here = lax.axis_index("core") * peers + lax.axis_index(wide)
    shared = jnp.logical_or(place_here < BROW // PIECE, place_here >= GROW // PIECE)
    others = jnp.zeros_like(piece)
    for step in range(1, lats):
        others = others + lax.ppermute(piece, "lat", [(a, (a + step) % lats) for a in range(lats)])
    piece = jnp.where(shared, piece + others, piece).astype(BF)
    spread = jnp.broadcast_to(piece[None], (peers, PIECE, LANES)).reshape(half.shape)
    mine = lax.all_to_all(spread, wide, 0, 0, tiled=True)
    return mine, swapped(mine)


def call(kernel, out_shape, scratch=(), smem=0, count=0, flops=0):
    specs = [pl.BlockSpec(memory_space=pltpu.SMEM)] * smem
    specs += [pl.BlockSpec(memory_space=pltpu.VMEM)] * (count - smem)
    return pl.pallas_call(
        kernel,
        out_shape=out_shape,
        in_specs=specs,
        out_specs=jax.tree.map(lambda _: pl.BlockSpec(memory_space=pltpu.VMEM), out_shape),
        scratch_shapes=list(scratch),
        compiler_params=pltpu.CompilerParams(vmem_limit_bytes=VMEM_LIMIT),
        cost_estimate=pl.CostEstimate(flops=flops, bytes_accessed=flops // 500, transcendentals=0),
    )


def sds(shape, dtype):
    return jax.ShapeDtypeStruct(shape, dtype)


def shards(weather, cotangent, norm_gain, qkv_weight, proj_weight, bias_table):
    samples, levels, rows_here, cols_here, channels = weather.shape
    lat_index = lax.axis_index("lat")
    lat_count = lax.axis_size("lat")
    plane = rows_here * cols_here
    own_cols = cols_here - SHIFT_LON
    wx = weather.reshape(levels, plane, CH)
    gx = cotangent.reshape(levels, plane, CH)
    edge = SHIFT_LAT * SHIFT_LON
    lat_shape = sds((levels, SHIFT_LAT * own_cols, 2 * CH), BF)
    edge_shape = sds((levels, edge, 2 * CH), BF)
    slat, scor = scatter_matrices(cols_here)
    scatter = (slat, scor[:, :edge], scor[:, edge:])
    strips = call(prep_kernel, (lat_shape, edge_shape, edge_shape), count=5, flops=10**9)(
        wx, gx, *[jnp.asarray(m.T, BF) for m in scatter]
    )
    lat_in = passed(strips[0], -1, 0)
    lon_in = passed(strips[1], 0, -1)
    diag_in = passed(strips[2], -1, -1)

    lev_windows = bias_table.shape[0]
    table = bias_table.reshape(lev_windows, HEADS, WLEV, WLEV, WLAT, WLAT, SPAN)
    table = table.transpose(0, 1, 3, 5, 2, 4, 6).reshape(lev_windows * HEADS * GROUPS, GROUPS * SPAN)
    place_lat = jnp.stack([lat_index, lat_count - 1]).astype(jnp.int32)
    sel = jnp.asarray(lon_selectors(), BF)
    bias_rows = lev_windows * HEADS * TOK
    bias_shape = sds((bias_rows, LANES), F32)
    bias_main, bias_rest = call(
        expand_kernel, (bias_shape, bias_shape), smem=1, count=3, flops=10**9
    )(place_lat, table, sel)

    own_m, lat_m, corner_m = gather_matrices(cols_here)
    mats = [jnp.asarray(m, BF) for m in (own_m, lat_m, corner_m[:, :edge], corner_m[:, edge:])]
    wqkv = qkv_weight.reshape(CH, 3, CH).transpose(1, 0, 2)
    n_win = 8
    plane_shape = sds((levels, plane, CH), BF)
    core = lax.axis_index("core").astype(jnp.int32).reshape(1)
    half_shape = sds((PAY // 2, LANES), BF)
    base, gbase, lat_out, lon_out, diag_out, keep, send = call(
        main_kernel,
        (
            plane_shape, plane_shape, lat_shape, edge_shape, edge_shape,
            half_shape, half_shape,
        ),
        scratch=[pltpu.VMEM((n_win, TOK, CH), F32)] * 4
        + [pltpu.VMEM((bias_rows, LANES), F32)] * 2
        + [
            pltpu.VMEM((3, CH, CH), F32), pltpu.VMEM((CH, CH), F32), pltpu.VMEM((1, CH), F32),
            pltpu.VMEM((BIAS_ROWS, 3 * LANES), F32), pltpu.VMEM((PAY, LANES), F32),
        ],
        smem=1,
        count=16,
        flops=10**10,
    )(core, wx, gx, lat_in, lon_in, diag_in, norm_gain.reshape(1, CH), wqkv, proj_weight, bias_main, bias_rest, sel, *mats)

    lat_back = passed(lat_out, 1, 0)
    lon_back = passed(lon_out, 0, 1)
    diag_back = passed(diag_out, 1, 1)
    mine, other = total_over_devices(keep, send)
    factor = (samples * levels * rows_here * cols_here * lax.axis_size(("ylo", "core", "yhi", "z", "lat"))) ** (-0.5)
    pairs = lev_windows * HEADS
    entries = bias_table.shape[-1]
    out, gout, gqkv, gproj, ggain, gbias = call(
        functools.partial(finish_kernel, factor),
        (
            plane_shape, plane_shape, sds(qkv_weight.shape, F32), sds(proj_weight.shape, F32),
            sds((1, CH), F32), sds((pairs, 1, entries), F32),
        ),
        scratch=[pltpu.VMEM((PAY, LANES), F32), pltpu.VMEM((pairs, -(-entries // LANES) * LANES), F32)],
        smem=1,
        count=11,
        flops=10**9,
    )(core, base, gbase, lat_back, lon_back, diag_back, *[jnp.asarray(m, BF) for m in scatter], mine, other)
    return (
        out.reshape(weather.shape),
        gout.reshape(weather.shape),
        gqkv,
        gproj,
        ggain.reshape(CH),
        gbias.reshape(lev_windows, HEADS, 1, entries).transpose(0, 2, 1, 3),
    )


def solution(mesh):
    fine = jax.sharding.Mesh(mesh.devices.reshape(2, 2, 2, 8, 4), ("ylo", "core", "yhi", "z", "lat"))
    dp, lon = ("ylo", "core"), ("yhi", "z")
    grid = P(dp, None, "lat", lon, None)
    table = P(None, "lat", None, None)
    return jax.shard_map(
        shards,
        mesh=fine,
        in_specs=(grid, grid, P(), P(), P(), table),
        out_specs=(grid, grid, P(), P(), P(), table),
        check_vma=False,
    )
```

time: 631 us -> 138 us (0.22); the launches traced: 622 us -> 137 us
  waiting for transfers between devices: 254 us -> 25.9 us
  local copies, waits for them, and re-layouts: 148 us -> 10.3 us
  matrix products: 91.9 us -> 0 us
  blocking collectives: 76.4 us -> 13.6 us
  Pallas kernels: 0 us -> 56.8 us
  other arithmetic: 22.6 us -> 1.66 us
  between operations: 14.9 us -> 0.78 us
  starting transfers between devices: 14.5 us -> 28.5 us
    psum x1 -> x0, waiting for transfers between devices: 240 us -> none  [shards(): lax.psum((grad_qkv, grad_proj, grad_gain, padded), ('dp', 'lon', 'lat'))]
    dot_general x28 -> x0, matrix products: 83.8 us -> none  [the longest x1 43.7 us: fold_bias(): jnp.einsum('lahzuxyvw,dxw->lahzyuvd', shaped, picker, precision=lax.Preci...]
    psum x1 -> x0, blocking collectives: 76.4 us -> none  [shards(): lax.psum((grad_qkv, grad_proj, grad_gain, padded), ('dp', 'lon', 'lat'))]
    while x42 -> x0, local copies, waits for them, and re-layouts: 58.8 us -> none  [the longest x2 58.7 us: shards(): lax.map(attend, (query_win, key_win, value_win, grad_win, bias_full, grou...]
    pallas_call x0 -> x4, Pallas kernels: none -> 56.8 us  [the longest x1 38.2 us: shards(): call(main_kernel, (plane_shape, plane_shape, lat_shape, edge_shape, edge_...]
    dynamic_update_slice x29 -> x0, local copies, waits for them, and re-layouts: 29.7 us -> none  [the longest x28 26.8 us: shards(): lax.map(attend, (query_win, key_win, value_win, grad_win, bias_full, grou...]
    another operation x10 -> x0, local copies, waits for them, and re-layouts: 24.6 us -> none
    all_to_all x0 -> x1, blocking collectives: none -> 13.6 us  [total_over_devices(): pieces = lax.all_to_all(half, wide, 0, 0, tiled=True)]
  transfers between devices with their start and end apart: 9 -> 12, of which waited for: 4 -> 6; matrix products, arithmetic and copies ran while one was open for 16% -> 6% of each run, Pallas kernels for 0% -> 6%
where the time goes in v1:
time: 138 us; the launch traced here: 137 us
  Pallas kernels  56.8 us (41%)
  starting transfers between devices  28.5 us (21%)
  waiting for transfers between devices  25.9 us (19%)
  blocking collectives  13.6 us (10%)
  local copies, waits for them, and re-layouts  10.3 us (7%)
  other arithmetic  1.66 us (1%)
    pallas_call x1, Pallas kernels, shards(): call(main_kernel, (plane_shape, plane_shape, lat_shape, edge_shape, edge_...  38.2 us
    ppermute x6, starting transfers between devices, passed(): return lax.ppermute(value, ('yhi', 'z', 'lat'), pairs)  14.2 us
    all_to_all x1, blocking collectives, total_over_devices(): pieces = lax.all_to_all(half, wide, 0, 0, tiled=True)  13.6 us
    ppermute x6, waiting for transfers between devices, passed(): return lax.ppermute(value, ('yhi', 'z', 'lat'), pairs)  10.8 us
    all_to_all x1, waiting for transfers between devices, total_over_devices(): mine = lax.all_to_all(spread, wide, 0, 0, tiled=True)  9.89 us
    pallas_call x1, Pallas kernels, shards(): call(expand_kernel, (bias_shape, bias_shape), smem=1, count=3, flops=10 *...  8.31 us
    pallas_call x1, Pallas kernels, shards(): call(functools.partial(finish_kernel, factor), (plane_shape, plane_shape,...  6.11 us
    ppermute x2, starting transfers between devices, swapped(): return lax.ppermute(value, 'core', [(0, 1), (1, 0)])  5.83 us
  transfers between devices with their start and end apart: 12, of which 6 were waited for; matrix products, arithmetic and copies ran while one was open for 6% of the time, Pallas kernels for 6%

profile of v1, /device:TPU:1, one launch (start us, length us, event | category | flops | bytes accessed | tf_op | source)
XLA Modules:
  0.0 137.5 jit_solution(12216544492035974232)
XLA Ops:
  0.7 4.2 %shard_map.208 = (bf16[8,54,384]{2,1,0:T(8,128)(2,1)}, bf16[8,18,384]{2,1,0:T(8,128)(2,1)}, bf16[8,18,384]{2,1,0:T(8,128)(2,1)}) custom-call(bf16[8,144,192]{2,1,0:T(8,128)(2,1)} %bitcast.22, bf16[8,144,192]{2,1,0:T(8,128)(2,1)} %bitcast.24, bf16[54,144]{1,0:T(8,128)(2,1)} %constant.58.clone.lat_pick, bf16[18,144]{1,0:T(8,128)(2,1)} %constant.59.clone.lon_pick, ...), custom_call_target="tpu_custom_call" | custom-call | flops 1000000000 | bytes 2000000 | tf_op jit(solution)/shard_map/pallas_call | solution.py:396
  4.9 3.3 %collective-permute-start = (bf16[8,54,384]{2,1,0:T(8,128)(2,1)}, bf16[8,54,384]{2,1,0:T(8,128)(2,1)S(1)}, u32[]{:S(2)}, u32[]{:S(2)}) collective-permute-start(bf16[8,54,384]{2,1,0:T(8,128)(2,1)} %get-tuple-element.24), channel_id=1, source_target_pairs={{0,3},{1,0},{2,1},{3,2},{4,7},{5,4},{6,5},{7,6},{8,11},{9,8},{10,9... | collective-permute-start | bytes 995336 | tf_op jit(solution)/shard_map/ppermute | solution.py:340
  8.2 8.2 %collective-permute-start.1 = (bf16[8,18,384]{2,1,0:T(8,128)(2,1)}, bf16[8,18,384]{2,1,0:T(8,128)(2,1)S(1)}, u32[]{:S(2)}, u32[]{:S(2)}) collective-permute-start(bf16[8,18,384]{2,1,0:T(8,128)(2,1)} %get-tuple-element.25), channel_id=1, source_target_pairs={{0,60},{1,61},{2,62},{3,63},{4,0},{5,1},{6,2},{7,3},{8,4},{9,5},{1... | collective-permute-start | bytes 331784 | tf_op jit(solution)/shard_map/ppermute | solution.py:340
  16.4 1.0 collective-permute-start.2
  17.4 0.6 pad_add_fusion.lat_ref
  17.9 0.0 copy-done.2
  17.9 0.2 copy.24
  18.1 0.9 copy.25
  19.0 0.0 copy-done
  19.0 0.1 copy.26
  19.1 1.7 %reshape.56 = f32[4,6,2,2,6,6,23]{6,5,4,3,2,0,1:T(8,128)S(1)} reshape(f32[4,1,6,3312]{3,0,2,1:T(4,128)S(1)} %copy.26) | data formatting | bytes 635904 | tf_op jit(solution)/shard_map/reshape | solution.py:404
  20.8 2.0 %copy.27 = f32[4,6,2,6,2,6,23]{6,5,4,3,2,1,0:T(8,128)} copy(f32[4,6,2,6,2,6,23]{6,3,5,2,4,0,1:T(8,128)S(1)} %bitcast.16) | data formatting | bytes 635904 | tf_op jit(solution)/shard_map/transpose | solution.py:405
  22.8 3.0 %reshape.57.table_ref = f32[288,276]{1,0:T(8,128)} reshape(f32[4,6,2,6,2,6,23]{6,5,4,3,2,1,0:T(8,128)} %copy.27) | data formatting | bytes 635904 | tf_op jit(solution)/shard_map/reshape | solution.py:405
  25.8 8.3 %shard_map.209 = (f32[3456,128]{1,0:T(8,128)}, f32[3456,128]{1,0:T(8,128)}) custom-call(s32[2]{0:T(128)} %pad_add_fusion.lat_ref, f32[288,276]{1,0:T(8,128)} %reshape.57.table_ref, bf16[12,384,256]{2,1,0:T(8,128)(2,1)} %constant.61.clone.sel_ref), custom_call_target="tpu_custom_call" | custom-call | flops 1000000000 | bytes 2000000 | tf_op jit(solution)/shard_map/pallas_call | solution.py:410
  34.1 0.0 collective-permute-done.1.lon_in
  34.2 0.0 collective-permute-done.2.diag_in
  34.2 0.0 collective-permute-done.lat_in
  34.2 0.0 copy-start.4
  34.2 0.6 copy-done.9
  34.8 0.1 copy-done.10
  34.9 0.1 copy-done.4
  35.0 38.2 %shard_map.210 = (bf16[8,144,192]{2,1,0:T(8,128)(2,1)}, bf16[8,144,192]{2,1,0:T(8,128)(2,1)}, bf16[8,54,384]{2,1,0:T(8,128)(2,1)}, bf16[8,18,384]{2,1,0:T(8,128)...) custom-call(s32[1]{0:T(128)} %bitcast.core_ref, ...), custom_call_target="tpu_custom_call" | custom-call | flops 10000000000 | bytes 20000000 | tf_op jit(solution)/shard_map/pallas_call | solution.py:421
  73.1 0.0 copy-start.7
  73.2 1.6 %collective-permute-start.6 = (bf16[1024,128]{1,0:T(8,128)(2,1)}, bf16[1024,128]{1,0:T(8,128)(2,1)S(1)}, u32[]{:S(2)}, u32[]{:S(2)}) collective-permute-start(bf16[1024,128]{1,0:T(8,128)(2,1)} %get-tuple-element.35), channel_id=1, source_target_pairs={{0,64},{64,0},{1,65},{65,1},{2,66},{66,2},{3,67},{67,3},{4,68},{68... | collective-permute-start | bytes 786440 | tf_op jit(solution)/shard_map/ppermute | solution.py:344
  74.8 1.4 collective-permute-done.6
  76.1 1.0 add_convert_fusion
  77.2 13.6 %all_to_all.17 = bf16[32,32,128]{2,1,0:T(8,128)(2,1)S(1)} all-to-all(bf16[32,32,128]{2,1,0:T(8,128)(2,1)S(1)} %bitcast.18), channel_id=1, replica_groups=mesh['ylo'=2,'core'=2,'yhi'=2,'z'=8,'lat'=4] {'ylo','yhi','z'}, dimensions={0} | all-to-all | bytes 524288 | tf_op jit(solution)/shard_map/all_to_all | solution.py:351
  90.8 0.3 collective-permute-start.9
  91.1 2.4 %collective-permute-start.8 = (f32[32,128]{1,0:T(8,128)S(1)}, f32[32,128]{1,0:T(8,128)S(1)}, u32[]{:S(2)}, u32[]{:S(2)}) collective-permute-start(f32[32,128]{1,0:T(8,128)S(1)} %convert_reduce_fusion), channel_id=1, source_target_pairs={{0,2},{1,3},{2,0},{3,1},{4,6},{5,7},{6,4},{7,5},{8,10},{9,11},{10,... | collective-permute-start | bytes 49160 | tf_op jit(solution)/shard_map/ppermute | solution.py:358
  93.5 0.0 collective-permute-start.7
  93.6 0.0 collective-permute-done.9
  93.6 1.6 %collective-permute-done.8 = f32[32,128]{1,0:T(8,128)S(1)} collective-permute-done((f32[32,128]{1,0:T(8,128)S(1)}, f32[32,128]{1,0:T(8,128)S(1)}, u32[]{:S(2)}, u32[]{:S(2)}) %collective-permute-start.8) | collective-permute-done | bytes 16416 | tf_op jit(solution)/shard_map/ppermute | solution.py:358
  95.2 2.2 %collective-permute-done.7 = f32[32,128]{1,0:T(8,128)S(1)} collective-permute-done((f32[32,128]{1,0:T(8,128)S(1)}, f32[32,128]{1,0:T(8,128)S(1)}, u32[]{:S(2)}, u32[]{:S(2)}) %collective-permute-start.7) | collective-permute-done | bytes 16416 | tf_op jit(solution)/shard_map/ppermute | solution.py:358
  97.4 0.7 broadcast_in_dim.2
  98.1 5.8 %all-to-all-start.1 = ((bf16[32,32,128]{2,1,0:T(8,128)(2,1)}), bf16[32,32,128]{2,1,0:T(8,128)(2,1)S(1)}, u32[]{:S(2)}, u32[]{:S(2)}) async-start(bf16[32,32,128]{2,1,0:T(8,128)(2,1)} %broadcast_in_dim.2), calls=%async_computation.1 | async-start | bytes 524288 | tf_op jit(solution)/shard_map/all_to_all | solution.py:361
  103.9 0.1 collective-permute-start.3
  104.0 9.9 %all-to-all-done.1 = bf16[32,32,128]{2,1,0:T(8,128)(2,1)S(1)} async-done(((bf16[32,32,128]{2,1,0:T(8,128)(2,1)}), bf16[32,32,128]{2,1,0:T(8,128)(2,1)S(1)}, u32[]{:S(2)}, u32[]{:S(2)}) %all-to-all-start.1) | async-done | bytes 262176 | tf_op jit(solution)/shard_map/all_to_all | solution.py:361
  113.9 4.2 %collective-permute-start.10 = (bf16[1024,128]{1,0:T(8,128)(2,1)S(1)}, bf16[1024,128]{1,0:T(8,128)(2,1)S(1)}, u32[]{:S(2)}, u32[]{:S(2)}) collective-permute-start(bf16[1024,128]{1,0:T(8,128)(2,1)S(1)} %bitcast.20), channel_id=1, source_target_pairs={{0,64},{64,0},{1,65},{65,1},{2,66},{66,2},{3,67},{67,3},{4,68},{68... | collective-permute-start | bytes 786440 | tf_op jit(solution)/shard_map/ppermute | solution.py:344
  118.1 1.6 %collective-permute-start.4 = (bf16[8,18,384]{2,1,0:T(8,128)(2,1)S(1)}, bf16[8,18,384]{2,1,0:T(8,128)(2,1)S(1)}, u32[]{:S(2)}, u32[]{:S(2)}) collective-permute-start(bf16[8,18,384]{2,1,0:T(8,128)(2,1)S(1)} %copy-done.8), channel_id=1, source_target_pairs={{0,4},{1,5},{2,6},{3,7},{4,8},{5,9},{6,10},{7,11},{8,12},{9,13},{1... | collective-permute-start | bytes 331784 | tf_op jit(solution)/shard_map/ppermute | solution.py:340
  119.7 0.0 collective-permute-start.5
  119.7 7.5 %collective-permute-done.4.lon_in = bf16[8,18,384]{2,1,0:T(8,128)(2,1)S(1)} collective-permute-done((bf16[8,18,384]{2,1,0:T(8,128)(2,1)S(1)}, bf16[8,18,384]{2,1,0:T(8,128)(2,1)S(1)}, u32[]{:S(2)}, u32[]{:S(2)}) %collective-permute-start.4) | collective-permute-done | bytes 110624 | tf_op jit(solution)/shard_map/ppermute | solution.py:340
  127.1 3.3 %collective-permute-done.5.diag_in = bf16[8,18,384]{2,1,0:T(8,128)(2,1)S(1)} collective-permute-done((bf16[8,18,384]{2,1,0:T(8,128)(2,1)S(1)}, bf16[8,18,384]{2,1,0:T(8,128)(2,1)S(1)}, u32[]{:S(2)}, u32[]{:S(2)}) %collective-permute-start.5) | collective-permute-done | bytes 110624 | tf_op jit(solution)/shard_map/ppermute | solution.py:340
  130.5 0.0 collective-permute-done.3.lat_in
  130.5 0.0 collective-permute-done.10.other_ref
  130.5 0.6 copy-done.12
  131.1 0.1 copy-done.5
  131.3 0.1 copy-done.6
  131.4 6.1 %shard_map.211 = (bf16[8,144,192]{2,1,0:T(8,128)(2,1)}, bf16[8,144,192]{2,1,0:T(8,128)(2,1)}, f32[192,576]{1,0:T(8,128)}, f32[192,192]{1,0:T(8,128)}, f32[1,192]{1,0:T(1,128)}, /*index=5*/f32[24,1,3312]{2,1,0:T(1,128)}) custom-call(s32[1]{0:T(128)} %bitcast.core_ref, bf16[8,144,192]{2,1,0:T(8,128)(2,1)} %get-tuple-element.29.base_ref, ...), custom_call_target="tpu_custom_call" | custom-call | flops 1000000000 | bytes 2000000 | tf_op jit(solution)/shard_map/pallas_call | solution.py:445
  (18 shorter events, 0.1 us)
Async XLA Ops:
  0.6 17.3 %copy-start.2 = (bf16[192,576]{1,0:T(8,128)(2,1)S(1)}, bf16[192,576]{1,0:T(8,128)(2,1)}, u32[]{:S(2)}) copy-start(bf16[192,576]{1,0:T(8,128)(2,1)} %param.20) | copy-start | bytes 663556
  0.6 18.4 %copy-start = (f32[4,1,6,3312]{3,1,2,0:T(1,128)S(1)}, f32[4,1,6,3312]{3,1,2,0:T(1,128)}, u32[]{:S(2)}) copy-start(f32[4,1,6,3312]{3,1,2,0:T(1,128)} %param.22) | copy-start | bytes 953860
  4.9 29.3 %collective-permute-start = (bf16[8,54,384]{2,1,0:T(8,128)(2,1)}, bf16[8,54,384]{2,1,0:T(8,128)(2,1)S(1)}, u32[]{:S(2)}, u32[]{:S(2)}) collective-permute-start(bf16[8,54,384]{2,1,0:T(8,128)(2,1)} %get-tuple-element.24), channel_id=1, source_target_pairs={{0,3},{1,0},{2,1},{3,2},{4,7},{5,4},{6,5},{7,6},{8,11},{9,8},{10,9... | collective-permute-start | bytes 995336 | tf_op jit(solution)/shard_map/ppermute | solution.py:340
  8.2 26.0 %collective-permute-start.1 = (bf16[8,18,384]{2,1,0:T(8,128)(2,1)}, bf16[8,18,384]{2,1,0:T(8,128)(2,1)S(1)}, u32[]{:S(2)}, u32[]{:S(2)}) collective-permute-start(bf16[8,18,384]{2,1,0:T(8,128)(2,1)} %get-tuple-element.25), channel_id=1, source_target_pairs={{0,60},{1,61},{2,62},{3,63},{4,0},{5,1},{6,2},{7,3},{8,4},{9,5},{1... | collective-permute-start | bytes 331784 | tf_op jit(solution)/shard_map/ppermute | solution.py:340
  16.4 17.8 %collective-permute-start.2 = (bf16[8,18,384]{2,1,0:T(8,128)(2,1)}, bf16[8,18,384]{2,1,0:T(8,128)(2,1)S(1)}, u32[]{:S(2)}, u32[]{:S(2)}) collective-permute-start(bf16[8,18,384]{2,1,0:T(8,128)(2,1)} %get-tuple-element.26), channel_id=1, source_target_pairs={{0,63},{1,60},{2,61},{3,62},{4,3},{5,0},{6,1},{7,2},{8,7},{9,4},{1... | collective-permute-start | bytes 331784 | tf_op jit(solution)/shard_map/ppermute | solution.py:340
  34.2 0.7 copy-start.9
  34.2 0.7 copy-start.10
  34.2 0.8 copy-start.4
  73.1 30.7 %copy-start.3 = (bf16[8,54,384]{2,1,0:T(8,128)(2,1)S(1)}, bf16[8,54,384]{2,1,0:T(8,128)(2,1)}, u32[]{:S(2)}) copy-start(bf16[8,54,384]{2,1,0:T(8,128)(2,1)} %get-tuple-element.31) | copy-start | bytes 995332
  73.1 45.0 %copy-start.8 = (bf16[8,18,384]{2,1,0:T(8,128)(2,1)S(1)}, bf16[8,18,384]{2,1,0:T(8,128)(2,1)}, u32[]{:S(2)}) copy-start(bf16[8,18,384]{2,1,0:T(8,128)(2,1)} %get-tuple-element.32) | copy-start | bytes 331780
  73.1 46.5 %copy-start.7 = (bf16[8,18,384]{2,1,0:T(8,128)(2,1)S(1)}, bf16[8,18,384]{2,1,0:T(8,128)(2,1)}, u32[]{:S(2)}) copy-start(bf16[8,18,384]{2,1,0:T(8,128)(2,1)} %get-tuple-element.33) | copy-start | bytes 331780
  73.2 3.0 %collective-permute-start.6 = (bf16[1024,128]{1,0:T(8,128)(2,1)}, bf16[1024,128]{1,0:T(8,128)(2,1)S(1)}, u32[]{:S(2)}, u32[]{:S(2)}) collective-permute-start(bf16[1024,128]{1,0:T(8,128)(2,1)} %get-tuple-element.35), channel_id=1, source_target_pairs={{0,64},{64,0},{1,65},{65,1},{2,66},{66,2},{3,67},{67,3},{4,68},{68... | collective-permute-start | bytes 786440 | tf_op jit(solution)/shard_map/ppermute | solution.py:344
  90.8 2.8 %collective-permute-start.9 = (f32[32,128]{1,0:T(8,128)S(1)}, f32[32,128]{1,0:T(8,128)S(1)}, u32[]{:S(2)}, u32[]{:S(2)}) collective-permute-start(f32[32,128]{1,0:T(8,128)S(1)} %convert_reduce_fusion), channel_id=1, source_target_pairs={{0,3},{1,0},{2,1},{3,2},{4,7},{5,4},{6,5},{7,6},{8,11},{9,8},{10,9... | collective-permute-start | bytes 49160 | tf_op jit(solution)/shard_map/ppermute | solution.py:358
  91.1 4.1 %collective-permute-start.8 = (f32[32,128]{1,0:T(8,128)S(1)}, f32[32,128]{1,0:T(8,128)S(1)}, u32[]{:S(2)}, u32[]{:S(2)}) collective-permute-start(f32[32,128]{1,0:T(8,128)S(1)} %convert_reduce_fusion), channel_id=1, source_target_pairs={{0,2},{1,3},{2,0},{3,1},{4,6},{5,7},{6,4},{7,5},{8,10},{9,11},{10,... | collective-permute-start | bytes 49160 | tf_op jit(solution)/shard_map/ppermute | solution.py:358
  93.5 3.8 %collective-permute-start.7 = (f32[32,128]{1,0:T(8,128)S(1)}, f32[32,128]{1,0:T(8,128)S(1)}, u32[]{:S(2)}, u32[]{:S(2)}) collective-permute-start(f32[32,128]{1,0:T(8,128)S(1)} %convert_reduce_fusion), channel_id=1, source_target_pairs={{0,1},{1,2},{2,3},{3,0},{4,5},{5,6},{6,7},{7,4},{8,9},{9,10},{10,1... | collective-permute-start | bytes 49160 | tf_op jit(solution)/shard_map/ppermute | solution.py:358
  98.1 15.8 %all-to-all-start.1 = ((bf16[32,32,128]{2,1,0:T(8,128)(2,1)}), bf16[32,32,128]{2,1,0:T(8,128)(2,1)S(1)}, u32[]{:S(2)}, u32[]{:S(2)}) async-start(bf16[32,32,128]{2,1,0:T(8,128)(2,1)} %broadcast_in_dim.2), calls=%async_computation.1 | async-start | bytes 524288 | tf_op jit(solution)/shard_map/all_to_all | solution.py:361
  103.9 26.6 %collective-permute-start.3 = (bf16[8,54,384]{2,1,0:T(8,128)(2,1)S(1)}, bf16[8,54,384]{2,1,0:T(8,128)(2,1)S(1)}, u32[]{:S(2)}, u32[]{:S(2)}) collective-permute-start(bf16[8,54,384]{2,1,0:T(8,128)(2,1)S(1)} %copy-done.3), channel_id=1, source_target_pairs={{0,1},{1,2},{2,3},{3,0},{4,5},{5,6},{6,7},{7,4},{8,9},{9,10},{10,1... | collective-permute-start | bytes 995336 | tf_op jit(solution)/shard_map/ppermute | solution.py:340
  113.9 16.6 %copy-start.1 = (bf16[32,32,128]{2,1,0:T(8,128)(2,1)}, bf16[32,32,128]{2,1,0:T(8,128)(2,1)S(1)}, u32[]{:S(2)}) copy-start(bf16[32,32,128]{2,1,0:T(8,128)(2,1)S(1)} %all-to-all-done.1) | copy-start | bytes 786436
  113.9 16.6 %collective-permute-start.10 = (bf16[1024,128]{1,0:T(8,128)(2,1)S(1)}, bf16[1024,128]{1,0:T(8,128)(2,1)S(1)}, u32[]{:S(2)}, u32[]{:S(2)}) collective-permute-start(bf16[1024,128]{1,0:T(8,128)(2,1)S(1)} %bitcast.20), channel_id=1, source_target_pairs={{0,64},{64,0},{1,65},{65,1},{2,66},{66,2},{3,67},{67,3},{4,68},{68... | collective-permute-start | bytes 786440 | tf_op jit(solution)/shard_map/ppermute | solution.py:344
  118.1 9.0 %collective-permute-start.4 = (bf16[8,18,384]{2,1,0:T(8,128)(2,1)S(1)}, bf16[8,18,384]{2,1,0:T(8,128)(2,1)S(1)}, u32[]{:S(2)}, u32[]{:S(2)}) collective-permute-start(bf16[8,18,384]{2,1,0:T(8,128)(2,1)S(1)} %copy-done.8), channel_id=1, source_target_pairs={{0,4},{1,5},{2,6},{3,7},{4,8},{5,9},{6,10},{7,11},{8,12},{9,13},{1... | collective-permute-start | bytes 331784 | tf_op jit(solution)/shard_map/ppermute | solution.py:340
  119.7 10.8 %collective-permute-start.5 = (bf16[8,18,384]{2,1,0:T(8,128)(2,1)S(1)}, bf16[8,18,384]{2,1,0:T(8,128)(2,1)S(1)}, u32[]{:S(2)}, u32[]{:S(2)}) collective-permute-start(bf16[8,18,384]{2,1,0:T(8,128)(2,1)S(1)} %copy-done.7), channel_id=1, source_target_pairs={{0,5},{1,6},{2,7},{3,4},{4,9},{5,10},{6,11},{7,8},{8,13},{9,14},{1... | collective-permute-start | bytes 331784 | tf_op jit(solution)/shard_map/ppermute | solution.py:340
  127.1 3.4 %copy-start.11 = (bf16[8,18,384]{2,1,0:T(8,128)(2,1)}, bf16[8,18,384]{2,1,0:T(8,128)(2,1)S(1)}, u32[]{:S(2)}) copy-start(bf16[8,18,384]{2,1,0:T(8,128)(2,1)S(1)} %collective-permute-done.4.lon_in) | copy-start | bytes 331780
  130.5 0.6 copy-start.12
  130.5 0.8 copy-start.5
  130.5 0.9 copy-start.6

commit v2 on v1

--- a/solution.py
+++ b/solution.py
@@ -101,35 +101,42 @@
             ).astype(BF)
         return carry
 
-    lax.fori_loop(0, wx_ref.shape[0], step, 0)
-
-
-def expand_kernel(lat_ref, table_ref, sel_ref, main_ref, rest_ref):
-    table = table_ref[...]
-    high = table.astype(BF)
-    rest = table - high.astype(F32)
-    mid = rest.astype(BF)
-    low = (rest - mid.astype(F32)).astype(BF)
-    rows = table.shape[0]
-    last = lat_ref[0] == lat_ref[1]
+    lax.fori_loop(0, wx_ref.shape[0], step, 0, unroll=True)
+
+
+def expand_kernel(last_ref, table_ref, sel_ref, main_ref, rest_ref, flat_s, table_s):
+    pairs, _, entries = table_ref.shape
+    for r in range(pairs):
+        flat_s[r : r + 1, :entries] = table_ref[r]
+    for m in range(GROUPS):
+        z_j, a_j = divmod(m, WLAT)
+        for g in range(GROUPS):
+            z_i, a_i = divmod(g, WLAT)
+            at = SPAN * (((z_i * WLEV + z_j) * WLAT + a_i) * WLAT + a_j)
+            table_s[m * pairs : (m + 1) * pairs, g * SPAN : (g + 1) * SPAN] = flat_s[:, at : at + SPAN]
+    high, low = split(table_s[...])
+    rows = BIAS_ROWS
     row_id = lax.broadcasted_iota(jnp.int32, (rows, 2 * LANES), 0)
     col_id = lax.broadcasted_iota(jnp.int32, (rows, 2 * LANES), 1)
-    a_j = row_id % WLAT
-    z_j = (row_id // WLAT) % WLEV
-    a_i = (col_id // WLON) % WLAT
+    z_j = row_id // (WLAT * pairs)
+    a_j = row_id // pairs % WLAT
+    lev = row_id % pairs // HEADS
+    a_i = col_id // WLON % WLAT
     z_i = col_id // (WLON * WLAT)
-    cross_lev = jnp.logical_and(row_id >= rows * 3 // 4, z_j != z_i)
-    cross_lat = jnp.logical_and(last, (a_j >= SHIFT_LAT) != (a_i >= SHIFT_LAT))
+    cross_lev = jnp.logical_and(lev == pairs // HEADS - 1, z_j != z_i)
+    cross_lat = jnp.logical_and(last_ref[0] == 1, (a_j >= SHIFT_LAT) != (a_i >= SHIFT_LAT))
     hide = jnp.where(jnp.logical_or(cross_lev, cross_lat), MASKED, 0.0)
 
     def step(xj, carry):
         sel = sel_ref[xj, : GROUPS * SPAN]
-        value = dot(high, sel) + dot(mid, sel) + dot(low, sel) + hide
-        main_ref[pl.ds(xj, rows, stride=WLON), :] = value[:, :LANES]
-        rest_ref[pl.ds(xj, rows, stride=WLON), :] = value[:, LANES:]
-        return carry
-
-    lax.fori_loop(0, WLON, step, 0)
+        value = dot(high, sel) + dot(low, sel) + hide
+        for m in range(GROUPS):
+            at = pl.ds(m * WLON + xj, pairs, stride=TOK)
+            main_ref[at, :] = value[m * pairs : (m + 1) * pairs, :LANES]
+            rest_ref[at, :] = value[m * pairs : (m + 1) * pairs, LANES:]
+        return carry
+
+    lax.fori_loop(0, WLON, step, 0, unroll=4)
 
 
 def main_kernel(
@@ -158,7 +165,7 @@
             g_s[2 * k + n, pl.ds(pl.multiple_of(z * half, 8), half), :] = gw[n * half : (n + 1) * half]
         return carry
 
-    lax.fori_loop(0, 8, load_level, 0)
+    lax.fori_loop(0, 8, load_level, 0, unroll=True)
     dsum_main[...] = jnp.zeros_like(dsum_main)
     dsum_rest[...] = jnp.zeros_like(dsum_rest)
     gw_ref[...] = jnp.zeros_like(gw_ref)
@@ -189,29 +196,34 @@
         key_t = dot(eye_c, key, 1, 1).astype(BF)
         v_t = dot(eye_c, v, 1, 1).astype(BF)
         zero = jnp.zeros((TOK, CH), BF)
-        att_parts = []
-        dq_parts = []
-        d_key = jnp.zeros((TOK, CH), F32)
-        d_val = jnp.zeros((TOK, CH), F32)
-        for h in range(HEADS):
-            lo, hi = h * HD, (h + 1) * HD
-            s = dot(jnp.where(head_mask[h], key, zero), q, 1, 1)
-            rows = pl.ds(pl.multiple_of((k * HEADS + h) * TOK, 8), TOK)
-            s = s + jnp.concatenate([bias_main[rows, :], bias_rest[rows, : TOK - LANES]], axis=1)
-            s = s - jnp.max(s, axis=0, keepdims=True)
-            e = jnp.exp(s)
-            probs = (e / jnp.sum(e, axis=0, keepdims=True)).astype(BF)
-            dp = dot(jnp.where(head_mask[h], v, zero), d_att, 1, 1)
-            att_parts.append(dot(v_t[lo:hi], probs))
-            d_val = d_val + dot(probs, jnp.where(head_mask[h], d_att, zero))
-            pf = probs.astype(F32)
-            t = pf * dp
-            ds = t - pf * jnp.sum(t, axis=0, keepdims=True)
-            dsum_main[rows, :] += ds[:, :LANES]
-            dsum_rest[rows, : TOK - LANES] += ds[:, LANES:]
-            dsb = ds.astype(BF)
-            dq_parts.append(dot(key_t[lo:hi], dsb))
-            d_key = d_key + dot(dsb, jnp.where(head_mask[h], q, zero))
+
+        def per_head(value):
+            return jnp.concatenate([jnp.where(mask, value, zero) for mask in head_mask], axis=0)
+
+        def own_head(value):
+            total = jnp.where(head_mask[0], value[:TOK], 0.0)
+            for h in range(1, HEADS):
+                total = jnp.where(head_mask[h], value[h * TOK : (h + 1) * TOK], total)
+            return total
+
+        rows = pl.ds(pl.multiple_of(k * HEADS * TOK, 8), HEADS * TOK)
+        scores = dot(per_head(key), q, 1, 1)
+        scores = scores + jnp.concatenate([bias_main[rows, :], bias_rest[rows, : TOK - LANES]], axis=1)
+        scores = scores.reshape(HEADS, TOK, TOK)
+        dp = dot(per_head(v), d_att, 1, 1).reshape(HEADS, TOK, TOK)
+        e = jnp.exp(scores - jnp.max(scores, axis=1, keepdims=True))
+        probs = (e * (1.0 / jnp.sum(e, axis=1, keepdims=True))).astype(BF)
+        d_val = own_head(dot(probs.reshape(HEADS * TOK, TOK), d_att))
+        pf = probs.astype(F32)
+        t = pf * dp
+        ds = t - pf * jnp.sum(t, axis=1, keepdims=True)
+        dsb = ds.astype(BF)
+        ds = ds.reshape(HEADS * TOK, TOK)
+        dsum_main[rows, :] += ds[:, :LANES]
+        dsum_rest[rows, : TOK - LANES] += ds[:, LANES:]
+        d_key = own_head(dot(dsb.reshape(HEADS * TOK, TOK), q))
+        att_parts = [dot(v_t[h * HD : (h + 1) * HD], probs[h]) for h in range(HEADS)]
+        dq_parts = [dot(key_t[h * HD : (h + 1) * HD], dsb[h]) for h in range(HEADS)]
         att_t = jnp.concatenate(att_parts, axis=0).astype(BF)
         dq_t = (jnp.concatenate(dq_parts, axis=0) * inv_root).astype(BF)
         att = dot(eye_t, att_t, 1, 1).astype(BF)
@@ -254,7 +266,7 @@
             ).astype(BF)
         return carry
 
-    lax.fori_loop(0, 8, store_level, 0)
+    lax.fori_loop(0, 8, store_level, 0, unroll=True)
 
     gbias_ref[...] = jnp.zeros_like(gbias_ref)
     pairs = dsum_main.shape[0] // TOK
@@ -326,7 +338,7 @@
         gout_ref[level] = gup.astype(BF)
         return carry
 
-    lax.fori_loop(0, 8, step, 0)
+    lax.fori_loop(0, 8, step, 0, unroll=True)
 
 
 def passed(value, lat_step, lon_step):
@@ -344,7 +356,7 @@
     return lax.ppermute(value, "core", [(0, 1), (1, 0)])
 
 
-def total_over_devices(keep, send):
+def total_over_devices(keep, send, backs):
     wide = ("ylo", "yhi", "z")
     peers = lax.axis_size("ylo") * lax.axis_size("yhi") * lax.axis_size("z")
     half = (keep.astype(F32) + swapped(send).astype(F32)).astype(BF)
@@ -358,8 +370,9 @@
         others = others + lax.ppermute(piece, "lat", [(a, (a + step) % lats) for a in range(lats)])
     piece = jnp.where(shared, piece + others, piece).astype(BF)
     spread = jnp.broadcast_to(piece[None], (peers, PIECE, LANES)).reshape(half.shape)
+    spread, backs = lax.optimization_barrier((spread, backs))
     mine = lax.all_to_all(spread, wide, 0, 0, tiled=True)
-    return mine, swapped(mine)
+    return mine, swapped(mine), backs
 
 
 def call(kernel, out_shape, scratch=(), smem=0, count=0, flops=0):
@@ -401,15 +414,18 @@
     diag_in = passed(strips[2], -1, -1)
 
     lev_windows = bias_table.shape[0]
-    table = bias_table.reshape(lev_windows, HEADS, WLEV, WLEV, WLAT, WLAT, SPAN)
-    table = table.transpose(0, 1, 3, 5, 2, 4, 6).reshape(lev_windows * HEADS * GROUPS, GROUPS * SPAN)
-    place_lat = jnp.stack([lat_index, lat_count - 1]).astype(jnp.int32)
+    pairs = lev_windows * HEADS
+    entries = bias_table.shape[-1]
+    table = bias_table.transpose(0, 2, 1, 3).reshape(pairs, 1, entries)
+    last = (lat_index == lat_count - 1).astype(jnp.int32).reshape(1)
     sel = jnp.asarray(lon_selectors(), BF)
-    bias_rows = lev_windows * HEADS * TOK
+    bias_rows = pairs * TOK
     bias_shape = sds((bias_rows, LANES), F32)
+    flat_shape = pltpu.VMEM((pairs, -(-entries // LANES) * LANES), F32)
     bias_main, bias_rest = call(
-        expand_kernel, (bias_shape, bias_shape), smem=1, count=3, flops=10**9
-    )(place_lat, table, sel)
+        expand_kernel, (bias_shape, bias_shape), scratch=[flat_shape, pltpu.VMEM((BIAS_ROWS, GROUPS * SPAN), F32)],
+        smem=1, count=3, flops=10**9,
+    )(last, table, sel)
 
     own_m, lat_m, corner_m = gather_matrices(cols_here)
     mats = [jnp.asarray(m, BF) for m in (own_m, lat_m, corner_m[:, :edge], corner_m[:, edge:])]
@@ -438,21 +454,19 @@
     lat_back = passed(lat_out, 1, 0)
     lon_back = passed(lon_out, 0, 1)
     diag_back = passed(diag_out, 1, 1)
-    mine, other = total_over_devices(keep, send)
+    mine, other, backs = total_over_devices(keep, send, (lat_back, lon_back, diag_back))
     factor = (samples * levels * rows_here * cols_here * lax.axis_size(("ylo", "core", "yhi", "z", "lat"))) ** (-0.5)
-    pairs = lev_windows * HEADS
-    entries = bias_table.shape[-1]
     out, gout, gqkv, gproj, ggain, gbias = call(
         functools.partial(finish_kernel, factor),
         (
             plane_shape, plane_shape, sds(qkv_weight.shape, F32), sds(proj_weight.shape, F32),
             sds((1, CH), F32), sds((pairs, 1, entries), F32),
         ),
-        scratch=[pltpu.VMEM((PAY, LANES), F32), pltpu.VMEM((pairs, -(-entries // LANES) * LANES), F32)],
+        scratch=[pltpu.VMEM((PAY, LANES), F32), flat_shape],
         smem=1,
         count=11,
         flops=10**9,
-    )(core, base, gbase, lat_back, lon_back, diag_back, *[jnp.asarray(m, BF) for m in scatter], mine, other)
+    )(core, base, gbase, *backs, *[jnp.asarray(m, BF) for m in scatter], mine, other)
     return (
         out.reshape(weather.shape),
         gout.reshape(weather.shape),

time: 138 us -> 114 us (0.83)
  Pallas kernels: 56.8 us -> 42.6 us
  local copies, waits for them, and re-layouts: 10.3 us -> 2.59 us
  waiting for transfers between devices: 25.9 us -> 21.1 us
  starting transfers between devices: 28.5 us -> 31.6 us
    pallas_call x1, Pallas kernels: 38.2 us -> 28.1 us  [shards(): call(main_kernel, (plane_shape, plane_shape, lat_shape, edge_shape, edge_...]
    reshape x2 -> x0, local copies, waits for them, and re-layouts: 4.76 us -> none  [the longest x1 3.01 us: shards(): table.transpose(0, 1, 3, 5, 2, 4, 6)]
    ppermute x6, starting transfers between devices: 14.2 us -> 18.4 us  [passed(): return lax.ppermute(value, ('yhi', 'z', 'lat'), pairs)]
    ppermute x3, waiting for transfers between devices: 3.8 us -> 0.01 us  [total_over_devices(): lax.ppermute(piece, 'lat', [(a, (a + step) % lats) for a in range(lats)])]
    pallas_call x1, Pallas kernels: 6.11 us -> 4.01 us  [shards(): call(functools.partial(finish_kernel, factor), (plane_shape, plane_shape,...]
    transpose x1 -> x0, local copies, waits for them, and re-layouts: 1.98 us -> none  [shards(): table.transpose(0, 1, 3, 5, 2, 4, 6)]
    all_to_all x1, starting transfers between devices: 5.77 us -> 3.87 us  [total_over_devices(): pieces = lax.all_to_all(half, wide, 0, 0, tiled=True)]
    ppermute x6, waiting for transfers between devices: 10.8 us -> 8.98 us  [passed(): return lax.ppermute(value, ('yhi', 'z', 'lat'), pairs)]
  transfers between devices with their start and end apart: 12 -> 12, of which waited for: 6 -> 5; matrix products, arithmetic and copies ran while one was open for 6% -> 1% of each run, Pallas kernels for 6% -> 7%
where the time goes in v2:
time: 114 us; the launch traced here: 113 us
  Pallas kernels  42.6 us (37%)
  starting transfers between devices  31.6 us (28%)
  waiting for transfers between devices  21.1 us (19%)
  blocking collectives  13 us (11%)
  local copies, waits for them, and re-layouts  2.59 us (2%)
  other arithmetic  1.78 us (2%)
    pallas_call x1, Pallas kernels, shards(): call(main_kernel, (plane_shape, plane_shape, lat_shape, edge_shape, edge_...  28.1 us
    ppermute x6, starting transfers between devices, passed(): return lax.ppermute(value, ('yhi', 'z', 'lat'), pairs)  18.4 us
    all_to_all x1, blocking collectives, total_over_devices(): mine = lax.all_to_all(spread, wide, 0, 0, tiled=True)  13 us
    all_to_all x1, waiting for transfers between devices, total_over_devices(): pieces = lax.all_to_all(half, wide, 0, 0, tiled=True)  9.59 us
    ppermute x6, waiting for transfers between devices, passed(): return lax.ppermute(value, ('yhi', 'z', 'lat'), pairs)  8.98 us
    pallas_call x1, Pallas kernels, shards(): call(expand_kernel, (bias_shape, bias_shape), scratch=[flat_shape, pltpu....  7.67 us
    ppermute x2, starting transfers between devices, swapped(): return lax.ppermute(value, 'core', [(0, 1), (1, 0)])  5.67 us
    pallas_call x1, Pallas kernels, shards(): call(functools.partial(finish_kernel, factor), (plane_shape, plane_shape,...  4.01 us
  transfers between devices with their start and end apart: 12, of which 5 were waited for; matrix products, arithmetic and copies ran while one was open for 1% of the time, Pallas kernels for 7%

profile of v2, /device:TPU:1, one launch (start us, length us, event | category | flops | bytes accessed | tf_op | source)
XLA Modules:
  0.0 113.4 jit_solution(7142012000412859254)
XLA Ops:
  0.6 0.0 copy-start.1
  0.6 2.8 %shard_map.208 = (bf16[8,54,384]{2,1,0:T(8,128)(2,1)}, bf16[8,18,384]{2,1,0:T(8,128)(2,1)}, bf16[8,18,384]{2,1,0:T(8,128)(2,1)}) custom-call(bf16[8,144,192]{2,1,0:T(8,128)(2,1)} %bitcast.20, bf16[8,144,192]{2,1,0:T(8,128)(2,1)} %bitcast.22, bf16[54,144]{1,0:T(8,128)(2,1)} %constant.58.clone.lat_pick, bf16[18,144]{1,0:T(8,128)(2,1)} %constant.59.clone.lon_pick, ...), custom_call_target="tpu_custom_call" | custom-call | flops 1000000000 | bytes 2000000 | tf_op jit(solution)/shard_map/pallas_call | solution.py:409
  3.4 3.3 %collective-permute-start = (bf16[8,54,384]{2,1,0:T(8,128)(2,1)}, bf16[8,54,384]{2,1,0:T(8,128)(2,1)S(1)}, u32[]{:S(2)}, u32[]{:S(2)}) collective-permute-start(bf16[8,54,384]{2,1,0:T(8,128)(2,1)} %get-tuple-element.28), channel_id=1, source_target_pairs={{0,3},{1,0},{2,1},{3,2},{4,7},{5,4},{6,5},{7,6},{8,11},{9,8},{10,9... | collective-permute-start | bytes 995336 | tf_op jit(solution)/shard_map/ppermute | solution.py:352
  6.7 8.2 %collective-permute-start.1 = (bf16[8,18,384]{2,1,0:T(8,128)(2,1)}, bf16[8,18,384]{2,1,0:T(8,128)(2,1)S(1)}, u32[]{:S(2)}, u32[]{:S(2)}) collective-permute-start(bf16[8,18,384]{2,1,0:T(8,128)(2,1)} %get-tuple-element.29), channel_id=1, source_target_pairs={{0,60},{1,61},{2,62},{3,63},{4,0},{5,1},{6,2},{7,3},{8,4},{9,5},{1... | collective-permute-start | bytes 331784 | tf_op jit(solution)/shard_map/ppermute | solution.py:352
  14.9 1.0 collective-permute-start.2
  15.9 0.0 copy-done.1
  15.9 0.2 copy.23
  16.1 0.9 copy.24
  17.0 7.7 %shard_map.209 = (f32[3456,128]{1,0:T(8,128)}, f32[3456,128]{1,0:T(8,128)}) custom-call(s32[1]{0:T(128)} %bitcast.6.last_ref, f32[24,1,3312]{2,1,0:T(1,128)} %bitcast.24, bf16[12,384,256]{2,1,0:T(8,128)(2,1)} %constant.61.clone.sel_ref), custom_call_target="tpu_custom_call" | custom-call | flops 1000000000 | bytes 2000000 | tf_op jit(solution)/shard_map/pallas_call | solution.py:425
  24.7 0.0 collective-permute-done.1.lon_in
  24.7 0.0 copy-start.6
  24.7 0.0 collective-permute-done.2.diag_in
  24.7 0.0 copy-start.7
  24.7 0.0 collective-permute-done.lat_in
  24.7 0.0 copy-start.3
  24.7 0.6 copy-done.6
  25.3 0.1 copy-done.7
  25.4 0.1 copy-done.3
  25.5 28.1 %shard_map.210 = (bf16[8,144,192]{2,1,0:T(8,128)(2,1)}, bf16[8,144,192]{2,1,0:T(8,128)(2,1)}, bf16[8,54,384]{2,1,0:T(8,128)(2,1)}, bf16[8,18,384]{2,1,0:T(8,128)...) custom-call(s32[1]{0:T(128)} %bitcast.core_ref, ...), custom_call_target="tpu_custom_call" | custom-call | flops 10000000000 | bytes 20000000 | tf_op jit(solution)/shard_map/pallas_call | solution.py:437
  53.6 1.5 %collective-permute-start.3 = (bf16[1024,128]{1,0:T(8,128)(2,1)}, bf16[1024,128]{1,0:T(8,128)(2,1)S(1)}, u32[]{:S(2)}, u32[]{:S(2)}) collective-permute-start(bf16[1024,128]{1,0:T(8,128)(2,1)} %get-tuple-element.36), channel_id=1, source_target_pairs={{0,64},{64,0},{1,65},{65,1},{2,66},{66,2},{3,67},{67,3},{4,68},{68... | collective-permute-start | bytes 786440 | tf_op jit(solution)/shard_map/ppermute | solution.py:356
  55.1 1.4 %collective-permute-done.3 = bf16[1024,128]{1,0:T(8,128)(2,1)S(1)} collective-permute-done((bf16[1024,128]{1,0:T(8,128)(2,1)}, bf16[1024,128]{1,0:T(8,128)(2,1)S(1)}, u32[]{:S(2)}, u32[]{:S(2)}) %collective-permute-start.3) | collective-permute-done | bytes 262176 | tf_op jit(solution)/shard_map/ppermute | solution.py:356
  56.5 1.7 %add_convert_fusion = bf16[1024,128]{1,0:T(8,128)(2,1)} fusion(bf16[1024,128]{1,0:T(8,128)(2,1)S(1)} %collective-permute-done.3, bf16[1024,128]{1,0:T(8,128)(2,1)} %get-tuple-element.35), kind=kLoop, calls=%fused_computation.1 | loop fusion | flops 524288 | bytes 786432 | tf_op jit(solution)/shard_map/convert_element_type | solution.py:362
  58.2 3.9 %all-to-all-start = ((bf16[32,32,128]{2,1,0:T(8,128)(2,1)}), bf16[32,32,128]{2,1,0:T(8,128)(2,1)S(1)}, u32[]{:S(2)}, u32[]{:S(2)}) async-start(bf16[32,32,128]{2,1,0:T(8,128)(2,1)} %bitcast.8), calls=%async_computation | async-start | bytes 524288 | tf_op jit(solution)/shard_map/all_to_all | solution.py:363
  62.1 1.0 collective-permute-start.7
  63.1 9.6 %all-to-all-done = bf16[32,32,128]{2,1,0:T(8,128)(2,1)S(1)} async-done(((bf16[32,32,128]{2,1,0:T(8,128)(2,1)}), bf16[32,32,128]{2,1,0:T(8,128)(2,1)S(1)}, u32[]{:S(2)}, u32[]{:S(2)}) %all-to-all-start) | async-done | bytes 262176 | tf_op jit(solution)/shard_map/all_to_all | solution.py:363
  72.7 3.0 %collective-permute-start.6 = (f32[32,128]{1,0:T(8,128)S(1)}, f32[32,128]{1,0:T(8,128)S(1)}, u32[]{:S(2)}, u32[]{:S(2)}) collective-permute-start(f32[32,128]{1,0:T(8,128)S(1)} %convert_reduce_fusion), channel_id=1, source_target_pairs={{0,3},{1,0},{2,1},{3,2},{4,7},{5,4},{6,5},{7,6},{8,11},{9,8},{10,9... | collective-permute-start | bytes 49160 | tf_op jit(solution)/shard_map/ppermute | solution.py:370
  75.7 0.0 collective-permute-start.5
  75.7 0.7 collective-permute-start.4
  76.4 3.0 %collective-permute-start.8 = (bf16[8,18,384]{2,1,0:T(8,128)(2,1)}, bf16[8,18,384]{2,1,0:T(8,128)(2,1)S(1)}, u32[]{:S(2)}, u32[]{:S(2)}) collective-permute-start(bf16[8,18,384]{2,1,0:T(8,128)(2,1)} %get-tuple-element.38), channel_id=1, source_target_pairs={{0,4},{1,5},{2,6},{3,7},{4,8},{5,9},{6,10},{7,11},{8,12},{9,13},{1... | collective-permute-start | bytes 331784 | tf_op jit(solution)/shard_map/ppermute | solution.py:352
  79.4 0.0 collective-permute-done.6
  79.4 1.9 %collective-permute-start.9 = (bf16[8,18,384]{2,1,0:T(8,128)(2,1)}, bf16[8,18,384]{2,1,0:T(8,128)(2,1)S(1)}, u32[]{:S(2)}, u32[]{:S(2)}) collective-permute-start(bf16[8,18,384]{2,1,0:T(8,128)(2,1)} %get-tuple-element.39), channel_id=1, source_target_pairs={{0,5},{1,6},{2,7},{3,4},{4,9},{5,10},{6,11},{7,8},{8,13},{9,14},{1... | collective-permute-start | bytes 331784 | tf_op jit(solution)/shard_map/ppermute | solution.py:352
  81.3 0.0 collective-permute-done.5
  81.3 0.0 collective-permute-done.4
  81.3 2.9 %collective-permute-done.8.lon_in = bf16[8,18,384]{2,1,0:T(8,128)(2,1)S(1)} collective-permute-done((bf16[8,18,384]{2,1,0:T(8,128)(2,1)}, bf16[8,18,384]{2,1,0:T(8,128)(2,1)S(1)}, u32[]{:S(2)}, u32[]{:S(2)}) %collective-permute-start.8) | collective-permute-done | bytes 110624 | tf_op jit(solution)/shard_map/ppermute | solution.py:352
  84.2 0.0 copy-start.5
  84.2 6.1 %collective-permute-done.9.diag_in = bf16[8,18,384]{2,1,0:T(8,128)(2,1)S(1)} collective-permute-done((bf16[8,18,384]{2,1,0:T(8,128)(2,1)}, bf16[8,18,384]{2,1,0:T(8,128)(2,1)S(1)}, u32[]{:S(2)}, u32[]{:S(2)}) %collective-permute-start.9) | collective-permute-done | bytes 110624 | tf_op jit(solution)/shard_map/ppermute | solution.py:352
  90.3 0.0 copy-start.8
  90.3 0.0 collective-permute-done.7.lat_in
  90.3 0.0 copy-start.2
  90.3 13.0 %all_to_all.20 = bf16[32,32,128]{2,1,0:T(8,128)(2,1)S(1)} all-to-all(bf16[32,32,128]{2,1,0:T(8,128)(2,1)S(1)} %broadcast_in_dim.2), channel_id=1, replica_groups=mesh['ylo'=2,'core'=2,'yhi'=2,'z'=8,'lat'=4] {'ylo','yhi','z'}, dimensions={0} | all-to-all | bytes 524288 | tf_op jit(solution)/shard_map/all_to_all | solution.py:374
  103.3 4.2 %collective-permute-start.10 = (bf16[1024,128]{1,0:T(8,128)(2,1)S(1)}, bf16[1024,128]{1,0:T(8,128)(2,1)S(1)}, u32[]{:S(2)}, u32[]{:S(2)}) collective-permute-start(bf16[1024,128]{1,0:T(8,128)(2,1)S(1)} %bitcast.18), channel_id=1, source_target_pairs={{0,64},{64,0},{1,65},{65,1},{2,66},{66,2},{3,67},{67,3},{4,68},{68... | collective-permute-start | bytes 786440 | tf_op jit(solution)/shard_map/ppermute | solution.py:356
  107.5 1.2 %collective-permute-done.10.other_ref = bf16[1024,128]{1,0:T(8,128)(2,1)S(1)} collective-permute-done((bf16[1024,128]{1,0:T(8,128)(2,1)S(1)}, bf16[1024,128]{1,0:T(8,128)(2,1)S(1)}, u32[]{:S(2)}, u32[]{:S(2)}) %collective-permute-start.10) | collective-permute-done | bytes 262176 | tf_op jit(solution)/shard_map/ppermute | solution.py:356
  108.7 0.0 copy-done.5
  108.7 0.0 copy-done.8
  108.7 0.0 copy-done.2
  108.7 0.0 copy-done
  108.7 0.7 copy-done.4
  109.4 4.0 %shard_map.211 = (bf16[8,144,192]{2,1,0:T(8,128)(2,1)}, bf16[8,144,192]{2,1,0:T(8,128)(2,1)}, f32[192,576]{1,0:T(8,128)}, f32[192,192]{1,0:T(8,128)}, f32[1,192]{1,0:T(1,128)}, /*index=5*/f32[24,1,3312]{2,1,0:T(1,128)}) custom-call(s32[1]{0:T(128)} %bitcast.core_ref, bf16[8,144,192]{2,1,0:T(8,128)(2,1)} %get-tuple-element.33.base_ref, ...), custom_call_target="tpu_custom_call" | custom-call | flops 1000000000 | bytes 2000000 | tf_op jit(solution)/shard_map/pallas_call | solution.py:459
  (5 shorter events, 0.1 us)
Async XLA Ops:
  0.6 15.3 %copy-start.1 = (bf16[192,576]{1,0:T(8,128)(2,1)S(1)}, bf16[192,576]{1,0:T(8,128)(2,1)}, u32[]{:S(2)}) copy-start(bf16[192,576]{1,0:T(8,128)(2,1)} %param.20) | copy-start | bytes 663556
  3.4 21.3 %collective-permute-start = (bf16[8,54,384]{2,1,0:T(8,128)(2,1)}, bf16[8,54,384]{2,1,0:T(8,128)(2,1)S(1)}, u32[]{:S(2)}, u32[]{:S(2)}) collective-permute-start(bf16[8,54,384]{2,1,0:T(8,128)(2,1)} %get-tuple-element.28), channel_id=1, source_target_pairs={{0,3},{1,0},{2,1},{3,2},{4,7},{5,4},{6,5},{7,6},{8,11},{9,8},{10,9... | collective-permute-start | bytes 995336 | tf_op jit(solution)/shard_map/ppermute | solution.py:352
  6.7 17.9 %collective-permute-start.1 = (bf16[8,18,384]{2,1,0:T(8,128)(2,1)}, bf16[8,18,384]{2,1,0:T(8,128)(2,1)S(1)}, u32[]{:S(2)}, u32[]{:S(2)}) collective-permute-start(bf16[8,18,384]{2,1,0:T(8,128)(2,1)} %get-tuple-element.29), channel_id=1, source_target_pairs={{0,60},{1,61},{2,62},{3,63},{4,0},{5,1},{6,2},{7,3},{8,4},{9,5},{1... | collective-permute-start | bytes 331784 | tf_op jit(solution)/shard_map/ppermute | solution.py:352
  14.9 9.7 %collective-permute-start.2 = (bf16[8,18,384]{2,1,0:T(8,128)(2,1)}, bf16[8,18,384]{2,1,0:T(8,128)(2,1)S(1)}, u32[]{:S(2)}, u32[]{:S(2)}) collective-permute-start(bf16[8,18,384]{2,1,0:T(8,128)(2,1)} %get-tuple-element.30), channel_id=1, source_target_pairs={{0,63},{1,60},{2,61},{3,62},{4,3},{5,0},{6,1},{7,2},{8,7},{9,4},{1... | collective-permute-start | bytes 331784 | tf_op jit(solution)/shard_map/ppermute | solution.py:352
  24.7 0.7 copy-start.6
  24.7 0.7 copy-start.7
  24.7 0.8 copy-start.3
  53.6 2.9 %collective-permute-start.3 = (bf16[1024,128]{1,0:T(8,128)(2,1)}, bf16[1024,128]{1,0:T(8,128)(2,1)S(1)}, u32[]{:S(2)}, u32[]{:S(2)}) collective-permute-start(bf16[1024,128]{1,0:T(8,128)(2,1)} %get-tuple-element.36), channel_id=1, source_target_pairs={{0,64},{64,0},{1,65},{65,1},{2,66},{66,2},{3,67},{67,3},{4,68},{68... | collective-permute-start | bytes 786440 | tf_op jit(solution)/shard_map/ppermute | solution.py:356
  58.2 14.5 %all-to-all-start = ((bf16[32,32,128]{2,1,0:T(8,128)(2,1)}), bf16[32,32,128]{2,1,0:T(8,128)(2,1)S(1)}, u32[]{:S(2)}, u32[]{:S(2)}) async-start(bf16[32,32,128]{2,1,0:T(8,128)(2,1)} %bitcast.8), calls=%async_computation | async-start | bytes 524288 | tf_op jit(solution)/shard_map/all_to_all | solution.py:363
  62.1 28.2 %collective-permute-start.7 = (bf16[8,54,384]{2,1,0:T(8,128)(2,1)}, bf16[8,54,384]{2,1,0:T(8,128)(2,1)S(1)}, u32[]{:S(2)}, u32[]{:S(2)}) collective-permute-start(bf16[8,54,384]{2,1,0:T(8,128)(2,1)} %get-tuple-element.37), channel_id=1, source_target_pairs={{0,1},{1,2},{2,3},{3,0},{4,5},{5,6},{6,7},{7,4},{8,9},{9,10},{10,1... | collective-permute-start | bytes 995336 | tf_op jit(solution)/shard_map/ppermute | solution.py:352
  72.7 6.7 %collective-permute-start.6 = (f32[32,128]{1,0:T(8,128)S(1)}, f32[32,128]{1,0:T(8,128)S(1)}, u32[]{:S(2)}, u32[]{:S(2)}) collective-permute-start(f32[32,128]{1,0:T(8,128)S(1)} %convert_reduce_fusion), channel_id=1, source_target_pairs={{0,3},{1,0},{2,1},{3,2},{4,7},{5,4},{6,5},{7,6},{8,11},{9,8},{10,9... | collective-permute-start | bytes 49160 | tf_op jit(solution)/shard_map/ppermute | solution.py:370
  75.7 5.6 %collective-permute-start.5 = (f32[32,128]{1,0:T(8,128)S(1)}, f32[32,128]{1,0:T(8,128)S(1)}, u32[]{:S(2)}, u32[]{:S(2)}) collective-permute-start(f32[32,128]{1,0:T(8,128)S(1)} %convert_reduce_fusion), channel_id=1, source_target_pairs={{0,2},{1,3},{2,0},{3,1},{4,6},{5,7},{6,4},{7,5},{8,10},{9,11},{10,... | collective-permute-start | bytes 49160 | tf_op jit(solution)/shard_map/ppermute | solution.py:370
  75.7 5.6 %collective-permute-start.4 = (f32[32,128]{1,0:T(8,128)S(1)}, f32[32,128]{1,0:T(8,128)S(1)}, u32[]{:S(2)}, u32[]{:S(2)}) collective-permute-start(f32[32,128]{1,0:T(8,128)S(1)} %convert_reduce_fusion), channel_id=1, source_target_pairs={{0,1},{1,2},{2,3},{3,0},{4,5},{5,6},{6,7},{7,4},{8,9},{9,10},{10,1... | collective-permute-start | bytes 49160 | tf_op jit(solution)/shard_map/ppermute | solution.py:370
  76.4 7.8 %collective-permute-start.8 = (bf16[8,18,384]{2,1,0:T(8,128)(2,1)}, bf16[8,18,384]{2,1,0:T(8,128)(2,1)S(1)}, u32[]{:S(2)}, u32[]{:S(2)}) collective-permute-start(bf16[8,18,384]{2,1,0:T(8,128)(2,1)} %get-tuple-element.38), channel_id=1, source_target_pairs={{0,4},{1,5},{2,6},{3,7},{4,8},{5,9},{6,10},{7,11},{8,12},{9,13},{1... | collective-permute-start | bytes 331784 | tf_op jit(solution)/shard_map/ppermute | solution.py:352
  79.4 10.9 %collective-permute-start.9 = (bf16[8,18,384]{2,1,0:T(8,128)(2,1)}, bf16[8,18,384]{2,1,0:T(8,128)(2,1)S(1)}, u32[]{:S(2)}, u32[]{:S(2)}) collective-permute-start(bf16[8,18,384]{2,1,0:T(8,128)(2,1)} %get-tuple-element.39), channel_id=1, source_target_pairs={{0,5},{1,6},{2,7},{3,4},{4,9},{5,10},{6,11},{7,8},{8,13},{9,14},{1... | collective-permute-start | bytes 331784 | tf_op jit(solution)/shard_map/ppermute | solution.py:352
  84.2 24.5 %copy-start.5 = (bf16[8,18,384]{2,1,0:T(8,128)(2,1)}, bf16[8,18,384]{2,1,0:T(8,128)(2,1)S(1)}, u32[]{:S(2)}) copy-start(bf16[8,18,384]{2,1,0:T(8,128)(2,1)S(1)} %collective-permute-done.8.lon_in) | copy-start | bytes 331780
  90.3 18.4 %copy-start.8 = (bf16[8,18,384]{2,1,0:T(8,128)(2,1)}, bf16[8,18,384]{2,1,0:T(8,128)(2,1)S(1)}, u32[]{:S(2)}) copy-start(bf16[8,18,384]{2,1,0:T(8,128)(2,1)S(1)} %collective-permute-done.9.diag_in) | copy-start | bytes 331780
  90.3 18.4 %copy-start.2 = (bf16[8,54,384]{2,1,0:T(8,128)(2,1)}, bf16[8,54,384]{2,1,0:T(8,128)(2,1)S(1)}, u32[]{:S(2)}) copy-start(bf16[8,54,384]{2,1,0:T(8,128)(2,1)S(1)} %collective-permute-done.7.lat_in) | copy-start | bytes 995332
  103.3 5.3 %copy-start = (bf16[32,32,128]{2,1,0:T(8,128)(2,1)}, bf16[32,32,128]{2,1,0:T(8,128)(2,1)S(1)}, u32[]{:S(2)}) copy-start(bf16[32,32,128]{2,1,0:T(8,128)(2,1)S(1)} %all_to_all.20) | copy-start | bytes 786436
  103.3 5.3 %collective-permute-start.10 = (bf16[1024,128]{1,0:T(8,128)(2,1)S(1)}, bf16[1024,128]{1,0:T(8,128)(2,1)S(1)}, u32[]{:S(2)}, u32[]{:S(2)}) collective-permute-start(bf16[1024,128]{1,0:T(8,128)(2,1)S(1)} %bitcast.18), channel_id=1, source_target_pairs={{0,64},{64,0},{1,65},{65,1},{2,66},{66,2},{3,67},{67,3},{4,68},{68... | collective-permute-start | bytes 786440 | tf_op jit(solution)/shard_map/ppermute | solution.py:356
  108.7 0.7 copy-start.4

commit v3 on v2

v3 whole, which is shorter than its diff:
```python
import functools

import numpy as np
import jax
import jax.numpy as jnp
from jax import lax
from jax.experimental import pallas as pl
from jax.experimental.pallas import tpu as pltpu
from jax.sharding import PartitionSpec as P

HEADS = 6
WLEV = 2
WLAT = 6
WLON = 12
HD = 32
CH = 192
TOK = 144
LANES = 128
SHIFT_LAT = 3
SHIFT_LON = 6
SPAN = 2 * WLON - 1
GROUPS = WLEV * WLAT
MASKED = -1e30
EPSILON = 1e-05
BF = jnp.bfloat16
F32 = jnp.float32
PAY = 2048
WTILES = 6
BIAS_ROWS = 288
BROW = WTILES * CH
GROW = BROW + 3 * BIAS_ROWS
PIECE = 32
HTILES = 7
HLANES = HTILES * LANES
CHUNK = 3 * LANES
VMEM_LIMIT = 56 * 1024 * 1024


def place(rows, cols):
    return np.zeros((rows, cols), np.float32)


def gather_matrices(cols_here):
    windows = cols_here // WLON
    own_cols = cols_here - SHIFT_LON
    own = place(windows * WLAT * WLON, WLAT * cols_here)
    lat = place(windows * WLAT * WLON, SHIFT_LAT * own_cols)
    corner = place(windows * WLAT * WLON, WLAT * SHIFT_LON)
    for n in range(windows):
        for a in range(WLAT):
            for x in range(WLON):
                row = (n * WLAT + a) * WLON + x
                col = n * WLON + x
                if col < own_cols:
                    if a < SHIFT_LAT:
                        own[row, (a + SHIFT_LAT) * cols_here + col + SHIFT_LON] = 1
                    else:
                        lat[row, (a - SHIFT_LAT) * own_cols + col] = 1
                else:
                    corner[row, a * SHIFT_LON + col - own_cols] = 1
    return own, lat, corner


def scatter_matrices(cols_here):
    own_cols = cols_here - SHIFT_LON
    lat = place(WLAT * cols_here, SHIFT_LAT * own_cols)
    corner = place(WLAT * cols_here, WLAT * SHIFT_LON)
    for a in range(WLAT):
        for c in range(cols_here):
            row = a * cols_here + c
            if c >= SHIFT_LON:
                if a < SHIFT_LAT:
                    lat[row, a * own_cols + c - SHIFT_LON] = 1
            elif a >= SHIFT_LAT:
                corner[row, (a - SHIFT_LAT) * SHIFT_LON + c] = 1
            else:
                corner[row, (a + SHIFT_LAT) * SHIFT_LON + c] = 1
    return lat, corner


def lon_selectors():
    out = np.zeros((WLON, 3 * LANES, 2 * LANES), np.float32)
    for xj in range(WLON):
        for g in range(GROUPS):
            for xi in range(WLON):
                out[xj, g * SPAN + xi - xj + WLON - 1, g * WLON + xi] = 1
    return out


def dot(a, b, ca=1, cb=0):
    return lax.dot_general(a, b, (((ca,), (cb,)), ((), ())), preferred_element_type=F32)


def split(value):
    high = value.astype(BF)
    return high, (value - high.astype(F32)).astype(BF)


def prep_kernel(wx_ref, gx_ref, lat_pick, lon_pick, diag_pick, lat_out, lon_out, diag_out):
    def step(level, carry):
        for pick, strip in ((lat_pick, lat_out), (lon_pick, lon_out), (diag_pick, diag_out)):
            strip[level] = jnp.concatenate(
                [dot(pick[...], ref[level]) for ref in (wx_ref, gx_ref)], axis=1
            ).astype(BF)
        return carry

    lax.fori_loop(0, wx_ref.shape[0], step, 0, unroll=True)


def expand_kernel(last_ref, table_ref, sel_ref, bias_ref, flat_s, block_s, table_s):
    pairs, _, entries = table_ref.shape
    levs = pairs // HEADS
    for h in range(HEADS):
        for lev in range(levs):
            r = h * levs + lev
            flat_s[r : r + 1, :entries] = table_ref[lev * HEADS + h]
    for m in range(GROUPS):
        z_j, a_j = divmod(m, WLAT)
        for g in range(GROUPS):
            z_i, a_i = divmod(g, WLAT)
            at = SPAN * (((z_i * WLEV + z_j) * WLAT + a_i) * WLAT + a_j)
            block_s[m, :, g * SPAN : (g + 1) * SPAN] = flat_s[:, at : at + SPAN]
        for j in range(3):
            table_s[j, pl.ds(m, pairs, stride=GROUPS), :] = block_s[m, :, j * LANES : (j + 1) * LANES]
    table = jnp.concatenate([table_s[j] for j in range(3)], axis=1)[:, : GROUPS * SPAN]
    high, low = split(table)
    rows = levs * GROUPS
    row_id = lax.broadcasted_iota(jnp.int32, (BIAS_ROWS, TOK), 0)
    col_id = lax.broadcasted_iota(jnp.int32, (BIAS_ROWS, TOK), 1)
    m_j = row_id % GROUPS
    lev = row_id // GROUPS % levs
    a_i = col_id // WLON % WLAT
    z_i = col_id // (WLON * WLAT)
    cross_lev = jnp.logical_and(lev == levs - 1, m_j // WLAT != z_i)
    cross_lat = jnp.logical_and(last_ref[0] == 1, (m_j % WLAT >= SHIFT_LAT) != (a_i >= SHIFT_LAT))
    hide = jnp.where(jnp.logical_or(cross_lev, cross_lat), MASKED, 0.0)
    pad = jnp.zeros((rows, HLANES - HEADS * TOK), F32)
    for xj in range(WLON):
        sel = sel_ref[xj, : GROUPS * SPAN, :TOK]
        value = dot(high, sel) + dot(low, sel) + hide
        wide = jnp.concatenate([value[h * rows : (h + 1) * rows] for h in range(HEADS)] + [pad], axis=1)
        for t in range(HTILES):
            bias_ref[t, pl.ds(xj, rows, stride=WLON), :] = wide[:, t * LANES : (t + 1) * LANES]


def main_kernel(
    core_ref, wx_ref, gx_ref, lat_in, lon_in, diag_in, gain_ref, wqkv_ref, proj_ref,
    pown_ref, plat_ref, plon_ref, pdiag_ref, bias_hbm, sel_hbm,
    att_ref, gi_ref, keep_ref, send_ref,
    x_s, g_s, normed_s, inv_s, q_s, k_s, v_s, da_s, dq_s, dk_s, dv_s, hid_t, dsum_s, pay_s, bias_s, sel_s, sems,
):
    bias_copy = pltpu.make_async_copy(bias_hbm, bias_s, sems.at[0])
    sel_copy = pltpu.make_async_copy(sel_hbm, sel_s, sems.at[1])
    bias_copy.start()
    sel_copy.start()
    levels = wx_ref.shape[0]
    half = TOK // 2
    windows = x_s.shape[0] // TOK
    for level in range(levels):
        back = (level + levels - 1) % levels
        k, z = back // WLEV, back % WLEV
        place_own = pown_ref[...]
        strips = ((plat_ref, lat_in), (plon_ref, lon_in), (pdiag_ref, diag_in))
        xw = dot(place_own, wx_ref[level])
        gw = dot(place_own, gx_ref[level])
        for where_ref, strip in strips:
            both = strip[level]
            xw = xw + dot(where_ref[...], both[:, :CH])
            gw = gw + dot(where_ref[...], both[:, CH:])
        for n in range(2):
            at = (2 * k + n) * TOK + z * half
            x_s[at : at + half, :] = xw[n * half : (n + 1) * half]
            g_s[at : at + half, :] = gw[n * half : (n + 1) * half]

    gain = gain_ref[...]
    inv_root = HD ** (-0.5)

    def eye(n):
        return (lax.broadcasted_iota(jnp.int32, (n, n), 0) == lax.broadcasted_iota(jnp.int32, (n, n), 1)).astype(F32).astype(BF)

    eye_c = eye(CH)
    eye_t = eye(TOK)
    chunks = [slice(at, at + CHUNK) for at in range(0, x_s.shape[0], CHUNK)]
    for rows in chunks:
        x = x_s[rows]
        centred = x - jnp.mean(x, axis=-1, keepdims=True)
        inv_std = lax.rsqrt(jnp.mean(centred * centred, axis=-1, keepdims=True) + EPSILON)
        normed = centred * inv_std
        normed_s[rows] = normed
        inv_s[rows] = jnp.broadcast_to(inv_std, (CHUNK, LANES))
        hidden = (normed * gain).astype(BF)
        q_s[rows] = (dot(hidden, wqkv_ref[0]) * inv_root).astype(BF)
        k_s[rows] = dot(hidden, wqkv_ref[1]).astype(BF)
        v_s[rows] = dot(hidden, wqkv_ref[2]).astype(BF)
        da_s[rows] = dot(g_s[rows].astype(BF), proj_ref[...], 1, 1).astype(BF)
        hid_t[:, rows] = dot(eye_c, hidden, 1, 1).astype(BF)

    channel = lax.broadcasted_iota(jnp.int32, (TOK, CH), 1)
    head_mask = [jnp.logical_and(channel >= h * HD, channel < (h + 1) * HD) for h in range(HEADS)]
    zero = jnp.zeros((TOK, CH), BF)
    tail = jnp.zeros((HLANES - HEADS * TOK, CH), BF)

    def per_head(value):
        return jnp.concatenate([jnp.where(mask, value, zero) for mask in head_mask] + [tail], axis=0)

    bias_copy.wait()
    gproj = jnp.zeros((CH, CH), F32)
    for w in range(windows):
        rows = slice(w * TOK, (w + 1) * TOK)
        first = w % 2 == 0
        lev_rows = slice(w // 2 * TOK, (w // 2 + 1) * TOK)
        key, v = k_s[rows], v_s[rows]
        q_heads = per_head(q_s[rows])
        da_heads = per_head(da_s[rows])
        key_t = dot(eye_c, key, 1, 1).astype(BF)
        v_t = dot(eye_c, v, 1, 1).astype(BF)
        scores = dot(key, q_heads, 1, 1)
        scores = scores + jnp.concatenate([bias_s[t, lev_rows, :] for t in range(HTILES)], axis=1)
        dp = dot(v, da_heads, 1, 1)
        e = jnp.exp(scores - jnp.max(scores, axis=0, keepdims=True))
        probs = (e * (1.0 / jnp.sum(e, axis=0, keepdims=True))).astype(BF)
        dv_s[rows] = dot(probs, da_heads).astype(BF)
        pf = probs.astype(F32)
        t_prod = pf * dp
        ds = t_prod - pf * jnp.sum(t_prod, axis=0, keepdims=True)
        dsb = ds.astype(BF)
        for t in range(HTILES):
            part = ds[:, t * LANES : (t + 1) * LANES]
            dsum_s[t, lev_rows, :] = part if first else dsum_s[t, lev_rows, :] + part
        dk_s[rows] = dot(dsb, q_heads).astype(BF)
        att_t = jnp.concatenate(
            [dot(v_t[h * HD : (h + 1) * HD], probs[:, h * TOK : (h + 1) * TOK]) for h in range(HEADS)], axis=0
        ).astype(BF)
        dq_t = jnp.concatenate(
            [dot(key_t[h * HD : (h + 1) * HD], dsb[:, h * TOK : (h + 1) * TOK]) for h in range(HEADS)], axis=0
        )
        dq_t = (dq_t * inv_root).astype(BF)
        att_ref[rows] = dot(eye_t, att_t, 1, 1).astype(BF)
        dq_s[rows] = dot(eye_t, dq_t, 1, 1).astype(BF)
        gproj = gproj + dot(att_t, g_s[rows].astype(BF))

    g_gain = jnp.zeros((1, CH), F32)
    for rows in chunks:
        gh = (
            dot(dq_s[rows], wqkv_ref[0], 1, 1)
            + dot(dk_s[rows], wqkv_ref[1], 1, 1)
            + dot(dv_s[rows], wqkv_ref[2], 1, 1)
        )
        normed = normed_s[rows]
        g_gain = g_gain + jnp.sum(gh * normed, axis=0, keepdims=True)
        gn = gh * gain
        gi = inv_s[rows][:, :1] * (
            gn
            - jnp.mean(gn, axis=-1, keepdims=True)
            - normed * jnp.mean(gn * normed, axis=-1, keepdims=True)
        )
        gi_ref[rows] = gi.astype(BF)

    g_wide = [dot(hid_t[...], part[...]) for part in (dq_s, dk_s, dv_s)]
    weights = jnp.concatenate(g_wide + [gproj], axis=1)
    for j in range(WTILES):
        pay_s[j * CH : (j + 1) * CH, :] = weights[:, j * LANES : (j + 1) * LANES]
    pay_s[GROW:, :] = jnp.zeros((PAY - GROW, LANES), F32)
    pay_s[GROW : GROW + 1, :] = g_gain[:, :LANES]
    pay_s[GROW + 1 : GROW + 2, : CH - LANES] = g_gain[:, LANES:]

    sel_copy.wait()
    lev_groups = dsum_s.shape[1] // WLON
    g_bias = jnp.zeros((BIAS_ROWS, 3 * LANES), F32)
    for xj in range(WLON):
        wide = jnp.concatenate(
            [dsum_s[t, pl.ds(xj, lev_groups, stride=WLON), :] for t in range(HTILES)], axis=1
        ).astype(BF)
        stacked = jnp.concatenate([wide[:, h * TOK : (h + 1) * TOK] for h in range(HEADS)], axis=0)
        g_bias = g_bias + dot(stacked, sel_s[xj, :, :TOK], 1, 1)
    for j in range(3):
        pay_s[BROW + j * BIAS_ROWS : BROW + (j + 1) * BIAS_ROWS, :] = g_bias[:, j * LANES : (j + 1) * LANES]
    core = core_ref[0]
    half_rows = PAY // 2
    keep_ref[...] = pay_s[pl.ds(pl.multiple_of(core * half_rows, half_rows), half_rows), :].astype(BF)
    send_ref[...] = pay_s[pl.ds(pl.multiple_of((1 - core) * half_rows, half_rows), half_rows), :].astype(BF)


def return_kernel(
    wx_ref, gx_ref, att_ref, gi_ref, proj_ref, pown_ref, plat_ref, plon_ref, pdiag_ref,
    base_ref, gbase_ref, lat_out, lon_out, diag_out, br_s, gi_s,
):
    br_s[...] = dot(att_ref[...], proj_ref[...])
    gi_s[...] = gi_ref[...].astype(F32)
    levels = wx_ref.shape[0]
    half = TOK // 2
    for level in range(levels):
        back = (level + levels - 1) % levels
        k, z = back // WLEV, back % WLEV
        moved = []
        for src, own_in, own_out in ((br_s, wx_ref, base_ref), (gi_s, gx_ref, gbase_ref)):
            starts = [(2 * k + n) * TOK + z * half for n in range(2)]
            rows = jnp.concatenate([src[at : at + half, :] for at in starts], axis=0).astype(BF)
            own_out[level] = (own_in[level].astype(F32) + dot(pown_ref[...], rows, 0, 0)).astype(BF)
            moved.append(rows)
        for where_ref, strip in ((plat_ref, lat_out), (plon_ref, lon_out), (pdiag_ref, diag_out)):
            strip[level] = jnp.concatenate(
                [dot(where_ref[...], rows, 0, 0) for rows in moved], axis=1
            ).astype(BF)


def add_kernel(base_ref, gbase_ref, lat_in, lon_in, diag_in, slat_ref, slon_ref, sdiag_ref, out_ref, gout_ref):
    for level in range(base_ref.shape[0]):
        up = base_ref[level].astype(F32)
        gup = gbase_ref[level].astype(F32)
        for where_ref, strip in ((slat_ref, lat_in), (slon_ref, lon_in), (sdiag_ref, diag_in)):
            both = strip[level]
            up = up + dot(where_ref[...], both[:, :CH])
            gup = gup + dot(where_ref[...], both[:, CH:])
        out_ref[level] = up.astype(BF)
        gout_ref[level] = gup.astype(BF)


def finish_kernel(
    factor, core_ref, mine_ref, other_ref, gqkv_ref, gproj_ref, ggain_ref, gbias_ref, full_s, table_s,
):
    core = core_ref[0]
    half_rows = PAY // 2
    full_s[pl.ds(pl.multiple_of(core * half_rows, half_rows), half_rows), :] = mine_ref[...].astype(F32) * factor
    full_s[pl.ds(pl.multiple_of((1 - core) * half_rows, half_rows), half_rows), :] = other_ref[...].astype(F32) * factor
    tiles = [full_s[j * CH : (j + 1) * CH, :] for j in range(WTILES)]
    for j in range(4):
        gqkv_ref[:, j * LANES : (j + 1) * LANES] = tiles[j]
    cut = 3 * CH - 4 * LANES
    gqkv_ref[:, 4 * LANES :] = tiles[4][:, :cut]
    gproj_ref[...] = jnp.concatenate([tiles[4][:, cut:], tiles[5]], axis=1)
    ggain_ref[...] = jnp.concatenate(
        [full_s[GROW : GROW + 1, :], full_s[GROW + 1 : GROW + 2, : CH - LANES]], axis=1
    )
    pairs = BIAS_ROWS // GROUPS
    levs = pairs // HEADS
    for m in range(GROUPS):
        z_j, a_j = divmod(m, WLAT)
        block = jnp.concatenate(
            [full_s[pl.ds(BROW + j * BIAS_ROWS + m, pairs, stride=GROUPS), :] for j in range(3)], axis=1
        )
        for g in range(GROUPS):
            z_i, a_i = divmod(g, WLAT)
            to = SPAN * (((z_i * WLEV + z_j) * WLAT + a_i) * WLAT + a_j)
            table_s[:, to : to + SPAN] = block[:, g * SPAN : (g + 1) * SPAN]
    for h in range(HEADS):
        for lev in range(levs):
            r = h * levs + lev
            gbias_ref[lev * HEADS + h] = table_s[r : r + 1, : gbias_ref.shape[2]]


def passed(value, lat_step, lon_step):
    lats, highs, zs = lax.axis_size("lat"), lax.axis_size("yhi"), lax.axis_size("z")
    lons = highs * zs
    pairs = [
        (b * lats + a, (b + lon_step) % lons * lats + (a + lat_step) % lats)
        for b in range(lons)
        for a in range(lats)
    ]
    return lax.ppermute(value, ("yhi", "z", "lat"), pairs)


def swapped(value):
    return lax.ppermute(value, "core", [(0, 1), (1, 0)])


def total_over_devices(keep, send, between, last):
    wide = ("ylo", "yhi", "z")
    peers = lax.axis_size("ylo") * lax.axis_size("yhi") * lax.axis_size("z")
    half = (keep.astype(F32) + swapped(send).astype(F32)).astype(BF)
    inputs, fn = between
    half, inputs = lax.optimization_barrier((half, inputs))
    pieces = lax.all_to_all(half, wide, 0, 0, tiled=True)
    keeps, strips = fn(inputs)
    pieces, _ = lax.optimization_barrier((pieces, strips))
    piece = jnp.sum(pieces.reshape(peers, PIECE, LANES).astype(F32), axis=0)
    lats = lax.axis_size("lat")
    place_here = lax.axis_index("core") * peers + lax.axis_index(wide)
    shared = jnp.logical_or(place_here < BROW // PIECE, place_here >= GROW // PIECE)
    others = jnp.zeros_like(piece)
    for step in range(1, lats):
        others = others + lax.ppermute(piece, "lat", [(a, (a + step) % lats) for a in range(lats)])
    piece = jnp.where(shared, piece + others, piece).astype(BF)
    spread = jnp.broadcast_to(piece[None], (peers, PIECE, LANES)).reshape(half.shape)
    spread, strips = lax.optimization_barrier((spread, strips))
    backs = [passed(strip, *step) for strip, step in zip(strips, ((1, 0), (0, 1), (1, 1)))]
    mine = lax.all_to_all(spread, wide, 0, 0, tiled=True)
    mine, backs = lax.optimization_barrier((mine, backs))
    return mine, swapped(mine), last(*keeps, *backs)


def call(kernel, out_shape, scratch=(), smem=0, count=0, flops=0, far=0):
    specs = [pl.BlockSpec(memory_space=pltpu.SMEM)] * smem
    specs += [pl.BlockSpec(memory_space=pltpu.VMEM)] * (count - smem - far)
    specs += [pl.BlockSpec(memory_space=pl.ANY)] * far
    return pl.pallas_call(
        kernel,
        out_shape=out_shape,
        in_specs=specs,
        out_specs=jax.tree.map(lambda _: pl.BlockSpec(memory_space=pltpu.VMEM), out_shape),
        scratch_shapes=list(scratch),
        compiler_params=pltpu.CompilerParams(vmem_limit_bytes=VMEM_LIMIT),
        cost_estimate=pl.CostEstimate(flops=flops, bytes_accessed=flops // 500, transcendentals=0),
    )


def sds(shape, dtype):
    return jax.ShapeDtypeStruct(shape, dtype)


def shards(weather, cotangent, norm_gain, qkv_weight, proj_weight, bias_table):
    samples, levels, rows_here, cols_here, channels = weather.shape
    lat_index = lax.axis_index("lat")
    lat_count = lax.axis_size("lat")
    plane = rows_here * cols_here
    own_cols = cols_here - SHIFT_LON
    wx = weather.reshape(levels, plane, CH)
    gx = cotangent.reshape(levels, plane, CH)
    edge = SHIFT_LAT * SHIFT_LON
    lat_shape = sds((levels, SHIFT_LAT * own_cols, 2 * CH), BF)
    edge_shape = sds((levels, edge, 2 * CH), BF)
    slat, scor = scatter_matrices(cols_here)
    scatter = (slat, scor[:, :edge], scor[:, edge:])
    strips = call(prep_kernel, (lat_shape, edge_shape, edge_shape), count=5, flops=10**9)(
        wx, gx, *[jnp.asarray(m.T, BF) for m in scatter]
    )
    lat_in = passed(strips[0], -1, 0)
    lon_in = passed(strips[1], 0, -1)
    diag_in = passed(strips[2], -1, -1)

    lev_windows = bias_table.shape[0]
    pairs = lev_windows * HEADS
    entries = bias_table.shape[-1]
    table = bias_table.transpose(0, 2, 1, 3).reshape(pairs, 1, entries)
    last = (lat_index == lat_count - 1).astype(jnp.int32).reshape(1)
    sel = jnp.asarray(lon_selectors(), BF)
    bias_rows = lev_windows * TOK
    flat_shape = pltpu.VMEM((pairs, -(-entries // LANES) * LANES), F32)
    bias_shape = (HTILES, bias_rows, LANES)
    bias = call(
        expand_kernel,
        sds(bias_shape, F32),
        scratch=[flat_shape, pltpu.VMEM((GROUPS, pairs, 3 * LANES), F32), pltpu.VMEM((3, BIAS_ROWS, LANES), F32)],
        smem=1, count=3, flops=10**9,
    )(last, table, sel)

    own_m, lat_m, corner_m = gather_matrices(cols_here)
    mats = [jnp.asarray(m, BF) for m in (own_m, lat_m, corner_m[:, :edge], corner_m[:, edge:])]
    wqkv = qkv_weight.reshape(CH, 3, CH).transpose(1, 0, 2)
    tokens = levels * plane
    plane_shape = sds((levels, plane, CH), BF)
    token_shape = sds((tokens, CH), BF)
    core = lax.axis_index("core").astype(jnp.int32).reshape(1)
    half_shape = sds((PAY // 2, LANES), BF)
    wide_f = pltpu.VMEM((tokens, CH), F32)
    wide_b = pltpu.VMEM((tokens, CH), BF)
    att, gi, keep, send = call(
        main_kernel,
        (token_shape, token_shape, half_shape, half_shape),
        scratch=[wide_f, wide_f, wide_f, pltpu.VMEM((tokens, LANES), F32)]
        + [wide_b] * 7
        + [
            pltpu.VMEM((CH, tokens), BF),
            pltpu.VMEM(bias_shape, F32),
            pltpu.VMEM((PAY, LANES), F32),
            pltpu.VMEM(bias_shape, F32),
            pltpu.VMEM(sel.shape, BF),
            pltpu.SemaphoreType.DMA((2,)),
        ],
        smem=1,
        count=15,
        far=2,
        flops=10**10,
    )(core, wx, gx, lat_in, lon_in, diag_in, norm_gain.reshape(1, CH), wqkv, proj_weight, *mats, bias, sel)

    def give_back(inputs):
        base, gbase, *strips = call(
            return_kernel,
            (plane_shape, plane_shape, lat_shape, edge_shape, edge_shape),
            scratch=[wide_f, wide_f],
            count=9,
            flops=2 * 10**9,
        )(wx, gx, *inputs, proj_weight, *mats)
        return (base, gbase), strips

    def add_up(*parts):
        return call(add_kernel, (plane_shape, plane_shape), count=8, flops=2 * 10**9)(
            *parts, *[jnp.asarray(m, BF) for m in scatter]
        )

    mine, other, (out, gout) = total_over_devices(keep, send, ((att, gi), give_back), add_up)
    factor = (samples * levels * rows_here * cols_here * lax.axis_size(("ylo", "core", "yhi", "z", "lat"))) ** (-0.5)
    gqkv, gproj, ggain, gbias = call(
        functools.partial(finish_kernel, factor),
        (sds(qkv_weight.shape, F32), sds(proj_weight.shape, F32), sds((1, CH), F32), sds((pairs, 1, entries), F32)),
        scratch=[pltpu.VMEM((PAY, LANES), F32), flat_shape],
        smem=1,
        count=3,
        flops=10**9,
    )(core, mine, other)
    return (
        out.reshape(weather.shape),
        gout.reshape(weather.shape),
        gqkv,
        gproj,
        ggain.reshape(CH),
        gbias.reshape(lev_windows, HEADS, 1, entries).transpose(0, 2, 1, 3),
    )


def solution(mesh):
    fine = jax.sharding.Mesh(mesh.devices.reshape(2, 2, 2, 8, 4), ("ylo", "core", "yhi", "z", "lat"))
    dp, lon = ("ylo", "core"), ("yhi", "z")
    grid = P(dp, None, "lat", lon, None)
    table = P(None, "lat", None, None)
    return jax.shard_map(
        shards,
        mesh=fine,
        in_specs=(grid, grid, P(), P(), P(), table),
        out_specs=(grid, grid, P(), P(), P(), table),
        check_vma=False,
    )
```

time: 114 us -> 98.7 us (0.87)
  blocking collectives: 13 us -> 0 us
  Pallas kernels: 42.6 us -> 33.4 us
  starting transfers between devices: 31.6 us -> 34.9 us
  waiting for transfers between devices: 21.1 us -> 24.1 us
    all_to_all x1 -> x0, blocking collectives: 13 us -> none  [total_over_devices(): mine = lax.all_to_all(spread, wide, 0, 0, tiled=True)]
    pallas_call x3 -> x5, Pallas kernels: 39.8 us -> 30.6 us  [the longest x1 14.3 us: shards(): call(main_kernel, (token_shape, token_shape, half_shape, half_shape), scr...]
    all_to_all x0 -> x1, starting transfers between devices: none -> 5.52 us  [total_over_devices(): mine = lax.all_to_all(spread, wide, 0, 0, tiled=True)]
    ppermute x6, waiting for transfers between devices: 8.98 us -> 13.1 us  [passed(): return lax.ppermute(value, ('yhi', 'z', 'lat'), pairs)]
    ppermute x3, waiting for transfers between devices: 0.01 us -> 3.42 us  [total_over_devices(): lax.ppermute(piece, 'lat', [(a, (a + step) % lats) for a in range(lats)])]
    all_to_all x1, waiting for transfers between devices: 9.59 us -> 6.21 us  [total_over_devices(): pieces = lax.all_to_all(half, wide, 0, 0, tiled=True)]
    ppermute x6, starting transfers between devices: 18.4 us -> 16.1 us  [passed(): return lax.ppermute(value, ('yhi', 'z', 'lat'), pairs)]
    ppermute x2, starting transfers between devices: 5.67 us -> 4.05 us  [swapped(): return lax.ppermute(value, 'core', [(0, 1), (1, 0)])]
  transfers between devices with their start and end apart: 12 -> 13, of which waited for: 5 -> 6; matrix products, arithmetic and copies ran while one was open for 1% -> 1% of each run, Pallas kernels for 7% -> 14%
where the time goes in v3:
time: 98.7 us; the launch traced here: 98.3 us
  starting transfers between devices  34.9 us (35%)
  Pallas kernels  33.4 us (34%)
  waiting for transfers between devices  24.1 us (24%)
  local copies, waits for them, and re-layouts  3.29 us (3%)
  other arithmetic  1.78 us (2%)
    ppermute x6, starting transfers between devices, passed(): return lax.ppermute(value, ('yhi', 'z', 'lat'), pairs)  16.1 us
    pallas_call x1, Pallas kernels, shards(): call(main_kernel, (token_shape, token_shape, half_shape, half_shape), scr...  14.3 us
    ppermute x6, waiting for transfers between devices, passed(): return lax.ppermute(value, ('yhi', 'z', 'lat'), pairs)  13.1 us
    all_to_all x1, waiting for transfers between devices, total_over_devices(): pieces = lax.all_to_all(half, wide, 0, 0, tiled=True)  6.21 us
    pallas_call x1, Pallas kernels, shards(): call(expand_kernel, sds(bias_shape, F32), scratch=[flat_shape, pltpu.VMEM...  5.93 us
    all_to_all x1, starting transfers between devices, total_over_devices(): mine = lax.all_to_all(spread, wide, 0, 0, tiled=True)  5.52 us
    all_to_all x1, starting transfers between devices, total_over_devices(): pieces = lax.all_to_all(half, wide, 0, 0, tiled=True)  5.37 us
    pallas_call x1, Pallas kernels, give_back(): call(return_kernel, (plane_shape, plane_shape, lat_shape, edge_shape, edg...  4.28 us
  transfers between devices with their start and end apart: 13, of which 6 were waited for; matrix products, arithmetic and copies ran while one was open for 1% of the time, Pallas kernels for 14%

profile of v3, /device:TPU:1, one launch (start us, length us, event | category | flops | bytes accessed | tf_op | source)
XLA Modules:
  0.0 98.3 jit_solution(2022688501377932670)
XLA Ops:
  0.6 0.0 copy-start.1
  0.6 2.8 %shard_map.208 = (bf16[8,54,384]{2,1,0:T(8,128)(2,1)}, bf16[8,18,384]{2,1,0:T(8,128)(2,1)}, bf16[8,18,384]{2,1,0:T(8,128)(2,1)}) custom-call(bf16[8,144,192]{2,1,0:T(8,128)(2,1)} %bitcast.24, bf16[8,144,192]{2,1,0:T(8,128)(2,1)} %bitcast.27, bf16[54,144]{1,0:T(8,128)(2,1)} %constant.58.clone.lat_pick, bf16[18,144]{1,0:T(8,128)(2,1)} %constant.59.clone.lon_pick, ...), custom_call_target="tpu_custom_call" | custom-call | flops 1000000000 | bytes 2000000 | tf_op jit(solution)/shard_map/pallas_call | solution.py:424
  3.4 3.3 %collective-permute-start = (bf16[8,54,384]{2,1,0:T(8,128)(2,1)}, bf16[8,54,384]{2,1,0:T(8,128)(2,1)S(1)}, u32[]{:S(2)}, u32[]{:S(2)}) collective-permute-start(bf16[8,54,384]{2,1,0:T(8,128)(2,1)} %get-tuple-element.36), channel_id=1, source_target_pairs={{0,3},{1,0},{2,1},{3,2},{4,7},{5,4},{6,5},{7,6},{8,11},{9,8},{10,9... | collective-permute-start | bytes 995336 | tf_op jit(solution)/shard_map/ppermute | solution.py:360
  6.7 8.2 %collective-permute-start.1 = (bf16[8,18,384]{2,1,0:T(8,128)(2,1)}, bf16[8,18,384]{2,1,0:T(8,128)(2,1)S(1)}, u32[]{:S(2)}, u32[]{:S(2)}) collective-permute-start(bf16[8,18,384]{2,1,0:T(8,128)(2,1)} %get-tuple-element.37), channel_id=1, source_target_pairs={{0,60},{1,61},{2,62},{3,63},{4,0},{5,1},{6,2},{7,3},{8,4},{9,5},{1... | collective-permute-start | bytes 331784 | tf_op jit(solution)/shard_map/ppermute | solution.py:360
  14.9 1.0 %collective-permute-start.2 = (bf16[8,18,384]{2,1,0:T(8,128)(2,1)}, bf16[8,18,384]{2,1,0:T(8,128)(2,1)S(1)}, u32[]{:S(2)}, u32[]{:S(2)}) collective-permute-start(bf16[8,18,384]{2,1,0:T(8,128)(2,1)} %get-tuple-element.38), channel_id=1, source_target_pairs={{0,63},{1,60},{2,61},{3,62},{4,3},{5,0},{6,1},{7,2},{8,7},{9,4},{1... | collective-permute-start | bytes 331784 | tf_op jit(solution)/shard_map/ppermute | solution.py:360
  15.9 0.0 copy-done.1
  15.9 0.2 copy.23
  16.1 0.9 copy.24
  17.0 5.9 %shard_map.209.bias_hbm = f32[7,576,128]{2,1,0:T(8,128)} custom-call(s32[1]{0:T(128)} %bitcast.6.last_ref, f32[24,1,3312]{2,1,0:T(1,128)} %bitcast.20, bf16[12,384,256]{2,1,0:T(8,128)(2,1)} %constant.61.clone.sel_ref.sel_hbm), custom_call_target="tpu_custom_call" | custom-call | flops 1000000000 | bytes 2000000 | tf_op jit(solution)/shard_map/pallas_call | solution.py:440
  22.9 0.0 collective-permute-done.1.lon_in
  22.9 0.0 collective-permute-done.2.diag_in
  22.9 0.0 copy-start.6
  22.9 0.0 collective-permute-done.lat_in
  22.9 0.0 copy-start.2
  23.0 0.6 copy-done.5
  23.6 0.1 copy-done.6
  23.6 0.1 copy-done.2
  23.7 14.3 %shard_map.210 = (bf16[1152,192]{1,0:T(8,128)(2,1)}, bf16[1152,192]{1,0:T(8,128)(2,1)}, bf16[1024,128]{1,0:T(8,128)(2,1)}, bf16[1024,128]{1,0:T(8,128)(2,1)}) custom-call(s32[1]{0:T(128)} %bitcast.2.core_ref, bf16[8,144,192]{2,1,0:T(8,128)(2,1)} %bitcast.25, bf16[8,144,192]{2,1,0:T(8,128)(2,1)} %bitcast.28, bf16[8,54,384]{2,1,0:T(8,128)(2,1)} %copy-done.2, ...), custom_call_target="tpu_custom_call" | custom-call | flops 10000000000 | bytes 20000000 | tf_op jit(solution)/shard_map/pallas_call | solution.py:457
  38.1 1.6 %collective-permute-start.3 = (bf16[1024,128]{1,0:T(8,128)(2,1)}, bf16[1024,128]{1,0:T(8,128)(2,1)S(1)}, u32[]{:S(2)}, u32[]{:S(2)}) collective-permute-start(bf16[1024,128]{1,0:T(8,128)(2,1)} %get-tuple-element.40), channel_id=1, source_target_pairs={{0,64},{64,0},{1,65},{65,1},{2,66},{66,2},{3,67},{67,3},{4,68},{68... | collective-permute-start | bytes 786440 | tf_op jit(solution)/shard_map/ppermute | solution.py:364
  39.7 1.4 %collective-permute-done.3 = bf16[1024,128]{1,0:T(8,128)(2,1)S(1)} collective-permute-done((bf16[1024,128]{1,0:T(8,128)(2,1)}, bf16[1024,128]{1,0:T(8,128)(2,1)S(1)}, u32[]{:S(2)}, u32[]{:S(2)}) %collective-permute-start.3) | collective-permute-done | bytes 262176 | tf_op jit(solution)/shard_map/ppermute | solution.py:364
  41.0 1.7 %add_convert_fusion = bf16[1024,128]{1,0:T(8,128)(2,1)} fusion(bf16[1024,128]{1,0:T(8,128)(2,1)S(1)} %collective-permute-done.3, bf16[1024,128]{1,0:T(8,128)(2,1)} %get-tuple-element.39), kind=kLoop, calls=%fused_computation.1 | loop fusion | flops 524288 | bytes 786432 | tf_op jit(solution)/shard_map/convert_element_type | solution.py:370
  42.8 5.4 %all-to-all-start = ((bf16[32,32,128]{2,1,0:T(8,128)(2,1)}), bf16[32,32,128]{2,1,0:T(8,128)(2,1)S(1)}, u32[]{:S(2)}, u32[]{:S(2)}) async-start(bf16[32,32,128]{2,1,0:T(8,128)(2,1)} %bitcast.8), calls=%async_computation | async-start | bytes 524288 | tf_op jit(solution)/shard_map/all_to_all | solution.py:373
  48.1 4.3 %shard_map.211 = (bf16[8,144,192]{2,1,0:T(8,128)(2,1)}, bf16[8,144,192]{2,1,0:T(8,128)(2,1)}, bf16[8,54,384]{2,1,0:T(8,128)(2,1)}, bf16[8,18,384]{2,1,0:T(8,128)(2,1)}, bf16[8,18,384]{2,1,0:T(8,128)(2,1)}) custom-call(bf16[8,144,192]{2,1,0:T(8,128)(2,1)} %bitcast.26, bf16[8,144,192]{2,1,0:T(8,128)(2,1)} %bitcast.29, ...), custom_call_target="tpu_custom_call" | custom-call | flops 2000000000 | bytes 4000000 | tf_op jit(solution)/shard_map/pallas_call | solution.py:477
  52.4 6.2 %all-to-all-done = bf16[32,32,128]{2,1,0:T(8,128)(2,1)S(1)} async-done(((bf16[32,32,128]{2,1,0:T(8,128)(2,1)}), bf16[32,32,128]{2,1,0:T(8,128)(2,1)S(1)}, u32[]{:S(2)}, u32[]{:S(2)}) %all-to-all-start) | async-done | bytes 262176 | tf_op jit(solution)/shard_map/all_to_all | solution.py:373
  58.7 3.2 %collective-permute-start.6 = (f32[32,128]{1,0:T(8,128)S(1)}, f32[32,128]{1,0:T(8,128)S(1)}, u32[]{:S(2)}, u32[]{:S(2)}) collective-permute-start(f32[32,128]{1,0:T(8,128)S(1)} %convert_reduce_fusion), channel_id=1, source_target_pairs={{0,3},{1,0},{2,1},{3,2},{4,7},{5,4},{6,5},{7,6},{8,11},{9,8},{10,9... | collective-permute-start | bytes 49160 | tf_op jit(solution)/shard_map/ppermute | solution.py:382
  61.8 0.0 collective-permute-start.5
  61.8 0.7 collective-permute-start.4
  62.5 0.2 collective-permute-done.6
  62.7 3.2 %collective-permute-done.5 = f32[32,128]{1,0:T(8,128)S(1)} collective-permute-done((f32[32,128]{1,0:T(8,128)S(1)}, f32[32,128]{1,0:T(8,128)S(1)}, u32[]{:S(2)}, u32[]{:S(2)}) %collective-permute-start.5) | collective-permute-done | bytes 16416 | tf_op jit(solution)/shard_map/ppermute | solution.py:382
  65.9 0.0 collective-permute-done.4
  66.0 0.7 broadcast_in_dim.2
  66.7 5.5 %all-to-all-start.1 = ((bf16[32,32,128]{2,1,0:T(8,128)(2,1)}), bf16[32,32,128]{2,1,0:T(8,128)(2,1)S(1)}, u32[]{:S(2)}, u32[]{:S(2)}) async-start(bf16[32,32,128]{2,1,0:T(8,128)(2,1)} %bitcast.12), calls=%async_computation.1 | async-start | bytes 524288 | tf_op jit(solution)/shard_map/all_to_all | solution.py:387
  72.2 0.1 collective-permute-start.7
  72.3 1.3 %collective-permute-start.8 = (bf16[8,18,384]{2,1,0:T(8,128)(2,1)}, bf16[8,18,384]{2,1,0:T(8,128)(2,1)S(1)}, u32[]{:S(2)}, u32[]{:S(2)}) collective-permute-start(bf16[8,18,384]{2,1,0:T(8,128)(2,1)} %get-tuple-element.54), channel_id=1, source_target_pairs={{0,4},{1,5},{2,6},{3,7},{4,8},{5,9},{6,10},{7,11},{8,12},{9,13},{1... | collective-permute-start | bytes 331784 | tf_op jit(solution)/shard_map/ppermute | solution.py:360
  73.6 2.2 %collective-permute-start.9 = (bf16[8,18,384]{2,1,0:T(8,128)(2,1)}, bf16[8,18,384]{2,1,0:T(8,128)(2,1)S(1)}, u32[]{:S(2)}, u32[]{:S(2)}) collective-permute-start(bf16[8,18,384]{2,1,0:T(8,128)(2,1)} %get-tuple-element.55), channel_id=1, source_target_pairs={{0,5},{1,6},{2,7},{3,4},{4,9},{5,10},{6,11},{7,8},{8,13},{9,14},{1... | collective-permute-start | bytes 331784 | tf_op jit(solution)/shard_map/ppermute | solution.py:360
  75.9 7.7 %collective-permute-done.8.lon_in = bf16[8,18,384]{2,1,0:T(8,128)(2,1)S(1)} collective-permute-done((bf16[8,18,384]{2,1,0:T(8,128)(2,1)}, bf16[8,18,384]{2,1,0:T(8,128)(2,1)S(1)}, u32[]{:S(2)}, u32[]{:S(2)}) %collective-permute-start.8) | collective-permute-done | bytes 110624 | tf_op jit(solution)/shard_map/ppermute | solution.py:360
  83.5 5.4 %collective-permute-done.9.diag_in = bf16[8,18,384]{2,1,0:T(8,128)(2,1)S(1)} collective-permute-done((bf16[8,18,384]{2,1,0:T(8,128)(2,1)}, bf16[8,18,384]{2,1,0:T(8,128)(2,1)S(1)}, u32[]{:S(2)}, u32[]{:S(2)}) %collective-permute-start.9) | collective-permute-done | bytes 110624 | tf_op jit(solution)/shard_map/ppermute | solution.py:360
  89.0 0.0 collective-permute-done.7.lat_in
  89.0 0.0 all-to-all-done.1
  89.0 0.0 copy-start
  89.0 2.4 %collective-permute-start.10 = (bf16[1024,128]{1,0:T(8,128)(2,1)S(1)}, bf16[1024,128]{1,0:T(8,128)(2,1)S(1)}, u32[]{:S(2)}, u32[]{:S(2)}) collective-permute-start(bf16[1024,128]{1,0:T(8,128)(2,1)S(1)} %bitcast.22), channel_id=1, source_target_pairs={{0,64},{64,0},{1,65},{65,1},{2,66},{66,2},{3,67},{67,3},{4,68},{68... | collective-permute-start | bytes 786440 | tf_op jit(solution)/shard_map/ppermute | solution.py:364
  91.5 0.0 copy-done.7
  91.5 0.0 copy-done.8
  91.5 0.0 copy-done.3
  91.5 3.5 %shard_map.212 = (bf16[8,144,192]{2,1,0:T(8,128)(2,1)}, bf16[8,144,192]{2,1,0:T(8,128)(2,1)}) custom-call(bf16[8,144,192]{2,1,0:T(8,128)(2,1)} %get-tuple-element.45.base_ref, bf16[8,144,192]{2,1,0:T(8,128)(2,1)} %get-tuple-element.46.gbase_ref, bf16[8,54,384]{2,1,0:T(8,128)(2,1)} %copy-done.3, bf16[8,18,384]{2,1,0:T(8,128)(2,1)} %copy-done.7, ...), custom_call_target="tpu_custom_call" | custom-call | flops 2000000000 | bytes 4000000 | tf_op jit(solution)/shard_map/pallas_call | solution.py:487
  95.0 0.0 collective-permute-done.10.other_ref
  95.0 0.7 copy-done.4
  95.7 2.6 %shard_map.213 = (f32[192,576]{1,0:T(8,128)}, f32[192,192]{1,0:T(8,128)}, f32[1,192]{1,0:T(1,128)}, f32[24,1,3312]{2,1,0:T(1,128)}) custom-call(s32[1]{0:T(128)} %bitcast.2.core_ref, bf16[1024,128]{1,0:T(8,128)(2,1)} %bitcast.23, bf16[1024,128]{1,0:T(8,128)(2,1)} %copy-done.4), custom_call_target="tpu_custom_call" | custom-call | flops 1000000000 | bytes 2000000 | tf_op jit(solution)/shard_map/pallas_call | solution.py:493
  (8 shorter events, 0.1 us)
Async XLA Ops:
  0.6 15.3 %copy-start.1 = (bf16[192,576]{1,0:T(8,128)(2,1)S(1)}, bf16[192,576]{1,0:T(8,128)(2,1)}, u32[]{:S(2)}) copy-start(bf16[192,576]{1,0:T(8,128)(2,1)} %param.20) | copy-start | bytes 663556
  3.4 19.5 %collective-permute-start = (bf16[8,54,384]{2,1,0:T(8,128)(2,1)}, bf16[8,54,384]{2,1,0:T(8,128)(2,1)S(1)}, u32[]{:S(2)}, u32[]{:S(2)}) collective-permute-start(bf16[8,54,384]{2,1,0:T(8,128)(2,1)} %get-tuple-element.36), channel_id=1, source_target_pairs={{0,3},{1,0},{2,1},{3,2},{4,7},{5,4},{6,5},{7,6},{8,11},{9,8},{10,9... | collective-permute-start | bytes 995336 | tf_op jit(solution)/shard_map/ppermute | solution.py:360
  6.7 16.2 %collective-permute-start.1 = (bf16[8,18,384]{2,1,0:T(8,128)(2,1)}, bf16[8,18,384]{2,1,0:T(8,128)(2,1)S(1)}, u32[]{:S(2)}, u32[]{:S(2)}) collective-permute-start(bf16[8,18,384]{2,1,0:T(8,128)(2,1)} %get-tuple-element.37), channel_id=1, source_target_pairs={{0,60},{1,61},{2,62},{3,63},{4,0},{5,1},{6,2},{7,3},{8,4},{9,5},{1... | collective-permute-start | bytes 331784 | tf_op jit(solution)/shard_map/ppermute | solution.py:360
  14.9 8.0 %collective-permute-start.2 = (bf16[8,18,384]{2,1,0:T(8,128)(2,1)}, bf16[8,18,384]{2,1,0:T(8,128)(2,1)S(1)}, u32[]{:S(2)}, u32[]{:S(2)}) collective-permute-start(bf16[8,18,384]{2,1,0:T(8,128)(2,1)} %get-tuple-element.38), channel_id=1, source_target_pairs={{0,63},{1,60},{2,61},{3,62},{4,3},{5,0},{6,1},{7,2},{8,7},{9,4},{1... | collective-permute-start | bytes 331784 | tf_op jit(solution)/shard_map/ppermute | solution.py:360
  22.9 0.7 copy-start.5
  22.9 0.7 copy-start.6
  22.9 0.8 copy-start.2
  38.1 3.0 %collective-permute-start.3 = (bf16[1024,128]{1,0:T(8,128)(2,1)}, bf16[1024,128]{1,0:T(8,128)(2,1)S(1)}, u32[]{:S(2)}, u32[]{:S(2)}) collective-permute-start(bf16[1024,128]{1,0:T(8,128)(2,1)} %get-tuple-element.40), channel_id=1, source_target_pairs={{0,64},{64,0},{1,65},{65,1},{2,66},{66,2},{3,67},{67,3},{4,68},{68... | collective-permute-start | bytes 786440 | tf_op jit(solution)/shard_map/ppermute | solution.py:364
  42.8 15.9 %all-to-all-start = ((bf16[32,32,128]{2,1,0:T(8,128)(2,1)}), bf16[32,32,128]{2,1,0:T(8,128)(2,1)S(1)}, u32[]{:S(2)}, u32[]{:S(2)}) async-start(bf16[32,32,128]{2,1,0:T(8,128)(2,1)} %bitcast.8), calls=%async_computation | async-start | bytes 524288 | tf_op jit(solution)/shard_map/all_to_all | solution.py:373
  58.7 4.0 %collective-permute-start.6 = (f32[32,128]{1,0:T(8,128)S(1)}, f32[32,128]{1,0:T(8,128)S(1)}, u32[]{:S(2)}, u32[]{:S(2)}) collective-permute-start(f32[32,128]{1,0:T(8,128)S(1)} %convert_reduce_fusion), channel_id=1, source_target_pairs={{0,3},{1,0},{2,1},{3,2},{4,7},{5,4},{6,5},{7,6},{8,11},{9,8},{10,9... | collective-permute-start | bytes 49160 | tf_op jit(solution)/shard_map/ppermute | solution.py:382
  61.8 4.1 %collective-permute-start.5 = (f32[32,128]{1,0:T(8,128)S(1)}, f32[32,128]{1,0:T(8,128)S(1)}, u32[]{:S(2)}, u32[]{:S(2)}) collective-permute-start(f32[32,128]{1,0:T(8,128)S(1)} %convert_reduce_fusion), channel_id=1, source_target_pairs={{0,2},{1,3},{2,0},{3,1},{4,6},{5,7},{6,4},{7,5},{8,10},{9,11},{10,... | collective-permute-start | bytes 49160 | tf_op jit(solution)/shard_map/ppermute | solution.py:382
  61.8 4.1 %collective-permute-start.4 = (f32[32,128]{1,0:T(8,128)S(1)}, f32[32,128]{1,0:T(8,128)S(1)}, u32[]{:S(2)}, u32[]{:S(2)}) collective-permute-start(f32[32,128]{1,0:T(8,128)S(1)} %convert_reduce_fusion), channel_id=1, source_target_pairs={{0,1},{1,2},{2,3},{3,0},{4,5},{5,6},{6,7},{7,4},{8,9},{9,10},{10,1... | collective-permute-start | bytes 49160 | tf_op jit(solution)/shard_map/ppermute | solution.py:382
  66.7 22.3 %all-to-all-start.1 = ((bf16[32,32,128]{2,1,0:T(8,128)(2,1)}), bf16[32,32,128]{2,1,0:T(8,128)(2,1)S(1)}, u32[]{:S(2)}, u32[]{:S(2)}) async-start(bf16[32,32,128]{2,1,0:T(8,128)(2,1)} %bitcast.12), calls=%async_computation.1 | async-start | bytes 524288 | tf_op jit(solution)/shard_map/all_to_all | solution.py:387
  72.2 16.8 %collective-permute-start.7 = (bf16[8,54,384]{2,1,0:T(8,128)(2,1)}, bf16[8,54,384]{2,1,0:T(8,128)(2,1)S(1)}, u32[]{:S(2)}, u32[]{:S(2)}) collective-permute-start(bf16[8,54,384]{2,1,0:T(8,128)(2,1)} %get-tuple-element.53), channel_id=1, source_target_pairs={{0,1},{1,2},{2,3},{3,0},{4,5},{5,6},{6,7},{7,4},{8,9},{9,10},{10,1... | collective-permute-start | bytes 995336 | tf_op jit(solution)/shard_map/ppermute | solution.py:360
  72.3 11.2 %collective-permute-start.8 = (bf16[8,18,384]{2,1,0:T(8,128)(2,1)}, bf16[8,18,384]{2,1,0:T(8,128)(2,1)S(1)}, u32[]{:S(2)}, u32[]{:S(2)}) collective-permute-start(bf16[8,18,384]{2,1,0:T(8,128)(2,1)} %get-tuple-element.54), channel_id=1, source_target_pairs={{0,4},{1,5},{2,6},{3,7},{4,8},{5,9},{6,10},{7,11},{8,12},{9,13},{1... | collective-permute-start | bytes 331784 | tf_op jit(solution)/shard_map/ppermute | solution.py:360
  73.6 15.4 %collective-permute-start.9 = (bf16[8,18,384]{2,1,0:T(8,128)(2,1)}, bf16[8,18,384]{2,1,0:T(8,128)(2,1)S(1)}, u32[]{:S(2)}, u32[]{:S(2)}) collective-permute-start(bf16[8,18,384]{2,1,0:T(8,128)(2,1)} %get-tuple-element.55), channel_id=1, source_target_pairs={{0,5},{1,6},{2,7},{3,4},{4,9},{5,10},{6,11},{7,8},{8,13},{9,14},{1... | collective-permute-start | bytes 331784 | tf_op jit(solution)/shard_map/ppermute | solution.py:360
  83.5 7.9 %copy-start.7 = (bf16[8,18,384]{2,1,0:T(8,128)(2,1)}, bf16[8,18,384]{2,1,0:T(8,128)(2,1)S(1)}, u32[]{:S(2)}) copy-start(bf16[8,18,384]{2,1,0:T(8,128)(2,1)S(1)} %collective-permute-done.8.lon_in) | copy-start | bytes 331780
  89.0 2.5 %copy-start.8 = (bf16[8,18,384]{2,1,0:T(8,128)(2,1)}, bf16[8,18,384]{2,1,0:T(8,128)(2,1)S(1)}, u32[]{:S(2)}) copy-start(bf16[8,18,384]{2,1,0:T(8,128)(2,1)S(1)} %collective-permute-done.9.diag_in) | copy-start | bytes 331780
  89.0 2.5 %copy-start.3 = (bf16[8,54,384]{2,1,0:T(8,128)(2,1)}, bf16[8,54,384]{2,1,0:T(8,128)(2,1)S(1)}, u32[]{:S(2)}) copy-start(bf16[8,54,384]{2,1,0:T(8,128)(2,1)S(1)} %collective-permute-done.7.lat_in) | copy-start | bytes 995332
  89.0 6.0 %copy-start = (bf16[32,32,128]{2,1,0:T(8,128)(2,1)}, bf16[32,32,128]{2,1,0:T(8,128)(2,1)S(1)}, u32[]{:S(2)}) copy-start(bf16[32,32,128]{2,1,0:T(8,128)(2,1)S(1)} %all-to-all-done.1) | copy-start | bytes 786436
  89.0 6.0 %collective-permute-start.10 = (bf16[1024,128]{1,0:T(8,128)(2,1)S(1)}, bf16[1024,128]{1,0:T(8,128)(2,1)S(1)}, u32[]{:S(2)}, u32[]{:S(2)}) collective-permute-start(bf16[1024,128]{1,0:T(8,128)(2,1)S(1)} %bitcast.22), channel_id=1, source_target_pairs={{0,64},{64,0},{1,65},{65,1},{2,66},{66,2},{3,67},{67,3},{4,68},{68... | collective-permute-start | bytes 786440 | tf_op jit(solution)/shard_map/ppermute | solution.py:364
  95.0 0.7 copy-start.4

commit v4 on v3

--- a/solution.py
+++ b/solution.py
@@ -373,20 +373,22 @@
     pieces = lax.all_to_all(half, wide, 0, 0, tiled=True)
     keeps, strips = fn(inputs)
     pieces, _ = lax.optimization_barrier((pieces, strips))
+    backs = [passed(strip, *step) for strip, step in zip(strips, ((1, 0), (0, 1), (1, 1)))]
     piece = jnp.sum(pieces.reshape(peers, PIECE, LANES).astype(F32), axis=0)
     lats = lax.axis_size("lat")
     place_here = lax.axis_index("core") * peers + lax.axis_index(wide)
     shared = jnp.logical_or(place_here < BROW // PIECE, place_here >= GROW // PIECE)
-    others = jnp.zeros_like(piece)
-    for step in range(1, lats):
-        others = others + lax.ppermute(piece, "lat", [(a, (a + step) % lats) for a in range(lats)])
+    others = [
+        lax.ppermute(piece, "lat", [(a, (a + step) % lats) for a in range(lats)]) for step in range(1, lats)
+    ]
+    others, backs = lax.optimization_barrier((others, tuple(backs)))
+    others = sum(others)
     piece = jnp.where(shared, piece + others, piece).astype(BF)
     spread = jnp.broadcast_to(piece[None], (peers, PIECE, LANES)).reshape(half.shape)
-    spread, strips = lax.optimization_barrier((spread, strips))
-    backs = [passed(strip, *step) for strip, step in zip(strips, ((1, 0), (0, 1), (1, 1)))]
+    spread, backs = lax.optimization_barrier((spread, backs))
     mine = lax.all_to_all(spread, wide, 0, 0, tiled=True)
-    mine, backs = lax.optimization_barrier((mine, backs))
-    return mine, swapped(mine), last(*keeps, *backs)
+    mine, outs = lax.optimization_barrier((mine, last(*keeps, *backs)))
+    return mine, swapped(mine), outs
 
 
 def call(kernel, out_shape, scratch=(), smem=0, count=0, flops=0, far=0):

time: 98.7 us -> 96.4 us (0.977)
  waiting for transfers between devices: 24.1 us -> 17.7 us
  starting transfers between devices: 34.9 us -> 38.8 us
    ppermute x6, waiting for transfers between devices: 13.1 us -> 6.49 us  [passed(): return lax.ppermute(value, ('yhi', 'z', 'lat'), pairs)]
    all_to_all x1, waiting for transfers between devices: 0.01 us -> 6.47 us  [total_over_devices(): mine = lax.all_to_all(spread, wide, 0, 0, tiled=True)]
    all_to_all x1, waiting for transfers between devices: 6.21 us -> 2.25 us  [total_over_devices(): pieces = lax.all_to_all(half, wide, 0, 0, tiled=True)]
    ppermute x3, waiting for transfers between devices: 3.42 us -> 0.01 us  [total_over_devices(): lax.ppermute(piece, 'lat', [(a, (a + step) % lats) for a in range(lats)])]
    all_to_all x1, starting transfers between devices: 5.52 us -> 7.62 us  [total_over_devices(): mine = lax.all_to_all(spread, wide, 0, 0, tiled=True)]
    ppermute x2, starting transfers between devices: 4.05 us -> 5.78 us  [swapped(): return lax.ppermute(value, 'core', [(0, 1), (1, 0)])]
    ppermute x2, waiting for transfers between devices: 1.38 us -> 2.53 us  [swapped(): return lax.ppermute(value, 'core', [(0, 1), (1, 0)])]
where the time goes in v4:
time: 96.4 us; the launch traced here: 95.9 us
  starting transfers between devices  38.8 us (40%)
  Pallas kernels  33.4 us (35%)
  waiting for transfers between devices  17.7 us (18%)
  local copies, waits for them, and re-layouts  3.36 us (3%)
  other arithmetic  1.78 us (2%)
    ppermute x6, starting transfers between devices, passed(): return lax.ppermute(value, ('yhi', 'z', 'lat'), pairs)  16.5 us
    pallas_call x1, Pallas kernels, shards(): call(main_kernel, (token_shape, token_shape, half_shape, half_shape), scr...  14.3 us
    all_to_all x1, starting transfers between devices, total_over_devices(): mine = lax.all_to_all(spread, wide, 0, 0, tiled=True)  7.62 us
    ppermute x6, waiting for transfers between devices, passed(): return lax.ppermute(value, ('yhi', 'z', 'lat'), pairs)  6.49 us
    all_to_all x1, waiting for transfers between devices, total_over_devices(): mine = lax.all_to_all(spread, wide, 0, 0, tiled=True)  6.47 us
    pallas_call x1, Pallas kernels, shards(): call(expand_kernel, sds(bias_shape, F32), scratch=[flat_shape, pltpu.VMEM...  5.93 us
    ppermute x2, starting transfers between devices, swapped(): return lax.ppermute(value, 'core', [(0, 1), (1, 0)])  5.78 us
    all_to_all x1, starting transfers between devices, total_over_devices(): pieces = lax.all_to_all(half, wide, 0, 0, tiled=True)  5.37 us
  transfers between devices with their start and end apart: 13, of which 6 were waited for; matrix products, arithmetic and copies ran while one was open for 1% of the time, Pallas kernels for 14%

profile of v4, /device:TPU:1, one launch (start us, length us, event | category | flops | bytes accessed | tf_op | source)
XLA Modules:
  0.0 95.9 jit_solution(3967212612060687356)
XLA Ops:
  0.6 0.0 copy-start.1
  0.6 2.8 %shard_map.208 = (bf16[8,54,384]{2,1,0:T(8,128)(2,1)}, bf16[8,18,384]{2,1,0:T(8,128)(2,1)}, bf16[8,18,384]{2,1,0:T(8,128)(2,1)}) custom-call(bf16[8,144,192]{2,1,0:T(8,128)(2,1)} %bitcast.24, bf16[8,144,192]{2,1,0:T(8,128)(2,1)} %bitcast.27, bf16[54,144]{1,0:T(8,128)(2,1)} %constant.58.clone.lat_pick, bf16[18,144]{1,0:T(8,128)(2,1)} %constant.59.clone.lon_pick, ...), custom_call_target="tpu_custom_call" | custom-call | flops 1000000000 | bytes 2000000 | tf_op jit(solution)/shard_map/pallas_call | solution.py:426
  3.4 3.3 %collective-permute-start = (bf16[8,54,384]{2,1,0:T(8,128)(2,1)}, bf16[8,54,384]{2,1,0:T(8,128)(2,1)S(1)}, u32[]{:S(2)}, u32[]{:S(2)}) collective-permute-start(bf16[8,54,384]{2,1,0:T(8,128)(2,1)} %get-tuple-element.41), channel_id=1, source_target_pairs={{0,3},{1,0},{2,1},{3,2},{4,7},{5,4},{6,5},{7,6},{8,11},{9,8},{10,9... | collective-permute-start | bytes 995336 | tf_op jit(solution)/shard_map/ppermute | solution.py:360
  6.7 8.2 %collective-permute-start.1 = (bf16[8,18,384]{2,1,0:T(8,128)(2,1)}, bf16[8,18,384]{2,1,0:T(8,128)(2,1)S(1)}, u32[]{:S(2)}, u32[]{:S(2)}) collective-permute-start(bf16[8,18,384]{2,1,0:T(8,128)(2,1)} %get-tuple-element.42), channel_id=1, source_target_pairs={{0,60},{1,61},{2,62},{3,63},{4,0},{5,1},{6,2},{7,3},{8,4},{9,5},{1... | collective-permute-start | bytes 331784 | tf_op jit(solution)/shard_map/ppermute | solution.py:360
  14.9 1.0 %collective-permute-start.2 = (bf16[8,18,384]{2,1,0:T(8,128)(2,1)}, bf16[8,18,384]{2,1,0:T(8,128)(2,1)S(1)}, u32[]{:S(2)}, u32[]{:S(2)}) collective-permute-start(bf16[8,18,384]{2,1,0:T(8,128)(2,1)} %get-tuple-element.43), channel_id=1, source_target_pairs={{0,63},{1,60},{2,61},{3,62},{4,3},{5,0},{6,1},{7,2},{8,7},{9,4},{1... | collective-permute-start | bytes 331784 | tf_op jit(solution)/shard_map/ppermute | solution.py:360
  15.9 0.0 copy-done.1
  15.9 0.2 copy.23
  16.1 0.9 copy.24
  17.0 5.9 %shard_map.209.bias_hbm = f32[7,576,128]{2,1,0:T(8,128)} custom-call(s32[1]{0:T(128)} %bitcast.6.last_ref, f32[24,1,3312]{2,1,0:T(1,128)} %bitcast.20, bf16[12,384,256]{2,1,0:T(8,128)(2,1)} %constant.61.clone.sel_ref.sel_hbm), custom_call_target="tpu_custom_call" | custom-call | flops 1000000000 | bytes 2000000 | tf_op jit(solution)/shard_map/pallas_call | solution.py:442
  22.9 0.0 collective-permute-done.1.lon_in
  22.9 0.0 collective-permute-done.2.diag_in
  22.9 0.0 copy-start.8
  22.9 0.0 collective-permute-done.lat_in
  22.9 0.0 copy-start.3
  23.0 0.6 copy-done.7
  23.6 0.1 copy-done.8
  23.6 0.1 copy-done.3
  23.7 14.3 %shard_map.210 = (bf16[1152,192]{1,0:T(8,128)(2,1)}, bf16[1152,192]{1,0:T(8,128)(2,1)}, bf16[1024,128]{1,0:T(8,128)(2,1)}, bf16[1024,128]{1,0:T(8,128)(2,1)}) custom-call(s32[1]{0:T(128)} %bitcast.core_ref, bf16[8,144,192]{2,1,0:T(8,128)(2,1)} %bitcast.25, bf16[8,144,192]{2,1,0:T(8,128)(2,1)} %bitcast.28, bf16[8,54,384]{2,1,0:T(8,128)(2,1)} %copy-done.3, ...), custom_call_target="tpu_custom_call" | custom-call | flops 10000000000 | bytes 20000000 | tf_op jit(solution)/shard_map/pallas_call | solution.py:459
  38.1 1.6 %collective-permute-start.3 = (bf16[1024,128]{1,0:T(8,128)(2,1)}, bf16[1024,128]{1,0:T(8,128)(2,1)S(1)}, u32[]{:S(2)}, u32[]{:S(2)}) collective-permute-start(bf16[1024,128]{1,0:T(8,128)(2,1)} %get-tuple-element.45), channel_id=1, source_target_pairs={{0,64},{64,0},{1,65},{65,1},{2,66},{66,2},{3,67},{67,3},{4,68},{68... | collective-permute-start | bytes 786440 | tf_op jit(solution)/shard_map/ppermute | solution.py:364
  39.7 1.4 %collective-permute-done.3 = bf16[1024,128]{1,0:T(8,128)(2,1)S(1)} collective-permute-done((bf16[1024,128]{1,0:T(8,128)(2,1)}, bf16[1024,128]{1,0:T(8,128)(2,1)S(1)}, u32[]{:S(2)}, u32[]{:S(2)}) %collective-permute-start.3) | collective-permute-done | bytes 262176 | tf_op jit(solution)/shard_map/ppermute | solution.py:364
  41.0 1.7 %add_convert_fusion = bf16[1024,128]{1,0:T(8,128)(2,1)} fusion(bf16[1024,128]{1,0:T(8,128)(2,1)S(1)} %collective-permute-done.3, bf16[1024,128]{1,0:T(8,128)(2,1)} %get-tuple-element.44), kind=kLoop, calls=%fused_computation.1 | loop fusion | flops 524288 | bytes 786432 | tf_op jit(solution)/shard_map/convert_element_type | solution.py:370
  42.8 5.4 %all-to-all-start = ((bf16[32,32,128]{2,1,0:T(8,128)(2,1)}), bf16[32,32,128]{2,1,0:T(8,128)(2,1)S(1)}, u32[]{:S(2)}, u32[]{:S(2)}) async-start(bf16[32,32,128]{2,1,0:T(8,128)(2,1)} %bitcast.8), calls=%async_computation | async-start | bytes 524288 | tf_op jit(solution)/shard_map/all_to_all | solution.py:373
  48.1 4.3 %shard_map.211 = (bf16[8,144,192]{2,1,0:T(8,128)(2,1)}, bf16[8,144,192]{2,1,0:T(8,128)(2,1)}, bf16[8,54,384]{2,1,0:T(8,128)(2,1)}, bf16[8,18,384]{2,1,0:T(8,128)(2,1)}, bf16[8,18,384]{2,1,0:T(8,128)(2,1)}) custom-call(bf16[8,144,192]{2,1,0:T(8,128)(2,1)} %bitcast.26, bf16[8,144,192]{2,1,0:T(8,128)(2,1)} %bitcast.29, ...), custom_call_target="tpu_custom_call" | custom-call | flops 2000000000 | bytes 4000000 | tf_op jit(solution)/shard_map/pallas_call | solution.py:479
  52.4 0.6 collective-permute-start.7
  53.0 1.2 %collective-permute-start.8 = (bf16[8,18,384]{2,1,0:T(8,128)(2,1)}, bf16[8,18,384]{2,1,0:T(8,128)(2,1)S(1)}, u32[]{:S(2)}, u32[]{:S(2)}) collective-permute-start(bf16[8,18,384]{2,1,0:T(8,128)(2,1)} %get-tuple-element.52), channel_id=1, source_target_pairs={{0,4},{1,5},{2,6},{3,7},{4,8},{5,9},{6,10},{7,11},{8,12},{9,13},{1... | collective-permute-start | bytes 331784 | tf_op jit(solution)/shard_map/ppermute | solution.py:360
  54.3 2.1 %collective-permute-start.9 = (bf16[8,18,384]{2,1,0:T(8,128)(2,1)}, bf16[8,18,384]{2,1,0:T(8,128)(2,1)S(1)}, u32[]{:S(2)}, u32[]{:S(2)}) collective-permute-start(bf16[8,18,384]{2,1,0:T(8,128)(2,1)} %get-tuple-element.53), channel_id=1, source_target_pairs={{0,5},{1,6},{2,7},{3,4},{4,9},{5,10},{6,11},{7,8},{8,13},{9,14},{1... | collective-permute-start | bytes 331784 | tf_op jit(solution)/shard_map/ppermute | solution.py:360
  56.4 2.2 %all-to-all-done = bf16[32,32,128]{2,1,0:T(8,128)(2,1)S(1)} async-done(((bf16[32,32,128]{2,1,0:T(8,128)(2,1)}), bf16[32,32,128]{2,1,0:T(8,128)(2,1)S(1)}, u32[]{:S(2)}, u32[]{:S(2)}) %all-to-all-start) | async-done | bytes 262176 | tf_op jit(solution)/shard_map/all_to_all | solution.py:373
  58.7 3.2 %collective-permute-start.6 = (f32[32,128]{1,0:T(8,128)S(1)}, f32[32,128]{1,0:T(8,128)S(1)}, u32[]{:S(2)}, u32[]{:S(2)}) collective-permute-start(f32[32,128]{1,0:T(8,128)S(1)} %convert_reduce_fusion), channel_id=1, source_target_pairs={{0,3},{1,0},{2,1},{3,2},{4,7},{5,4},{6,5},{7,6},{8,11},{9,8},{10,9... | collective-permute-start | bytes 49160 | tf_op jit(solution)/shard_map/ppermute | solution.py:382
  61.8 0.0 collective-permute-start.5
  61.8 1.1 %collective-permute-done.8.lon_in = bf16[8,18,384]{2,1,0:T(8,128)(2,1)S(1)} collective-permute-done((bf16[8,18,384]{2,1,0:T(8,128)(2,1)}, bf16[8,18,384]{2,1,0:T(8,128)(2,1)S(1)}, u32[]{:S(2)}, u32[]{:S(2)}) %collective-permute-start.8) | collective-permute-done | bytes 110624 | tf_op jit(solution)/shard_map/ppermute | solution.py:360
  63.0 0.4 collective-permute-start.4
  63.4 5.4 %collective-permute-done.9.diag_in = bf16[8,18,384]{2,1,0:T(8,128)(2,1)S(1)} collective-permute-done((bf16[8,18,384]{2,1,0:T(8,128)(2,1)}, bf16[8,18,384]{2,1,0:T(8,128)(2,1)S(1)}, u32[]{:S(2)}, u32[]{:S(2)}) %collective-permute-start.9) | collective-permute-done | bytes 110624 | tf_op jit(solution)/shard_map/ppermute | solution.py:360
  68.8 0.0 collective-permute-done.7.lat_in
  68.8 0.0 collective-permute-done.6
  68.8 0.0 collective-permute-done.5
  68.8 0.0 collective-permute-done.4
  68.8 0.8 broadcast_in_dim.2
  69.6 7.6 %all-to-all-start.1 = ((bf16[32,32,128]{2,1,0:T(8,128)(2,1)}), bf16[32,32,128]{2,1,0:T(8,128)(2,1)S(1)}, u32[]{:S(2)}, u32[]{:S(2)}) async-start(bf16[32,32,128]{2,1,0:T(8,128)(2,1)} %bitcast.12), calls=%async_computation.1 | async-start | bytes 524288 | tf_op jit(solution)/shard_map/all_to_all | solution.py:389
  77.3 0.0 copy-done.5
  77.3 0.0 copy-done.6
  77.3 0.0 copy-done.2
  77.3 3.5 %shard_map.212 = (bf16[8,144,192]{2,1,0:T(8,128)(2,1)}, bf16[8,144,192]{2,1,0:T(8,128)(2,1)}) custom-call(bf16[8,144,192]{2,1,0:T(8,128)(2,1)} %get-tuple-element.62.base_ref, bf16[8,144,192]{2,1,0:T(8,128)(2,1)} %get-tuple-element.63.gbase_ref, bf16[8,54,384]{2,1,0:T(8,128)(2,1)} %copy-done.2, bf16[8,18,384]{2,1,0:T(8,128)(2,1)} %copy-done.5, ...), custom_call_target="tpu_custom_call" | custom-call | flops 2000000000 | bytes 4000000 | tf_op jit(solution)/shard_map/pallas_call | solution.py:489
  80.8 6.5 %all-to-all-done.1 = bf16[32,32,128]{2,1,0:T(8,128)(2,1)S(1)} async-done(((bf16[32,32,128]{2,1,0:T(8,128)(2,1)}), bf16[32,32,128]{2,1,0:T(8,128)(2,1)S(1)}, u32[]{:S(2)}, u32[]{:S(2)}) %all-to-all-start.1) | async-done | bytes 262176 | tf_op jit(solution)/shard_map/all_to_all | solution.py:389
  87.3 4.2 %collective-permute-start.10 = (bf16[1024,128]{1,0:T(8,128)(2,1)S(1)}, bf16[1024,128]{1,0:T(8,128)(2,1)S(1)}, u32[]{:S(2)}, u32[]{:S(2)}) collective-permute-start(bf16[1024,128]{1,0:T(8,128)(2,1)S(1)} %bitcast.22), channel_id=1, source_target_pairs={{0,64},{64,0},{1,65},{65,1},{2,66},{66,2},{3,67},{67,3},{4,68},{68... | collective-permute-start | bytes 786440 | tf_op jit(solution)/shard_map/ppermute | solution.py:364
  91.4 1.2 %collective-permute-done.10.other_ref = bf16[1024,128]{1,0:T(8,128)(2,1)S(1)} collective-permute-done((bf16[1024,128]{1,0:T(8,128)(2,1)S(1)}, bf16[1024,128]{1,0:T(8,128)(2,1)S(1)}, u32[]{:S(2)}, u32[]{:S(2)}) %collective-permute-start.10) | collective-permute-done | bytes 262176 | tf_op jit(solution)/shard_map/ppermute | solution.py:364
  92.6 0.0 copy-done
  92.6 0.7 copy-done.4
  93.3 2.6 %shard_map.213 = (f32[192,576]{1,0:T(8,128)}, f32[192,192]{1,0:T(8,128)}, f32[1,192]{1,0:T(1,128)}, f32[24,1,3312]{2,1,0:T(1,128)}) custom-call(s32[1]{0:T(128)} %bitcast.core_ref, bf16[1024,128]{1,0:T(8,128)(2,1)} %bitcast.23, bf16[1024,128]{1,0:T(8,128)(2,1)} %copy-done.4), custom_call_target="tpu_custom_call" | custom-call | flops 1000000000 | bytes 2000000 | tf_op jit(solution)/shard_map/pallas_call | solution.py:495
  (8 shorter events, 0.1 us)
Async XLA Ops:
  0.6 15.3 %copy-start.1 = (bf16[192,576]{1,0:T(8,128)(2,1)S(1)}, bf16[192,576]{1,0:T(8,128)(2,1)}, u32[]{:S(2)}) copy-start(bf16[192,576]{1,0:T(8,128)(2,1)} %param.20) | copy-start | bytes 663556
  3.4 19.5 %collective-permute-start = (bf16[8,54,384]{2,1,0:T(8,128)(2,1)}, bf16[8,54,384]{2,1,0:T(8,128)(2,1)S(1)}, u32[]{:S(2)}, u32[]{:S(2)}) collective-permute-start(bf16[8,54,384]{2,1,0:T(8,128)(2,1)} %get-tuple-element.41), channel_id=1, source_target_pairs={{0,3},{1,0},{2,1},{3,2},{4,7},{5,4},{6,5},{7,6},{8,11},{9,8},{10,9... | collective-permute-start | bytes 995336 | tf_op jit(solution)/shard_map/ppermute | solution.py:360
  6.7 16.2 %collective-permute-start.1 = (bf16[8,18,384]{2,1,0:T(8,128)(2,1)}, bf16[8,18,384]{2,1,0:T(8,128)(2,1)S(1)}, u32[]{:S(2)}, u32[]{:S(2)}) collective-permute-start(bf16[8,18,384]{2,1,0:T(8,128)(2,1)} %get-tuple-element.42), channel_id=1, source_target_pairs={{0,60},{1,61},{2,62},{3,63},{4,0},{5,1},{6,2},{7,3},{8,4},{9,5},{1... | collective-permute-start | bytes 331784 | tf_op jit(solution)/shard_map/ppermute | solution.py:360
  14.9 8.0 %collective-permute-start.2 = (bf16[8,18,384]{2,1,0:T(8,128)(2,1)}, bf16[8,18,384]{2,1,0:T(8,128)(2,1)S(1)}, u32[]{:S(2)}, u32[]{:S(2)}) collective-permute-start(bf16[8,18,384]{2,1,0:T(8,128)(2,1)} %get-tuple-element.43), channel_id=1, source_target_pairs={{0,63},{1,60},{2,61},{3,62},{4,3},{5,0},{6,1},{7,2},{8,7},{9,4},{1... | collective-permute-start | bytes 331784 | tf_op jit(solution)/shard_map/ppermute | solution.py:360
  22.9 0.7 copy-start.7
  22.9 0.7 copy-start.8
  22.9 0.8 copy-start.3
  38.1 3.0 %collective-permute-start.3 = (bf16[1024,128]{1,0:T(8,128)(2,1)}, bf16[1024,128]{1,0:T(8,128)(2,1)S(1)}, u32[]{:S(2)}, u32[]{:S(2)}) collective-permute-start(bf16[1024,128]{1,0:T(8,128)(2,1)} %get-tuple-element.45), channel_id=1, source_target_pairs={{0,64},{64,0},{1,65},{65,1},{2,66},{66,2},{3,67},{67,3},{4,68},{68... | collective-permute-start | bytes 786440 | tf_op jit(solution)/shard_map/ppermute | solution.py:364
  42.8 15.9 %all-to-all-start = ((bf16[32,32,128]{2,1,0:T(8,128)(2,1)}), bf16[32,32,128]{2,1,0:T(8,128)(2,1)S(1)}, u32[]{:S(2)}, u32[]{:S(2)}) async-start(bf16[32,32,128]{2,1,0:T(8,128)(2,1)} %bitcast.8), calls=%async_computation | async-start | bytes 524288 | tf_op jit(solution)/shard_map/all_to_all | solution.py:373
  52.4 16.4 %collective-permute-start.7 = (bf16[8,54,384]{2,1,0:T(8,128)(2,1)}, bf16[8,54,384]{2,1,0:T(8,128)(2,1)S(1)}, u32[]{:S(2)}, u32[]{:S(2)}) collective-permute-start(bf16[8,54,384]{2,1,0:T(8,128)(2,1)} %get-tuple-element.51), channel_id=1, source_target_pairs={{0,1},{1,2},{2,3},{3,0},{4,5},{5,6},{6,7},{7,4},{8,9},{9,10},{10,1... | collective-permute-start | bytes 995336 | tf_op jit(solution)/shard_map/ppermute | solution.py:360
  53.0 9.9 %collective-permute-start.8 = (bf16[8,18,384]{2,1,0:T(8,128)(2,1)}, bf16[8,18,384]{2,1,0:T(8,128)(2,1)S(1)}, u32[]{:S(2)}, u32[]{:S(2)}) collective-permute-start(bf16[8,18,384]{2,1,0:T(8,128)(2,1)} %get-tuple-element.52), channel_id=1, source_target_pairs={{0,4},{1,5},{2,6},{3,7},{4,8},{5,9},{6,10},{7,11},{8,12},{9,13},{1... | collective-permute-start | bytes 331784 | tf_op jit(solution)/shard_map/ppermute | solution.py:360
  54.3 14.5 %collective-permute-start.9 = (bf16[8,18,384]{2,1,0:T(8,128)(2,1)}, bf16[8,18,384]{2,1,0:T(8,128)(2,1)S(1)}, u32[]{:S(2)}, u32[]{:S(2)}) collective-permute-start(bf16[8,18,384]{2,1,0:T(8,128)(2,1)} %get-tuple-element.53), channel_id=1, source_target_pairs={{0,5},{1,6},{2,7},{3,4},{4,9},{5,10},{6,11},{7,8},{8,13},{9,14},{1... | collective-permute-start | bytes 331784 | tf_op jit(solution)/shard_map/ppermute | solution.py:360
  58.7 10.1 %collective-permute-start.6 = (f32[32,128]{1,0:T(8,128)S(1)}, f32[32,128]{1,0:T(8,128)S(1)}, u32[]{:S(2)}, u32[]{:S(2)}) collective-permute-start(f32[32,128]{1,0:T(8,128)S(1)} %convert_reduce_fusion), channel_id=1, source_target_pairs={{0,3},{1,0},{2,1},{3,2},{4,7},{5,4},{6,5},{7,6},{8,11},{9,8},{10,9... | collective-permute-start | bytes 49160 | tf_op jit(solution)/shard_map/ppermute | solution.py:382
  61.8 6.9 %collective-permute-start.5 = (f32[32,128]{1,0:T(8,128)S(1)}, f32[32,128]{1,0:T(8,128)S(1)}, u32[]{:S(2)}, u32[]{:S(2)}) collective-permute-start(f32[32,128]{1,0:T(8,128)S(1)} %convert_reduce_fusion), channel_id=1, source_target_pairs={{0,2},{1,3},{2,0},{3,1},{4,6},{5,7},{6,4},{7,5},{8,10},{9,11},{10,... | collective-permute-start | bytes 49160 | tf_op jit(solution)/shard_map/ppermute | solution.py:382
  63.0 14.3 %copy-start.5 = (bf16[8,18,384]{2,1,0:T(8,128)(2,1)}, bf16[8,18,384]{2,1,0:T(8,128)(2,1)S(1)}, u32[]{:S(2)}) copy-start(bf16[8,18,384]{2,1,0:T(8,128)(2,1)S(1)} %collective-permute-done.8.lon_in) | copy-start | bytes 331780
  63.0 5.8 %collective-permute-start.4 = (f32[32,128]{1,0:T(8,128)S(1)}, f32[32,128]{1,0:T(8,128)S(1)}, u32[]{:S(2)}, u32[]{:S(2)}) collective-permute-start(f32[32,128]{1,0:T(8,128)S(1)} %convert_reduce_fusion), channel_id=1, source_target_pairs={{0,1},{1,2},{2,3},{3,0},{4,5},{5,6},{6,7},{7,4},{8,9},{9,10},{10,1... | collective-permute-start | bytes 49160 | tf_op jit(solution)/shard_map/ppermute | solution.py:382
  68.8 8.5 %copy-start.6 = (bf16[8,18,384]{2,1,0:T(8,128)(2,1)}, bf16[8,18,384]{2,1,0:T(8,128)(2,1)S(1)}, u32[]{:S(2)}) copy-start(bf16[8,18,384]{2,1,0:T(8,128)(2,1)S(1)} %collective-permute-done.9.diag_in) | copy-start | bytes 331780
  68.8 8.5 %copy-start.2 = (bf16[8,54,384]{2,1,0:T(8,128)(2,1)}, bf16[8,54,384]{2,1,0:T(8,128)(2,1)S(1)}, u32[]{:S(2)}) copy-start(bf16[8,54,384]{2,1,0:T(8,128)(2,1)S(1)} %collective-permute-done.7.lat_in) | copy-start | bytes 995332
  69.6 17.6 %all-to-all-start.1 = ((bf16[32,32,128]{2,1,0:T(8,128)(2,1)}), bf16[32,32,128]{2,1,0:T(8,128)(2,1)S(1)}, u32[]{:S(2)}, u32[]{:S(2)}) async-start(bf16[32,32,128]{2,1,0:T(8,128)(2,1)} %bitcast.12), calls=%async_computation.1 | async-start | bytes 524288 | tf_op jit(solution)/shard_map/all_to_all | solution.py:389
  87.3 5.3 %copy-start = (bf16[32,32,128]{2,1,0:T(8,128)(2,1)}, bf16[32,32,128]{2,1,0:T(8,128)(2,1)S(1)}, u32[]{:S(2)}) copy-start(bf16[32,32,128]{2,1,0:T(8,128)(2,1)S(1)} %all-to-all-done.1) | copy-start | bytes 786436
  87.3 5.3 %collective-permute-start.10 = (bf16[1024,128]{1,0:T(8,128)(2,1)S(1)}, bf16[1024,128]{1,0:T(8,128)(2,1)S(1)}, u32[]{:S(2)}, u32[]{:S(2)}) collective-permute-start(bf16[1024,128]{1,0:T(8,128)(2,1)S(1)} %bitcast.22), channel_id=1, source_target_pairs={{0,64},{64,0},{1,65},{65,1},{2,66},{66,2},{3,67},{67,3},{4,68},{68... | collective-permute-start | bytes 786440 | tf_op jit(solution)/shard_map/ppermute | solution.py:364
  92.6 0.7 copy-start.4

commit v5 on v4

--- a/solution.py
+++ b/solution.py
@@ -33,49 +33,48 @@
 HTILES = 7
 HLANES = HTILES * LANES
 CHUNK = 3 * LANES
-VMEM_LIMIT = 56 * 1024 * 1024
-
-
-def place(rows, cols):
-    return np.zeros((rows, cols), np.float32)
-
-
-def gather_matrices(cols_here):
-    windows = cols_here // WLON
+MIB = 1024 * 1024
+
+
+def one_hot(rows, cols, choose):
+    row = lax.broadcasted_iota(jnp.int32, (rows, cols), 0)
+    col = lax.broadcasted_iota(jnp.int32, (rows, cols), 1)
+    return jnp.where(choose(row) == col, 1.0, 0.0).astype(BF)
+
+
+def window_places(cols_here):
     own_cols = cols_here - SHIFT_LON
-    own = place(windows * WLAT * WLON, WLAT * cols_here)
-    lat = place(windows * WLAT * WLON, SHIFT_LAT * own_cols)
-    corner = place(windows * WLAT * WLON, WLAT * SHIFT_LON)
-    for n in range(windows):
-        for a in range(WLAT):
-            for x in range(WLON):
-                row = (n * WLAT + a) * WLON + x
-                col = n * WLON + x
-                if col < own_cols:
-                    if a < SHIFT_LAT:
-                        own[row, (a + SHIFT_LAT) * cols_here + col + SHIFT_LON] = 1
-                    else:
-                        lat[row, (a - SHIFT_LAT) * own_cols + col] = 1
-                else:
-                    corner[row, a * SHIFT_LON + col - own_cols] = 1
-    return own, lat, corner
-
-
-def scatter_matrices(cols_here):
+    plane = WLAT * cols_here
+    strip = SHIFT_LAT * SHIFT_LON
+
+    def chooser(low_rows, low_cols, first, stride, offset):
+        def choose(row):
+            a = row // WLON % WLAT
+            col = row // (WLAT * WLON) * WLON + row % WLON
+            inside_rows = a < SHIFT_LAT if low_rows else a >= SHIFT_LAT
+            inside_cols = col < own_cols if low_cols else col >= own_cols
+            source = (a + first) * stride + col + offset
+            return jnp.where(jnp.logical_and(inside_rows, inside_cols), source, -1)
+
+        return choose
+
+    return (
+        one_hot(plane, plane, chooser(True, True, SHIFT_LAT, cols_here, SHIFT_LON)),
+        one_hot(plane, SHIFT_LAT * own_cols, chooser(False, True, -SHIFT_LAT, own_cols, 0)),
+        one_hot(plane, strip, chooser(True, False, 0, SHIFT_LON, -own_cols)),
+        one_hot(plane, strip, chooser(False, False, -SHIFT_LAT, SHIFT_LON, -own_cols)),
+    )
+
+
+def strip_places(cols_here):
     own_cols = cols_here - SHIFT_LON
-    lat = place(WLAT * cols_here, SHIFT_LAT * own_cols)
-    corner = place(WLAT * cols_here, WLAT * SHIFT_LON)
-    for a in range(WLAT):
-        for c in range(cols_here):
-            row = a * cols_here + c
-            if c >= SHIFT_LON:
-                if a < SHIFT_LAT:
-                    lat[row, a * own_cols + c - SHIFT_LON] = 1
-            elif a >= SHIFT_LAT:
-                corner[row, (a - SHIFT_LAT) * SHIFT_LON + c] = 1
-            else:
-                corner[row, (a + SHIFT_LAT) * SHIFT_LON + c] = 1
-    return lat, corner
+    plane = WLAT * cols_here
+    strip = SHIFT_LAT * SHIFT_LON
+    return (
+        one_hot(SHIFT_LAT * own_cols, plane, lambda i: i // own_cols * cols_here + SHIFT_LON + i % own_cols),
+        one_hot(strip, plane, lambda i: (i // SHIFT_LON + SHIFT_LAT) * cols_here + i % SHIFT_LON),
+        one_hot(strip, plane, lambda i: i // SHIFT_LON * cols_here + i % SHIFT_LON),
+    )
 
 
 def lon_selectors():
@@ -96,15 +95,18 @@
     return high, (value - high.astype(F32)).astype(BF)
 
 
-def prep_kernel(wx_ref, gx_ref, lat_pick, lon_pick, diag_pick, lat_out, lon_out, diag_out):
-    def step(level, carry):
-        for pick, strip in ((lat_pick, lat_out), (lon_pick, lon_out), (diag_pick, diag_out)):
-            strip[level] = jnp.concatenate(
-                [dot(pick[...], ref[level]) for ref in (wx_ref, gx_ref)], axis=1
-            ).astype(BF)
-        return carry
-
-    lax.fori_loop(0, wx_ref.shape[0], step, 0, unroll=True)
+def prep_kernel(wx_far, gx_far, lat_out, lon_out, diag_out, wx_ref, gx_ref, sems):
+    copies = [
+        pltpu.make_async_copy(far, near, sems.at[i]) for i, (far, near) in enumerate(((wx_far, wx_ref), (gx_far, gx_ref)))
+    ]
+    for copy in copies:
+        copy.start()
+    picks = strip_places(wx_ref.shape[1] // WLAT)
+    for copy in copies:
+        copy.wait()
+    for level in range(wx_ref.shape[0]):
+        for pick, strip in zip(picks, (lat_out, lon_out, diag_out)):
+            strip[level] = jnp.concatenate([dot(pick, ref[level]) for ref in (wx_ref, gx_ref)], axis=1).astype(BF)
 
 
 def expand_kernel(last_ref, table_ref, sel_ref, bias_ref, flat_s, block_s, table_s):
@@ -145,7 +147,7 @@
 
 def main_kernel(
     core_ref, wx_ref, gx_ref, lat_in, lon_in, diag_in, gain_ref, wqkv_ref, proj_ref,
-    pown_ref, plat_ref, plon_ref, pdiag_ref, bias_hbm, sel_hbm,
+    bias_hbm, sel_hbm,
     att_ref, gi_ref, keep_ref, send_ref,
     x_s, g_s, normed_s, inv_s, q_s, k_s, v_s, da_s, dq_s, dk_s, dv_s, hid_t, dsum_s, pay_s, bias_s, sel_s, sems,
 ):
@@ -156,17 +158,16 @@
     levels = wx_ref.shape[0]
     half = TOK // 2
     windows = x_s.shape[0] // TOK
+    place_own, *places = window_places(wx_ref.shape[1] // WLAT)
     for level in range(levels):
         back = (level + levels - 1) % levels
         k, z = back // WLEV, back % WLEV
-        place_own = pown_ref[...]
-        strips = ((plat_ref, lat_in), (plon_ref, lon_in), (pdiag_ref, diag_in))
         xw = dot(place_own, wx_ref[level])
         gw = dot(place_own, gx_ref[level])
-        for where_ref, strip in strips:
+        for place, strip in zip(places, (lat_in, lon_in, diag_in)):
             both = strip[level]
-            xw = xw + dot(where_ref[...], both[:, :CH])
-            gw = gw + dot(where_ref[...], both[:, CH:])
+            xw = xw + dot(place, both[:, :CH])
+            gw = gw + dot(place, both[:, CH:])
         for n in range(2):
             at = (2 * k + n) * TOK + z * half
             x_s[at : at + half, :] = xw[n * half : (n + 1) * half]
@@ -282,11 +283,12 @@
 
 
 def return_kernel(
-    wx_ref, gx_ref, att_ref, gi_ref, proj_ref, pown_ref, plat_ref, plon_ref, pdiag_ref,
+    wx_ref, gx_ref, att_ref, gi_ref, proj_ref,
     base_ref, gbase_ref, lat_out, lon_out, diag_out, br_s, gi_s,
 ):
     br_s[...] = dot(att_ref[...], proj_ref[...])
     gi_s[...] = gi_ref[...].astype(F32)
+    place_own, *places = window_places(wx_ref.shape[1] // WLAT)
     levels = wx_ref.shape[0]
     half = TOK // 2
     for level in range(levels):
@@ -296,22 +298,23 @@
         for src, own_in, own_out in ((br_s, wx_ref, base_ref), (gi_s, gx_ref, gbase_ref)):
             starts = [(2 * k + n) * TOK + z * half for n in range(2)]
             rows = jnp.concatenate([src[at : at + half, :] for at in starts], axis=0).astype(BF)
-            own_out[level] = (own_in[level].astype(F32) + dot(pown_ref[...], rows, 0, 0)).astype(BF)
+            own_out[level] = (own_in[level].astype(F32) + dot(place_own, rows, 0, 0)).astype(BF)
             moved.append(rows)
-        for where_ref, strip in ((plat_ref, lat_out), (plon_ref, lon_out), (pdiag_ref, diag_out)):
+        for place, strip in zip(places, (lat_out, lon_out, diag_out)):
             strip[level] = jnp.concatenate(
-                [dot(where_ref[...], rows, 0, 0) for rows in moved], axis=1
+                [dot(place, rows, 0, 0) for rows in moved], axis=1
             ).astype(BF)
 
 
-def add_kernel(base_ref, gbase_ref, lat_in, lon_in, diag_in, slat_ref, slon_ref, sdiag_ref, out_ref, gout_ref):
+def add_kernel(base_ref, gbase_ref, lat_in, lon_in, diag_in, out_ref, gout_ref):
+    picks = strip_places(base_ref.shape[1] // WLAT)
     for level in range(base_ref.shape[0]):
         up = base_ref[level].astype(F32)
         gup = gbase_ref[level].astype(F32)
-        for where_ref, strip in ((slat_ref, lat_in), (slon_ref, lon_in), (sdiag_ref, diag_in)):
+        for pick, strip in zip(picks, (lat_in, lon_in, diag_in)):
             both = strip[level]
-            up = up + dot(where_ref[...], both[:, :CH])
-            gup = gup + dot(where_ref[...], both[:, CH:])
+            up = up + dot(pick, both[:, :CH], 0, 0)
+            gup = gup + dot(pick, both[:, CH:], 0, 0)
         out_ref[level] = up.astype(BF)
         gout_ref[level] = gup.astype(BF)
 
@@ -391,7 +394,7 @@
     return mine, swapped(mine), outs
 
 
-def call(kernel, out_shape, scratch=(), smem=0, count=0, flops=0, far=0):
+def call(kernel, out_shape, scratch=(), smem=0, count=0, flops=0, far=0, room=12):
     specs = [pl.BlockSpec(memory_space=pltpu.SMEM)] * smem
     specs += [pl.BlockSpec(memory_space=pltpu.VMEM)] * (count - smem - far)
     specs += [pl.BlockSpec(memory_space=pl.ANY)] * far
@@ -401,7 +404,7 @@
         in_specs=specs,
         out_specs=jax.tree.map(lambda _: pl.BlockSpec(memory_space=pltpu.VMEM), out_shape),
         scratch_shapes=list(scratch),
-        compiler_params=pltpu.CompilerParams(vmem_limit_bytes=VMEM_LIMIT),
+        compiler_params=pltpu.CompilerParams(vmem_limit_bytes=room * MIB),
         cost_estimate=pl.CostEstimate(flops=flops, bytes_accessed=flops // 500, transcendentals=0),
     )
 
@@ -421,11 +424,11 @@
     edge = SHIFT_LAT * SHIFT_LON
     lat_shape = sds((levels, SHIFT_LAT * own_cols, 2 * CH), BF)
     edge_shape = sds((levels, edge, 2 * CH), BF)
-    slat, scor = scatter_matrices(cols_here)
-    scatter = (slat, scor[:, :edge], scor[:, edge:])
-    strips = call(prep_kernel, (lat_shape, edge_shape, edge_shape), count=5, flops=10**9)(
-        wx, gx, *[jnp.asarray(m.T, BF) for m in scatter]
-    )
+    near = [pltpu.VMEM((levels, plane, CH), BF)] * 2
+    strips = call(
+        prep_kernel, (lat_shape, edge_shape, edge_shape), scratch=near + [pltpu.SemaphoreType.DMA((2,))],
+        count=2, far=2, flops=10**9,
+    )(*[pltpu.with_memory_space_constraint(v, pltpu.HBM) for v in (wx, gx)])
     lat_in = passed(strips[0], -1, 0)
     lon_in = passed(strips[1], 0, -1)
     diag_in = passed(strips[2], -1, -1)
@@ -446,8 +449,6 @@
         smem=1, count=3, flops=10**9,
     )(last, table, sel)
 
-    own_m, lat_m, corner_m = gather_matrices(cols_here)
-    mats = [jnp.asarray(m, BF) for m in (own_m, lat_m, corner_m[:, :edge], corner_m[:, edge:])]
     wqkv = qkv_weight.reshape(CH, 3, CH).transpose(1, 0, 2)
     tokens = levels * plane
     plane_shape = sds((levels, plane, CH), BF)
@@ -470,25 +471,25 @@
             pltpu.SemaphoreType.DMA((2,)),
         ],
         smem=1,
-        count=15,
+        count=11,
         far=2,
         flops=10**10,
-    )(core, wx, gx, lat_in, lon_in, diag_in, norm_gain.reshape(1, CH), wqkv, proj_weight, *mats, bias, sel)
+        room=28,
+    )(core, wx, gx, lat_in, lon_in, diag_in, norm_gain.reshape(1, CH), wqkv, proj_weight, bias, sel)
 
     def give_back(inputs):
         base, gbase, *strips = call(
             return_kernel,
             (plane_shape, plane_shape, lat_shape, edge_shape, edge_shape),
             scratch=[wide_f, wide_f],
-            count=9,
+            count=5,
             flops=2 * 10**9,
-        )(wx, gx, *inputs, proj_weight, *mats)
+            room=56,
+        )(wx, gx, *inputs, proj_weight)
         return (base, gbase), strips
 
     def add_up(*parts):
-        return call(add_kernel, (plane_shape, plane_shape), count=8, flops=2 * 10**9)(
-            *parts, *[jnp.asarray(m, BF) for m in scatter]
-        )
+        return call(add_kernel, (plane_shape, plane_shape), count=5, flops=2 * 10**9)(*parts)
 
     mine, other, (out, gout) = total_over_devices(keep, send, ((att, gi), give_back), add_up)
     factor = (samples * levels * rows_here * cols_here * lax.axis_size(("ylo", "core", "yhi", "z", "lat"))) ** (-0.5)

time: 96.4 us -> 92.4 us (0.959)
  Pallas kernels: 33.4 us -> 26.7 us
  local copies, waits for them, and re-layouts: 3.36 us -> 5.72 us
  starting transfers between devices: 38.8 us -> 40.8 us
    pallas_call x1, Pallas kernels: 5.93 us -> 2.81 us  [shards(): call(expand_kernel, sds(bias_shape, F32), scratch=[flat_shape, pltpu.VMEM...]
    all_to_all x1, starting transfers between devices: 5.37 us -> 7.65 us  [total_over_devices(): pieces = lax.all_to_all(half, wide, 0, 0, tiled=True)]
    unnamed x19 -> x23, local copies, waits for them, and re-layouts: 1.66 us -> 3.85 us
    pallas_call x2, Pallas kernels: 6.28 us -> 5.02 us  [the longest x1 2.88 us: shards(): call(prep_kernel, (lat_shape, edge_shape, edge_shape), scratch=near + [pl...]
    pallas_call x1, Pallas kernels: 14.3 us -> 13.2 us  [shards(): call(main_kernel, (token_shape, token_shape, half_shape, half_shape), scr...]
    pallas_call x1, Pallas kernels: 2.63 us -> 1.61 us  [shards(): call(functools.partial(finish_kernel, factor), (sds(qkv_weight.shape, F32...]
  transfers between devices with their start and end apart: 13 -> 13, of which waited for: 6 -> 6; matrix products, arithmetic and copies ran while one was open for 1% -> 2% of each run, Pallas kernels for 14% -> 10%
where the time goes in v5:
time: 92.4 us; the launch traced here: 92 us
  starting transfers between devices  40.8 us (44%)
  Pallas kernels  26.7 us (29%)
  waiting for transfers between devices  17 us (18%)
  local copies, waits for them, and re-layouts  5.72 us (6%)
    ppermute x6, starting transfers between devices, passed(): return lax.ppermute(value, ('yhi', 'z', 'lat'), pairs)  16.3 us
    pallas_call x1, Pallas kernels, shards(): call(main_kernel, (token_shape, token_shape, half_shape, half_shape), scr...  13.2 us
    all_to_all x1, starting transfers between devices, total_over_devices(): pieces = lax.all_to_all(half, wide, 0, 0, tiled=True)  7.65 us
    all_to_all x1, starting transfers between devices, total_over_devices(): mine = lax.all_to_all(spread, wide, 0, 0, tiled=True)  7.6 us
    ppermute x6, waiting for transfers between devices, passed(): return lax.ppermute(value, ('yhi', 'z', 'lat'), pairs)  6.47 us
    ppermute x2, starting transfers between devices, swapped(): return lax.ppermute(value, 'core', [(0, 1), (1, 0)])  5.83 us
    all_to_all x1, waiting for transfers between devices, total_over_devices(): mine = lax.all_to_all(spread, wide, 0, 0, tiled=True)  5.73 us
    pallas_call x1, Pallas kernels, give_back(): call(return_kernel, (plane_shape, plane_shape, lat_shape, edge_shape, edg...  4.07 us
  transfers between devices with their start and end apart: 13, of which 6 were waited for; matrix products, arithmetic and copies ran while one was open for 2% of the time, Pallas kernels for 10%

profile of v5, /device:TPU:1, one launch (start us, length us, event | category | flops | bytes accessed | tf_op | source)
XLA Modules:
  0.0 92.0 jit_solution(15644558393917113531)
XLA Ops:
  0.6 0.0 copy-start.10
  0.6 0.0 copy-start
  0.7 0.0 copy-start.1
  0.7 2.9 %shard_map.118 = (bf16[8,54,384]{2,1,0:T(8,128)(2,1)}, bf16[8,18,384]{2,1,0:T(8,128)(2,1)}, bf16[8,18,384]{2,1,0:T(8,128)(2,1)}) custom-call(bf16[8,144,192]{2,1,0:T(8,128)(2,1)} %bitcast.23, bf16[8,144,192]{2,1,0:T(8,128)(2,1)} %bitcast.26), custom_call_target="tpu_custom_call" | custom-call | flops 1000000000 | bytes 2000000 | tf_op jit(solution)/shard_map/pallas_call | solution.py:428
  3.6 3.4 %collective-permute-start = (bf16[8,54,384]{2,1,0:T(8,128)(2,1)}, bf16[8,54,384]{2,1,0:T(8,128)(2,1)S(1)}, u32[]{:S(2)}, u32[]{:S(2)}) collective-permute-start(bf16[8,54,384]{2,1,0:T(8,128)(2,1)} %get-tuple-element.41), channel_id=1, source_target_pairs={{0,3},{1,0},{2,1},{3,2},{4,7},{5,4},{6,5},{7,6},{8,11},{9,8},{10,9... | collective-permute-start | bytes 995336 | tf_op jit(solution)/shard_map/ppermute | solution.py:363
  6.9 8.2 %collective-permute-start.1 = (bf16[8,18,384]{2,1,0:T(8,128)(2,1)}, bf16[8,18,384]{2,1,0:T(8,128)(2,1)S(1)}, u32[]{:S(2)}, u32[]{:S(2)}) collective-permute-start(bf16[8,18,384]{2,1,0:T(8,128)(2,1)} %get-tuple-element.42), channel_id=1, source_target_pairs={{0,60},{1,61},{2,62},{3,63},{4,0},{5,1},{6,2},{7,3},{8,4},{9,5},{1... | collective-permute-start | bytes 331784 | tf_op jit(solution)/shard_map/ppermute | solution.py:363
  15.1 1.0 %collective-permute-start.2 = (bf16[8,18,384]{2,1,0:T(8,128)(2,1)}, bf16[8,18,384]{2,1,0:T(8,128)(2,1)}, u32[]{:S(2)}, u32[]{:S(2)}) collective-permute-start(bf16[8,18,384]{2,1,0:T(8,128)(2,1)} %get-tuple-element.43), channel_id=1, source_target_pairs={{0,63},{1,60},{2,61},{3,62},{4,3},{5,0},{6,1},{7,2},{8,7},{9,4},{1... | collective-permute-start | bytes 331784 | tf_op jit(solution)/shard_map/ppermute | solution.py:363
  16.1 0.0 copy-done.10
  16.1 0.9 copy.13
  17.0 1.1 %copy.14 = bf16[192,3,192]{2,0,1:T(8,128)(2,1)S(1)} copy(bf16[192,3,192]{0,2,1:T(8,128)(2,1)} %bitcast.30) | data formatting | bytes 442368 | tf_op jit(solution)/shard_map/reshape | solution.py:452
  18.2 0.0 copy-start.2
  18.2 0.0 copy-start.3
  18.2 0.0 copy-start.4
  18.2 0.0 copy-start.5
  18.2 2.8 %shard_map.119.bias_hbm = f32[7,576,128]{2,1,0:T(8,128)S(1)} custom-call(s32[1]{0:T(128)} %bitcast.6.last_ref, f32[24,1,3312]{2,1,0:T(1,128)S(1)} %bitcast.19, bf16[12,384,256]{2,1,0:T(8,128)(2,1)S(1)} %copy-done), custom_call_target="tpu_custom_call" | custom-call | flops 1000000000 | bytes 2000000 | tf_op jit(solution)/shard_map/pallas_call | solution.py:445
  21.0 0.0 collective-permute-done.1.lon_in
  21.1 0.0 collective-permute-done.2.diag_in
  21.1 0.0 collective-permute-done.lat_in
  21.1 13.2 %shard_map.120 = (bf16[1152,192]{1,0:T(8,128)(2,1)S(1)}, bf16[1152,192]{1,0:T(8,128)(2,1)S(1)}, bf16[1024,128]{1,0:T(8,128)(2,1)S(1)}, bf16[1024,128]{1,0:T(8,128)(2,1)S(1)}) custom-call(s32[1]{0:T(128)} %bitcast.core_ref, bf16[8,144,192]{2,1,0:T(8,128)(2,1)S(1)} %bitcast.25, bf16[8,144,192]{2,1,0:T(8,128)(2,1)S(1)} %bitcast.28, ...), custom_call_target="tpu_custom_call" | custom-call | flops 10000000000 | bytes 20000000 | tf_op jit(solution)/shard_map/pallas_call | solution.py:460
  34.4 0.0 copy-start.9
  34.4 0.8 copy-done.9
  35.2 1.7 %collective-permute-start.3 = (bf16[1024,128]{1,0:T(8,128)(2,1)S(1)}, bf16[1024,128]{1,0:T(8,128)(2,1)S(1)}, u32[]{:S(2)}, u32[]{:S(2)}) collective-permute-start(bf16[1024,128]{1,0:T(8,128)(2,1)S(1)} %get-tuple-element.45), channel_id=1, source_target_pairs={{0,64},{64,0},{1,65},{65,1},{2,66},{66,2},{3,67},{67,3},{4,68},{68... | collective-permute-start | bytes 786440 | tf_op jit(solution)/shard_map/ppermute | solution.py:367
  36.8 1.2 %collective-permute-done.3 = bf16[1024,128]{1,0:T(8,128)(2,1)S(1)} collective-permute-done((bf16[1024,128]{1,0:T(8,128)(2,1)S(1)}, bf16[1024,128]{1,0:T(8,128)(2,1)S(1)}, u32[]{:S(2)}, u32[]{:S(2)}) %collective-permute-start.3) | collective-permute-done | bytes 262176 | tf_op jit(solution)/shard_map/ppermute | solution.py:367
  38.0 0.8 add_convert_fusion
  38.8 7.6 %all-to-all-start = ((bf16[32,32,128]{2,1,0:T(8,128)(2,1)}), bf16[32,32,128]{2,1,0:T(8,128)(2,1)S(1)}, u32[]{:S(2)}, u32[]{:S(2)}) async-start(bf16[32,32,128]{2,1,0:T(8,128)(2,1)} %bitcast.8), calls=%async_computation | async-start | bytes 524288 | tf_op jit(solution)/shard_map/all_to_all | solution.py:376
  46.4 4.1 %shard_map.121 = (bf16[8,144,192]{2,1,0:T(8,128)(2,1)}, bf16[8,144,192]{2,1,0:T(8,128)(2,1)}, bf16[8,54,384]{2,1,0:T(8,128)(2,1)}, bf16[8,18,384]{2,1,0:T(8,128)(2,1)}, bf16[8,18,384]{2,1,0:T(8,128)(2,1)}) custom-call(bf16[8,144,192]{2,1,0:T(8,128)(2,1)} %bitcast.24, bf16[8,144,192]{2,1,0:T(8,128)(2,1)} %bitcast.27, bf16[1152,192]{1,0:T(8,128)(2,1)} %copy-done.8, ...), custom_call_target="tpu_custom_call" | custom-call | flops 2000000000 | bytes 4000000 | tf_op jit(solution)/shard_map/pallas_call | solution.py:481
  50.5 0.5 collective-permute-start.7
  51.0 1.0 %collective-permute-start.8 = (bf16[8,18,384]{2,1,0:T(8,128)(2,1)}, bf16[8,18,384]{2,1,0:T(8,128)(2,1)S(1)}, u32[]{:S(2)}, u32[]{:S(2)}) collective-permute-start(bf16[8,18,384]{2,1,0:T(8,128)(2,1)} %get-tuple-element.52), channel_id=1, source_target_pairs={{0,4},{1,5},{2,6},{3,7},{4,8},{5,9},{6,10},{7,11},{8,12},{9,13},{1... | collective-permute-start | bytes 331784 | tf_op jit(solution)/shard_map/ppermute | solution.py:363
  52.1 2.1 %collective-permute-start.9 = (bf16[8,18,384]{2,1,0:T(8,128)(2,1)}, bf16[8,18,384]{2,1,0:T(8,128)(2,1)S(1)}, u32[]{:S(2)}, u32[]{:S(2)}) collective-permute-start(bf16[8,18,384]{2,1,0:T(8,128)(2,1)} %get-tuple-element.53), channel_id=1, source_target_pairs={{0,5},{1,6},{2,7},{3,4},{4,9},{5,10},{6,11},{7,8},{8,13},{9,14},{1... | collective-permute-start | bytes 331784 | tf_op jit(solution)/shard_map/ppermute | solution.py:363
  54.2 2.5 %all-to-all-done = bf16[32,32,128]{2,1,0:T(8,128)(2,1)S(1)} async-done(((bf16[32,32,128]{2,1,0:T(8,128)(2,1)}), bf16[32,32,128]{2,1,0:T(8,128)(2,1)S(1)}, u32[]{:S(2)}, u32[]{:S(2)}) %all-to-all-start) | async-done | bytes 262176 | tf_op jit(solution)/shard_map/all_to_all | solution.py:376
  56.7 3.1 %collective-permute-start.6 = (f32[32,128]{1,0:T(8,128)S(1)}, f32[32,128]{1,0:T(8,128)S(1)}, u32[]{:S(2)}, u32[]{:S(2)}) collective-permute-start(f32[32,128]{1,0:T(8,128)S(1)} %convert_reduce_fusion), channel_id=1, source_target_pairs={{0,3},{1,0},{2,1},{3,2},{4,7},{5,4},{6,5},{7,6},{8,11},{9,8},{10,9... | collective-permute-start | bytes 49160 | tf_op jit(solution)/shard_map/ppermute | solution.py:385
  59.8 0.0 collective-permute-start.5
  59.9 1.2 %collective-permute-done.8.lon_in = bf16[8,18,384]{2,1,0:T(8,128)(2,1)S(1)} collective-permute-done((bf16[8,18,384]{2,1,0:T(8,128)(2,1)}, bf16[8,18,384]{2,1,0:T(8,128)(2,1)S(1)}, u32[]{:S(2)}, u32[]{:S(2)}) %collective-permute-start.8) | collective-permute-done | bytes 110624 | tf_op jit(solution)/shard_map/ppermute | solution.py:363
  61.0 0.4 collective-permute-start.4
  61.4 5.3 %collective-permute-done.9.diag_in = bf16[8,18,384]{2,1,0:T(8,128)(2,1)S(1)} collective-permute-done((bf16[8,18,384]{2,1,0:T(8,128)(2,1)}, bf16[8,18,384]{2,1,0:T(8,128)(2,1)S(1)}, u32[]{:S(2)}, u32[]{:S(2)}) %collective-permute-start.9) | collective-permute-done | bytes 110624 | tf_op jit(solution)/shard_map/ppermute | solution.py:363
  66.7 0.0 collective-permute-done.7.lat_in
  66.7 0.0 collective-permute-done.6
  66.7 0.0 collective-permute-done.5
  66.7 0.0 collective-permute-done.4
  66.7 0.7 broadcast_in_dim.2
  67.5 7.6 %all-to-all-start.1 = ((bf16[32,32,128]{2,1,0:T(8,128)(2,1)}), bf16[32,32,128]{2,1,0:T(8,128)(2,1)S(1)}, u32[]{:S(2)}, u32[]{:S(2)}) async-start(bf16[32,32,128]{2,1,0:T(8,128)(2,1)} %bitcast.12), calls=%async_computation.1 | async-start | bytes 524288 | tf_op jit(solution)/shard_map/all_to_all | solution.py:392
  75.1 1.1 %copy-done.6 = bf16[8,144,192]{2,1,0:T(8,128)(2,1)S(1)} copy-done((bf16[8,144,192]{2,1,0:T(8,128)(2,1)S(1)}, bf16[8,144,192]{2,1,0:T(8,128)(2,1)}, u32[]{:S(2)}) %copy-start.6) | copy-done | bytes 442392
  76.1 1.1 %copy-done.7 = bf16[8,144,192]{2,1,0:T(8,128)(2,1)S(1)} copy-done((bf16[8,144,192]{2,1,0:T(8,128)(2,1)S(1)}, bf16[8,144,192]{2,1,0:T(8,128)(2,1)}, u32[]{:S(2)}) %copy-start.7) | copy-done | bytes 442392
  77.2 2.1 %shard_map.122 = (bf16[8,144,192]{2,1,0:T(8,128)(2,1)}, bf16[8,144,192]{2,1,0:T(8,128)(2,1)}) custom-call(bf16[8,144,192]{2,1,0:T(8,128)(2,1)S(1)} %copy-done.6, bf16[8,144,192]{2,1,0:T(8,128)(2,1)S(1)} %copy-done.7, bf16[8,54,384]{2,1,0:T(8,128)(2,1)S(1)} %collective-permute-done.7.lat_in, bf16[8,18,384]{2,1,0:T(8,128)(2,1)S(1)} %collective-permute-done.8.lon_in, ...), custom_call_target="tpu_custom_call" | custom-call | flops 2000000000 | bytes 4000000 | tf_op jit(solution)/shard_map/pallas_call | solution.py:492
  79.3 5.7 %all-to-all-done.1 = bf16[32,32,128]{2,1,0:T(8,128)(2,1)S(1)} async-done(((bf16[32,32,128]{2,1,0:T(8,128)(2,1)}), bf16[32,32,128]{2,1,0:T(8,128)(2,1)S(1)}, u32[]{:S(2)}, u32[]{:S(2)}) %all-to-all-start.1) | async-done | bytes 262176 | tf_op jit(solution)/shard_map/all_to_all | solution.py:392
  85.1 4.2 %collective-permute-start.10 = (bf16[1024,128]{1,0:T(8,128)(2,1)S(1)}, bf16[1024,128]{1,0:T(8,128)(2,1)S(1)}, u32[]{:S(2)}, u32[]{:S(2)}) collective-permute-start(bf16[1024,128]{1,0:T(8,128)(2,1)S(1)} %bitcast.21), channel_id=1, source_target_pairs={{0,64},{64,0},{1,65},{65,1},{2,66},{66,2},{3,67},{67,3},{4,68},{68... | collective-permute-start | bytes 786440 | tf_op jit(solution)/shard_map/ppermute | solution.py:367
  89.2 1.2 %collective-permute-done.10.other_ref = bf16[1024,128]{1,0:T(8,128)(2,1)S(1)} collective-permute-done((bf16[1024,128]{1,0:T(8,128)(2,1)S(1)}, bf16[1024,128]{1,0:T(8,128)(2,1)S(1)}, u32[]{:S(2)}, u32[]{:S(2)}) %collective-permute-start.10) | collective-permute-done | bytes 262176 | tf_op jit(solution)/shard_map/ppermute | solution.py:367
  90.4 1.6 %shard_map.123 = (f32[192,576]{1,0:T(8,128)}, f32[192,192]{1,0:T(8,128)}, f32[1,192]{1,0:T(1,128)}, f32[24,1,3312]{2,1,0:T(1,128)}) custom-call(s32[1]{0:T(128)} %bitcast.core_ref, bf16[1024,128]{1,0:T(8,128)(2,1)S(1)} %bitcast.22, bf16[1024,128]{1,0:T(8,128)(2,1)S(1)} %collective-permute-done.10.other_ref), custom_call_target="tpu_custom_call" | custom-call | flops 1000000000 | bytes 2000000 | tf_op jit(solution)/shard_map/pallas_call | solution.py:496
  (12 shorter events, 0.1 us)
Async XLA Ops:
  0.6 15.5 %copy-start.10 = (bf16[192,576]{1,0:T(8,128)(2,1)S(1)}, bf16[192,576]{1,0:T(8,128)(2,1)}, u32[]{:S(2)}) copy-start(bf16[192,576]{1,0:T(8,128)(2,1)} %param.10) | copy-start | bytes 663556
  0.6 17.5 %copy-start = (bf16[12,384,256]{2,1,0:T(8,128)(2,1)S(1)}, bf16[12,384,256]{2,1,0:T(8,128)(2,1)}, u32[]{:S(2)}) copy-start(bf16[12,384,256]{2,1,0:T(8,128)(2,1)} %constant.38.clone.sel_ref.sel_hbm) | copy-start | bytes 7077892
  0.7 17.5 %copy-start.1 = (f32[4,1,6,3312]{3,1,2,0:T(1,128)S(1)}, f32[4,1,6,3312]{3,1,2,0:T(1,128)}, u32[]{:S(2)}) copy-start(f32[4,1,6,3312]{3,1,2,0:T(1,128)} %param.12) | copy-start | bytes 953860
  3.6 17.5 %collective-permute-start = (bf16[8,54,384]{2,1,0:T(8,128)(2,1)}, bf16[8,54,384]{2,1,0:T(8,128)(2,1)S(1)}, u32[]{:S(2)}, u32[]{:S(2)}) collective-permute-start(bf16[8,54,384]{2,1,0:T(8,128)(2,1)} %get-tuple-element.41), channel_id=1, source_target_pairs={{0,3},{1,0},{2,1},{3,2},{4,7},{5,4},{6,5},{7,6},{8,11},{9,8},{10,9... | collective-permute-start | bytes 995336 | tf_op jit(solution)/shard_map/ppermute | solution.py:363
  6.9 14.1 %collective-permute-start.1 = (bf16[8,18,384]{2,1,0:T(8,128)(2,1)}, bf16[8,18,384]{2,1,0:T(8,128)(2,1)S(1)}, u32[]{:S(2)}, u32[]{:S(2)}) collective-permute-start(bf16[8,18,384]{2,1,0:T(8,128)(2,1)} %get-tuple-element.42), channel_id=1, source_target_pairs={{0,60},{1,61},{2,62},{3,63},{4,0},{5,1},{6,2},{7,3},{8,4},{9,5},{1... | collective-permute-start | bytes 331784 | tf_op jit(solution)/shard_map/ppermute | solution.py:363
  15.1 5.9 %collective-permute-start.2 = (bf16[8,18,384]{2,1,0:T(8,128)(2,1)}, bf16[8,18,384]{2,1,0:T(8,128)(2,1)}, u32[]{:S(2)}, u32[]{:S(2)}) collective-permute-start(bf16[8,18,384]{2,1,0:T(8,128)(2,1)} %get-tuple-element.43), channel_id=1, source_target_pairs={{0,63},{1,60},{2,61},{3,62},{4,3},{5,0},{6,1},{7,2},{8,7},{9,4},{1... | collective-permute-start | bytes 331784 | tf_op jit(solution)/shard_map/ppermute | solution.py:363
  18.2 2.9 %copy-start.2 = (bf16[1,8,6,24,192]{4,3,2,1,0:T(8,128)(2,1)S(1)}, bf16[1,8,6,24,192]{4,3,2,1,0:T(8,128)(2,1)}, u32[]{:S(2)}) copy-start(bf16[1,8,6,24,192]{4,3,2,1,0:T(8,128)(2,1)} %param.7) | copy-start | bytes 1327108
  18.2 2.9 %copy-start.3 = (bf16[1,8,6,24,192]{4,3,2,1,0:T(8,128)(2,1)S(1)}, bf16[1,8,6,24,192]{4,3,2,1,0:T(8,128)(2,1)}, u32[]{:S(2)}) copy-start(bf16[1,8,6,24,192]{4,3,2,1,0:T(8,128)(2,1)} %param.8) | copy-start | bytes 1327108
  18.2 2.9 %copy-start.4 = (bf16[192,192]{1,0:T(8,128)(2,1)S(1)}, bf16[192,192]{1,0:T(8,128)(2,1)}, u32[]{:S(2)}) copy-start(bf16[192,192]{1,0:T(8,128)(2,1)} %proj_ref.3) | copy-start | bytes 221188
  18.2 2.9 %copy-start.5 = (f32[192]{0:T(256)S(1)}, f32[192]{0:T(256)}, u32[]{:S(2)}) copy-start(f32[192]{0:T(256)} %param.9) | copy-start | bytes 2308
  34.4 0.8 copy-start.9
  35.2 3.6 %copy-start.8 = (bf16[1152,192]{1,0:T(8,128)(2,1)}, bf16[1152,192]{1,0:T(8,128)(2,1)S(1)}, u32[]{:S(2)}) copy-start(bf16[1152,192]{1,0:T(8,128)(2,1)S(1)} %get-tuple-element.49.att_ref) | copy-start | bytes 1327108
  35.2 2.8 %collective-permute-start.3 = (bf16[1024,128]{1,0:T(8,128)(2,1)S(1)}, bf16[1024,128]{1,0:T(8,128)(2,1)S(1)}, u32[]{:S(2)}, u32[]{:S(2)}) collective-permute-start(bf16[1024,128]{1,0:T(8,128)(2,1)S(1)} %get-tuple-element.45), channel_id=1, source_target_pairs={{0,64},{64,0},{1,65},{65,1},{2,66},{66,2},{3,67},{67,3},{4,68},{68... | collective-permute-start | bytes 786440 | tf_op jit(solution)/shard_map/ppermute | solution.py:367
  38.8 17.9 %all-to-all-start = ((bf16[32,32,128]{2,1,0:T(8,128)(2,1)}), bf16[32,32,128]{2,1,0:T(8,128)(2,1)S(1)}, u32[]{:S(2)}, u32[]{:S(2)}) async-start(bf16[32,32,128]{2,1,0:T(8,128)(2,1)} %bitcast.8), calls=%async_computation | async-start | bytes 524288 | tf_op jit(solution)/shard_map/all_to_all | solution.py:376
  50.5 16.2 %collective-permute-start.7 = (bf16[8,54,384]{2,1,0:T(8,128)(2,1)}, bf16[8,54,384]{2,1,0:T(8,128)(2,1)S(1)}, u32[]{:S(2)}, u32[]{:S(2)}) collective-permute-start(bf16[8,54,384]{2,1,0:T(8,128)(2,1)} %get-tuple-element.51), channel_id=1, source_target_pairs={{0,1},{1,2},{2,3},{3,0},{4,5},{5,6},{6,7},{7,4},{8,9},{9,10},{10,1... | collective-permute-start | bytes 995336 | tf_op jit(solution)/shard_map/ppermute | solution.py:363
  51.0 10.0 %collective-permute-start.8 = (bf16[8,18,384]{2,1,0:T(8,128)(2,1)}, bf16[8,18,384]{2,1,0:T(8,128)(2,1)S(1)}, u32[]{:S(2)}, u32[]{:S(2)}) collective-permute-start(bf16[8,18,384]{2,1,0:T(8,128)(2,1)} %get-tuple-element.52), channel_id=1, source_target_pairs={{0,4},{1,5},{2,6},{3,7},{4,8},{5,9},{6,10},{7,11},{8,12},{9,13},{1... | collective-permute-start | bytes 331784 | tf_op jit(solution)/shard_map/ppermute | solution.py:363
  52.1 14.6 %collective-permute-start.9 = (bf16[8,18,384]{2,1,0:T(8,128)(2,1)}, bf16[8,18,384]{2,1,0:T(8,128)(2,1)S(1)}, u32[]{:S(2)}, u32[]{:S(2)}) collective-permute-start(bf16[8,18,384]{2,1,0:T(8,128)(2,1)} %get-tuple-element.53), channel_id=1, source_target_pairs={{0,5},{1,6},{2,7},{3,4},{4,9},{5,10},{6,11},{7,8},{8,13},{9,14},{1... | collective-permute-start | bytes 331784 | tf_op jit(solution)/shard_map/ppermute | solution.py:363
  56.7 9.9 %collective-permute-start.6 = (f32[32,128]{1,0:T(8,128)S(1)}, f32[32,128]{1,0:T(8,128)S(1)}, u32[]{:S(2)}, u32[]{:S(2)}) collective-permute-start(f32[32,128]{1,0:T(8,128)S(1)} %convert_reduce_fusion), channel_id=1, source_target_pairs={{0,3},{1,0},{2,1},{3,2},{4,7},{5,4},{6,5},{7,6},{8,11},{9,8},{10,9... | collective-permute-start | bytes 49160 | tf_op jit(solution)/shard_map/ppermute | solution.py:385
  59.8 6.8 %collective-permute-start.5 = (f32[32,128]{1,0:T(8,128)S(1)}, f32[32,128]{1,0:T(8,128)S(1)}, u32[]{:S(2)}, u32[]{:S(2)}) collective-permute-start(f32[32,128]{1,0:T(8,128)S(1)} %convert_reduce_fusion), channel_id=1, source_target_pairs={{0,2},{1,3},{2,0},{3,1},{4,6},{5,7},{6,4},{7,5},{8,10},{9,11},{10,... | collective-permute-start | bytes 49160 | tf_op jit(solution)/shard_map/ppermute | solution.py:385
  61.0 5.7 %collective-permute-start.4 = (f32[32,128]{1,0:T(8,128)S(1)}, f32[32,128]{1,0:T(8,128)S(1)}, u32[]{:S(2)}, u32[]{:S(2)}) collective-permute-start(f32[32,128]{1,0:T(8,128)S(1)} %convert_reduce_fusion), channel_id=1, source_target_pairs={{0,1},{1,2},{2,3},{3,0},{4,5},{5,6},{6,7},{7,4},{8,9},{9,10},{10,1... | collective-permute-start | bytes 49160 | tf_op jit(solution)/shard_map/ppermute | solution.py:385
  67.5 17.6 %all-to-all-start.1 = ((bf16[32,32,128]{2,1,0:T(8,128)(2,1)}), bf16[32,32,128]{2,1,0:T(8,128)(2,1)S(1)}, u32[]{:S(2)}, u32[]{:S(2)}) async-start(bf16[32,32,128]{2,1,0:T(8,128)(2,1)} %bitcast.12), calls=%async_computation.1 | async-start | bytes 524288 | tf_op jit(solution)/shard_map/all_to_all | solution.py:392
  75.1 1.1 %copy-start.6 = (bf16[8,144,192]{2,1,0:T(8,128)(2,1)S(1)}, bf16[8,144,192]{2,1,0:T(8,128)(2,1)}, u32[]{:S(2)}) copy-start(bf16[8,144,192]{2,1,0:T(8,128)(2,1)} %get-tuple-element.62.base_ref) | copy-start | bytes 1327108
  76.1 1.1 %copy-start.7 = (bf16[8,144,192]{2,1,0:T(8,128)(2,1)S(1)}, bf16[8,144,192]{2,1,0:T(8,128)(2,1)}, u32[]{:S(2)}) copy-start(bf16[8,144,192]{2,1,0:T(8,128)(2,1)} %get-tuple-element.63.gbase_ref) | copy-start | bytes 1327108
  85.1 5.3 %collective-permute-start.10 = (bf16[1024,128]{1,0:T(8,128)(2,1)S(1)}, bf16[1024,128]{1,0:T(8,128)(2,1)S(1)}, u32[]{:S(2)}, u32[]{:S(2)}) collective-permute-start(bf16[1024,128]{1,0:T(8,128)(2,1)S(1)} %bitcast.21), channel_id=1, source_target_pairs={{0,64},{64,0},{1,65},{65,1},{2,66},{66,2},{3,67},{67,3},{4,68},{68... | collective-permute-start | bytes 786440 | tf_op jit(solution)/shard_map/ppermute | solution.py:367

commit v6 on v5

--- a/solution.py
+++ b/solution.py
@@ -148,8 +148,8 @@
 def main_kernel(
     core_ref, wx_ref, gx_ref, lat_in, lon_in, diag_in, gain_ref, wqkv_ref, proj_ref,
     bias_hbm, sel_hbm,
-    att_ref, gi_ref, keep_ref, send_ref,
-    x_s, g_s, normed_s, inv_s, q_s, k_s, v_s, da_s, dq_s, dk_s, dv_s, hid_t, dsum_s, pay_s, bias_s, sel_s, sems,
+    att_far, gi_far, keep_ref, send_ref,
+    att_ref, gi_ref, x_s, g_s, normed_s, inv_s, q_s, k_s, v_s, da_s, dq_s, dk_s, dv_s, hid_t, dsum_s, pay_s, bias_s, sel_s, sems,
 ):
     bias_copy = pltpu.make_async_copy(bias_hbm, bias_s, sems.at[0])
     sel_copy = pltpu.make_async_copy(sel_hbm, sel_s, sems.at[1])
@@ -240,6 +240,8 @@
         dq_s[rows] = dot(eye_t, dq_t, 1, 1).astype(BF)
         gproj = gproj + dot(att_t, g_s[rows].astype(BF))
 
+    att_copy = pltpu.make_async_copy(att_ref, att_far, sems.at[2])
+    att_copy.start()
     g_gain = jnp.zeros((1, CH), F32)
     for rows in chunks:
         gh = (
@@ -257,6 +259,8 @@
         )
         gi_ref[rows] = gi.astype(BF)
 
+    gi_copy = pltpu.make_async_copy(gi_ref, gi_far, sems.at[3])
+    gi_copy.start()
     g_wide = [dot(hid_t[...], part[...]) for part in (dq_s, dk_s, dv_s)]
     weights = jnp.concatenate(g_wide + [gproj], axis=1)
     for j in range(WTILES):
@@ -280,6 +284,8 @@
     half_rows = PAY // 2
     keep_ref[...] = pay_s[pl.ds(pl.multiple_of(core * half_rows, half_rows), half_rows), :].astype(BF)
     send_ref[...] = pay_s[pl.ds(pl.multiple_of((1 - core) * half_rows, half_rows), half_rows), :].astype(BF)
+    att_copy.wait()
+    gi_copy.wait()
 
 
 def return_kernel(
@@ -394,7 +400,7 @@
     return mine, swapped(mine), outs
 
 
-def call(kernel, out_shape, scratch=(), smem=0, count=0, flops=0, far=0, room=12):
+def call(kernel, out_shape, scratch=(), smem=0, count=0, flops=0, far=0, room=12, far_out=()):
     specs = [pl.BlockSpec(memory_space=pltpu.SMEM)] * smem
     specs += [pl.BlockSpec(memory_space=pltpu.VMEM)] * (count - smem - far)
     specs += [pl.BlockSpec(memory_space=pl.ANY)] * far
@@ -402,7 +408,13 @@
         kernel,
         out_shape=out_shape,
         in_specs=specs,
-        out_specs=jax.tree.map(lambda _: pl.BlockSpec(memory_space=pltpu.VMEM), out_shape),
+        out_specs=jax.tree.unflatten(
+            jax.tree.structure(out_shape),
+            [
+                pl.BlockSpec(memory_space=pl.ANY if i in far_out else pltpu.VMEM)
+                for i in range(len(jax.tree.leaves(out_shape)))
+            ],
+        ),
         scratch_shapes=list(scratch),
         compiler_params=pltpu.CompilerParams(vmem_limit_bytes=room * MIB),
         cost_estimate=pl.CostEstimate(flops=flops, bytes_accessed=flops // 500, transcendentals=0),
@@ -459,8 +471,8 @@
     wide_b = pltpu.VMEM((tokens, CH), BF)
     att, gi, keep, send = call(
         main_kernel,
-        (token_shape, token_shape, half_shape, half_shape),
-        scratch=[wide_f, wide_f, wide_f, pltpu.VMEM((tokens, LANES), F32)]
+        (pltpu.HBM(token_shape.shape, BF), pltpu.HBM(token_shape.shape, BF), half_shape, half_shape),
+        scratch=[wide_b, wide_b, wide_f, wide_f, wide_f, pltpu.VMEM((tokens, LANES), F32)]
         + [wide_b] * 7
         + [
             pltpu.VMEM((CH, tokens), BF),
@@ -468,11 +480,12 @@
             pltpu.VMEM((PAY, LANES), F32),
             pltpu.VMEM(bias_shape, F32),
             pltpu.VMEM(sel.shape, BF),
-            pltpu.SemaphoreType.DMA((2,)),
+            pltpu.SemaphoreType.DMA((4,)),
         ],
         smem=1,
         count=11,
         far=2,
+        far_out=(0, 1),
         flops=10**10,
         room=28,
     )(core, wx, gx, lat_in, lon_in, diag_in, norm_gain.reshape(1, CH), wqkv, proj_weight, bias, sel)

time: 92.4 us -> 91.7 us (level)
    unnamed x23 -> x19, local copies, waits for them, and re-layouts: 3.85 us -> 3.04 us
where the time goes in v6:
time: 91.7 us; the launch traced here: 91.3 us
  starting transfers between devices  40.9 us (45%)
  Pallas kernels  26.8 us (29%)
  waiting for transfers between devices  17 us (19%)
  local copies, waits for them, and re-layouts  4.91 us (5%)
    ppermute x6, starting transfers between devices, passed(): return lax.ppermute(value, ('yhi', 'z', 'lat'), pairs)  16.3 us
    pallas_call x1, Pallas kernels, shards(): call(main_kernel, (pltpu.HBM(token_shape.shape, BF), pltpu.HBM(token_shap...  13.3 us
    all_to_all x1, starting transfers between devices, total_over_devices(): pieces = lax.all_to_all(half, wide, 0, 0, tiled=True)  7.64 us
    all_to_all x1, starting transfers between devices, total_over_devices(): mine = lax.all_to_all(spread, wide, 0, 0, tiled=True)  7.6 us
    ppermute x6, waiting for transfers between devices, passed(): return lax.ppermute(value, ('yhi', 'z', 'lat'), pairs)  6.48 us
    ppermute x2, starting transfers between devices, swapped(): return lax.ppermute(value, 'core', [(0, 1), (1, 0)])  5.92 us
    all_to_all x1, waiting for transfers between devices, total_over_devices(): mine = lax.all_to_all(spread, wide, 0, 0, tiled=True)  5.72 us
    pallas_call x1, Pallas kernels, give_back(): call(return_kernel, (plane_shape, plane_shape, lat_shape, edge_shape, edg...  4.07 us
  transfers between devices with their start and end apart: 13, of which 6 were waited for; matrix products, arithmetic and copies ran while one was open for 2% of the time, Pallas kernels for 10%

profile of v6, /device:TPU:1, one launch (start us, length us, event | category | flops | bytes accessed | tf_op | source)
XLA Modules:
  0.0 91.3 jit_solution(2546538625509621583)
XLA Ops:
  0.6 0.0 copy-start.8
  0.6 0.0 copy-start
  0.7 0.0 copy-start.1
  0.7 2.9 %shard_map.118 = (bf16[8,54,384]{2,1,0:T(8,128)(2,1)}, bf16[8,18,384]{2,1,0:T(8,128)(2,1)}, bf16[8,18,384]{2,1,0:T(8,128)(2,1)}) custom-call(bf16[8,144,192]{2,1,0:T(8,128)(2,1)} %bitcast.23, bf16[8,144,192]{2,1,0:T(8,128)(2,1)} %bitcast.26), custom_call_target="tpu_custom_call" | custom-call | flops 1000000000 | bytes 2000000 | tf_op jit(solution)/shard_map/pallas_call | solution.py:440
  3.6 3.4 %collective-permute-start = (bf16[8,54,384]{2,1,0:T(8,128)(2,1)}, bf16[8,54,384]{2,1,0:T(8,128)(2,1)S(1)}, u32[]{:S(2)}, u32[]{:S(2)}) collective-permute-start(bf16[8,54,384]{2,1,0:T(8,128)(2,1)} %get-tuple-element.41), channel_id=1, source_target_pairs={{0,3},{1,0},{2,1},{3,2},{4,7},{5,4},{6,5},{7,6},{8,11},{9,8},{10,9... | collective-permute-start | bytes 995336 | tf_op jit(solution)/shard_map/ppermute | solution.py:369
  6.9 8.2 %collective-permute-start.1 = (bf16[8,18,384]{2,1,0:T(8,128)(2,1)}, bf16[8,18,384]{2,1,0:T(8,128)(2,1)S(1)}, u32[]{:S(2)}, u32[]{:S(2)}) collective-permute-start(bf16[8,18,384]{2,1,0:T(8,128)(2,1)} %get-tuple-element.42), channel_id=1, source_target_pairs={{0,60},{1,61},{2,62},{3,63},{4,0},{5,1},{6,2},{7,3},{8,4},{9,5},{1... | collective-permute-start | bytes 331784 | tf_op jit(solution)/shard_map/ppermute | solution.py:369
  15.1 1.0 %collective-permute-start.2 = (bf16[8,18,384]{2,1,0:T(8,128)(2,1)}, bf16[8,18,384]{2,1,0:T(8,128)(2,1)}, u32[]{:S(2)}, u32[]{:S(2)}) collective-permute-start(bf16[8,18,384]{2,1,0:T(8,128)(2,1)} %get-tuple-element.43), channel_id=1, source_target_pairs={{0,63},{1,60},{2,61},{3,62},{4,3},{5,0},{6,1},{7,2},{8,7},{9,4},{1... | collective-permute-start | bytes 331784 | tf_op jit(solution)/shard_map/ppermute | solution.py:369
  16.1 0.0 copy-done.8
  16.1 0.9 copy.13
  17.0 1.1 %copy.14 = bf16[192,3,192]{2,0,1:T(8,128)(2,1)S(1)} copy(bf16[192,3,192]{0,2,1:T(8,128)(2,1)} %bitcast.30) | data formatting | bytes 442368 | tf_op jit(solution)/shard_map/reshape | solution.py:464
  18.2 0.0 copy-done
  18.2 0.0 copy-done.1
  18.2 0.0 copy-start.2
  18.2 0.0 copy-start.3
  18.2 0.0 copy-start.4
  18.2 0.0 copy-start.5
  18.2 2.8 %shard_map.119.bias_hbm = f32[7,576,128]{2,1,0:T(8,128)S(1)} custom-call(s32[1]{0:T(128)} %bitcast.6.last_ref, f32[24,1,3312]{2,1,0:T(1,128)S(1)} %bitcast.19, bf16[12,384,256]{2,1,0:T(8,128)(2,1)S(1)} %copy-done), custom_call_target="tpu_custom_call" | custom-call | flops 1000000000 | bytes 2000000 | tf_op jit(solution)/shard_map/pallas_call | solution.py:457
  21.0 0.0 collective-permute-done.1.lon_in
  21.1 0.0 collective-permute-done.2.diag_in
  21.1 0.0 collective-permute-done.lat_in
  21.1 13.3 %shard_map.120 = (bf16[1152,192]{1,0:T(8,128)(2,1)}, bf16[1152,192]{1,0:T(8,128)(2,1)}, bf16[1024,128]{1,0:T(8,128)(2,1)S(1)}, bf16[1024,128]{1,0:T(8,128)(2,1)S(1)}) custom-call(s32[1]{0:T(128)} %bitcast.core_ref, bf16[8,144,192]{2,1,0:T(8,128)(2,1)S(1)} %bitcast.25, bf16[8,144,192]{2,1,0:T(8,128)(2,1)S(1)} %bitcast.28, ...), custom_call_target="tpu_custom_call" | custom-call | flops 10000000000 | bytes 20000000 | tf_op jit(solution)/shard_map/pallas_call | solution.py:472
  34.4 1.7 %collective-permute-start.3 = (bf16[1024,128]{1,0:T(8,128)(2,1)S(1)}, bf16[1024,128]{1,0:T(8,128)(2,1)S(1)}, u32[]{:S(2)}, u32[]{:S(2)}) collective-permute-start(bf16[1024,128]{1,0:T(8,128)(2,1)S(1)} %get-tuple-element.45), channel_id=1, source_target_pairs={{0,64},{64,0},{1,65},{65,1},{2,66},{66,2},{3,67},{67,3},{4,68},{68... | collective-permute-start | bytes 786440 | tf_op jit(solution)/shard_map/ppermute | solution.py:373
  36.1 1.2 %collective-permute-done.3 = bf16[1024,128]{1,0:T(8,128)(2,1)S(1)} collective-permute-done((bf16[1024,128]{1,0:T(8,128)(2,1)S(1)}, bf16[1024,128]{1,0:T(8,128)(2,1)S(1)}, u32[]{:S(2)}, u32[]{:S(2)}) %collective-permute-start.3) | collective-permute-done | bytes 262176 | tf_op jit(solution)/shard_map/ppermute | solution.py:373
  37.3 0.8 add_convert_fusion
  38.1 7.6 %all-to-all-start = ((bf16[32,32,128]{2,1,0:T(8,128)(2,1)}), bf16[32,32,128]{2,1,0:T(8,128)(2,1)S(1)}, u32[]{:S(2)}, u32[]{:S(2)}) async-start(bf16[32,32,128]{2,1,0:T(8,128)(2,1)} %bitcast.8), calls=%async_computation | async-start | bytes 524288 | tf_op jit(solution)/shard_map/all_to_all | solution.py:382
  45.7 4.1 %shard_map.121 = (bf16[8,144,192]{2,1,0:T(8,128)(2,1)}, bf16[8,144,192]{2,1,0:T(8,128)(2,1)}, bf16[8,54,384]{2,1,0:T(8,128)(2,1)}, bf16[8,18,384]{2,1,0:T(8,128)(2,1)}, bf16[8,18,384]{2,1,0:T(8,128)(2,1)}) custom-call(bf16[8,144,192]{2,1,0:T(8,128)(2,1)} %bitcast.24, bf16[8,144,192]{2,1,0:T(8,128)(2,1)} %bitcast.27, ...), custom_call_target="tpu_custom_call" | custom-call | flops 2000000000 | bytes 4000000 | tf_op jit(solution)/shard_map/pallas_call | solution.py:494
  49.8 0.6 collective-permute-start.7
  50.4 1.0 %collective-permute-start.8 = (bf16[8,18,384]{2,1,0:T(8,128)(2,1)}, bf16[8,18,384]{2,1,0:T(8,128)(2,1)S(1)}, u32[]{:S(2)}, u32[]{:S(2)}) collective-permute-start(bf16[8,18,384]{2,1,0:T(8,128)(2,1)} %get-tuple-element.52), channel_id=1, source_target_pairs={{0,4},{1,5},{2,6},{3,7},{4,8},{5,9},{6,10},{7,11},{8,12},{9,13},{1... | collective-permute-start | bytes 331784 | tf_op jit(solution)/shard_map/ppermute | solution.py:369
  51.4 2.1 %collective-permute-start.9 = (bf16[8,18,384]{2,1,0:T(8,128)(2,1)}, bf16[8,18,384]{2,1,0:T(8,128)(2,1)S(1)}, u32[]{:S(2)}, u32[]{:S(2)}) collective-permute-start(bf16[8,18,384]{2,1,0:T(8,128)(2,1)} %get-tuple-element.53), channel_id=1, source_target_pairs={{0,5},{1,6},{2,7},{3,4},{4,9},{5,10},{6,11},{7,8},{8,13},{9,14},{1... | collective-permute-start | bytes 331784 | tf_op jit(solution)/shard_map/ppermute | solution.py:369
  53.5 2.5 %all-to-all-done = bf16[32,32,128]{2,1,0:T(8,128)(2,1)S(1)} async-done(((bf16[32,32,128]{2,1,0:T(8,128)(2,1)}), bf16[32,32,128]{2,1,0:T(8,128)(2,1)S(1)}, u32[]{:S(2)}, u32[]{:S(2)}) %all-to-all-start) | async-done | bytes 262176 | tf_op jit(solution)/shard_map/all_to_all | solution.py:382
  56.0 3.1 %collective-permute-start.6 = (f32[32,128]{1,0:T(8,128)S(1)}, f32[32,128]{1,0:T(8,128)S(1)}, u32[]{:S(2)}, u32[]{:S(2)}) collective-permute-start(f32[32,128]{1,0:T(8,128)S(1)} %convert_reduce_fusion), channel_id=1, source_target_pairs={{0,3},{1,0},{2,1},{3,2},{4,7},{5,4},{6,5},{7,6},{8,11},{9,8},{10,9... | collective-permute-start | bytes 49160 | tf_op jit(solution)/shard_map/ppermute | solution.py:391
  59.1 0.0 collective-permute-start.5
  59.1 1.2 %collective-permute-done.8.lon_in = bf16[8,18,384]{2,1,0:T(8,128)(2,1)S(1)} collective-permute-done((bf16[8,18,384]{2,1,0:T(8,128)(2,1)}, bf16[8,18,384]{2,1,0:T(8,128)(2,1)S(1)}, u32[]{:S(2)}, u32[]{:S(2)}) %collective-permute-start.8) | collective-permute-done | bytes 110624 | tf_op jit(solution)/shard_map/ppermute | solution.py:369
  60.3 0.4 collective-permute-start.4
  60.7 5.3 %collective-permute-done.9.diag_in = bf16[8,18,384]{2,1,0:T(8,128)(2,1)S(1)} collective-permute-done((bf16[8,18,384]{2,1,0:T(8,128)(2,1)}, bf16[8,18,384]{2,1,0:T(8,128)(2,1)S(1)}, u32[]{:S(2)}, u32[]{:S(2)}) %collective-permute-start.9) | collective-permute-done | bytes 110624 | tf_op jit(solution)/shard_map/ppermute | solution.py:369
  66.0 0.0 collective-permute-done.7.lat_in
  66.0 0.0 collective-permute-done.6
  66.0 0.0 collective-permute-done.5
  66.0 0.0 collective-permute-done.4
  66.0 0.7 broadcast_in_dim.2
  66.8 7.6 %all-to-all-start.1 = ((bf16[32,32,128]{2,1,0:T(8,128)(2,1)}), bf16[32,32,128]{2,1,0:T(8,128)(2,1)S(1)}, u32[]{:S(2)}, u32[]{:S(2)}) async-start(bf16[32,32,128]{2,1,0:T(8,128)(2,1)} %bitcast.12), calls=%async_computation.1 | async-start | bytes 524288 | tf_op jit(solution)/shard_map/all_to_all | solution.py:398
  74.4 1.1 %copy-done.6 = bf16[8,144,192]{2,1,0:T(8,128)(2,1)S(1)} copy-done((bf16[8,144,192]{2,1,0:T(8,128)(2,1)S(1)}, bf16[8,144,192]{2,1,0:T(8,128)(2,1)}, u32[]{:S(2)}) %copy-start.6) | copy-done | bytes 442392
  75.4 1.1 %copy-done.7 = bf16[8,144,192]{2,1,0:T(8,128)(2,1)S(1)} copy-done((bf16[8,144,192]{2,1,0:T(8,128)(2,1)S(1)}, bf16[8,144,192]{2,1,0:T(8,128)(2,1)}, u32[]{:S(2)}) %copy-start.7) | copy-done | bytes 442392
  76.5 2.1 %shard_map.122 = (bf16[8,144,192]{2,1,0:T(8,128)(2,1)}, bf16[8,144,192]{2,1,0:T(8,128)(2,1)}) custom-call(bf16[8,144,192]{2,1,0:T(8,128)(2,1)S(1)} %copy-done.6, bf16[8,144,192]{2,1,0:T(8,128)(2,1)S(1)} %copy-done.7, bf16[8,54,384]{2,1,0:T(8,128)(2,1)S(1)} %collective-permute-done.7.lat_in, bf16[8,18,384]{2,1,0:T(8,128)(2,1)S(1)} %collective-permute-done.8.lon_in, ...), custom_call_target="tpu_custom_call" | custom-call | flops 2000000000 | bytes 4000000 | tf_op jit(solution)/shard_map/pallas_call | solution.py:505
  78.6 5.7 %all-to-all-done.1 = bf16[32,32,128]{2,1,0:T(8,128)(2,1)S(1)} async-done(((bf16[32,32,128]{2,1,0:T(8,128)(2,1)}), bf16[32,32,128]{2,1,0:T(8,128)(2,1)S(1)}, u32[]{:S(2)}, u32[]{:S(2)}) %all-to-all-start.1) | async-done | bytes 262176 | tf_op jit(solution)/shard_map/all_to_all | solution.py:398
  84.4 4.2 %collective-permute-start.10 = (bf16[1024,128]{1,0:T(8,128)(2,1)S(1)}, bf16[1024,128]{1,0:T(8,128)(2,1)S(1)}, u32[]{:S(2)}, u32[]{:S(2)}) collective-permute-start(bf16[1024,128]{1,0:T(8,128)(2,1)S(1)} %bitcast.21), channel_id=1, source_target_pairs={{0,64},{64,0},{1,65},{65,1},{2,66},{66,2},{3,67},{67,3},{4,68},{68... | collective-permute-start | bytes 786440 | tf_op jit(solution)/shard_map/ppermute | solution.py:373
  88.5 1.2 %collective-permute-done.10.other_ref = bf16[1024,128]{1,0:T(8,128)(2,1)S(1)} collective-permute-done((bf16[1024,128]{1,0:T(8,128)(2,1)S(1)}, bf16[1024,128]{1,0:T(8,128)(2,1)S(1)}, u32[]{:S(2)}, u32[]{:S(2)}) %collective-permute-start.10) | collective-permute-done | bytes 262176 | tf_op jit(solution)/shard_map/ppermute | solution.py:373
  89.7 1.6 %shard_map.123 = (f32[192,576]{1,0:T(8,128)}, f32[192,192]{1,0:T(8,128)}, f32[1,192]{1,0:T(1,128)}, f32[24,1,3312]{2,1,0:T(1,128)}) custom-call(s32[1]{0:T(128)} %bitcast.core_ref, bf16[1024,128]{1,0:T(8,128)(2,1)S(1)} %bitcast.22, bf16[1024,128]{1,0:T(8,128)(2,1)S(1)} %collective-permute-done.10.other_ref), custom_call_target="tpu_custom_call" | custom-call | flops 1000000000 | bytes 2000000 | tf_op jit(solution)/shard_map/pallas_call | solution.py:509
  (8 shorter events, 0.1 us)
Async XLA Ops:
  0.6 15.5 %copy-start.8 = (bf16[192,576]{1,0:T(8,128)(2,1)S(1)}, bf16[192,576]{1,0:T(8,128)(2,1)}, u32[]{:S(2)}) copy-start(bf16[192,576]{1,0:T(8,128)(2,1)} %param.10) | copy-start | bytes 663556
  0.6 17.5 %copy-start = (bf16[12,384,256]{2,1,0:T(8,128)(2,1)S(1)}, bf16[12,384,256]{2,1,0:T(8,128)(2,1)}, u32[]{:S(2)}) copy-start(bf16[12,384,256]{2,1,0:T(8,128)(2,1)} %constant.38.clone.sel_ref.sel_hbm) | copy-start | bytes 7077892
  0.7 17.5 %copy-start.1 = (f32[4,1,6,3312]{3,1,2,0:T(1,128)S(1)}, f32[4,1,6,3312]{3,1,2,0:T(1,128)}, u32[]{:S(2)}) copy-start(f32[4,1,6,3312]{3,1,2,0:T(1,128)} %param.12) | copy-start | bytes 953860
  3.6 17.5 %collective-permute-start = (bf16[8,54,384]{2,1,0:T(8,128)(2,1)}, bf16[8,54,384]{2,1,0:T(8,128)(2,1)S(1)}, u32[]{:S(2)}, u32[]{:S(2)}) collective-permute-start(bf16[8,54,384]{2,1,0:T(8,128)(2,1)} %get-tuple-element.41), channel_id=1, source_target_pairs={{0,3},{1,0},{2,1},{3,2},{4,7},{5,4},{6,5},{7,6},{8,11},{9,8},{10,9... | collective-permute-start | bytes 995336 | tf_op jit(solution)/shard_map/ppermute | solution.py:369
  6.9 14.1 %collective-permute-start.1 = (bf16[8,18,384]{2,1,0:T(8,128)(2,1)}, bf16[8,18,384]{2,1,0:T(8,128)(2,1)S(1)}, u32[]{:S(2)}, u32[]{:S(2)}) collective-permute-start(bf16[8,18,384]{2,1,0:T(8,128)(2,1)} %get-tuple-element.42), channel_id=1, source_target_pairs={{0,60},{1,61},{2,62},{3,63},{4,0},{5,1},{6,2},{7,3},{8,4},{9,5},{1... | collective-permute-start | bytes 331784 | tf_op jit(solution)/shard_map/ppermute | solution.py:369
  15.1 5.9 %collective-permute-start.2 = (bf16[8,18,384]{2,1,0:T(8,128)(2,1)}, bf16[8,18,384]{2,1,0:T(8,128)(2,1)}, u32[]{:S(2)}, u32[]{:S(2)}) collective-permute-start(bf16[8,18,384]{2,1,0:T(8,128)(2,1)} %get-tuple-element.43), channel_id=1, source_target_pairs={{0,63},{1,60},{2,61},{3,62},{4,3},{5,0},{6,1},{7,2},{8,7},{9,4},{1... | collective-permute-start | bytes 331784 | tf_op jit(solution)/shard_map/ppermute | solution.py:369
  18.2 2.9 %copy-start.2 = (bf16[1,8,6,24,192]{4,3,2,1,0:T(8,128)(2,1)S(1)}, bf16[1,8,6,24,192]{4,3,2,1,0:T(8,128)(2,1)}, u32[]{:S(2)}) copy-start(bf16[1,8,6,24,192]{4,3,2,1,0:T(8,128)(2,1)} %param.7) | copy-start | bytes 1327108
  18.2 2.9 %copy-start.3 = (bf16[1,8,6,24,192]{4,3,2,1,0:T(8,128)(2,1)S(1)}, bf16[1,8,6,24,192]{4,3,2,1,0:T(8,128)(2,1)}, u32[]{:S(2)}) copy-start(bf16[1,8,6,24,192]{4,3,2,1,0:T(8,128)(2,1)} %param.8) | copy-start | bytes 1327108
  18.2 2.9 %copy-start.4 = (bf16[192,192]{1,0:T(8,128)(2,1)S(1)}, bf16[192,192]{1,0:T(8,128)(2,1)}, u32[]{:S(2)}) copy-start(bf16[192,192]{1,0:T(8,128)(2,1)} %proj_ref.3) | copy-start | bytes 221188
  18.2 2.9 %copy-start.5 = (f32[192]{0:T(256)S(1)}, f32[192]{0:T(256)}, u32[]{:S(2)}) copy-start(f32[192]{0:T(256)} %param.9) | copy-start | bytes 2308
  34.4 2.9 %collective-permute-start.3 = (bf16[1024,128]{1,0:T(8,128)(2,1)S(1)}, bf16[1024,128]{1,0:T(8,128)(2,1)S(1)}, u32[]{:S(2)}, u32[]{:S(2)}) collective-permute-start(bf16[1024,128]{1,0:T(8,128)(2,1)S(1)} %get-tuple-element.45), channel_id=1, source_target_pairs={{0,64},{64,0},{1,65},{65,1},{2,66},{66,2},{3,67},{67,3},{4,68},{68... | collective-permute-start | bytes 786440 | tf_op jit(solution)/shard_map/ppermute | solution.py:373
  38.1 17.9 %all-to-all-start = ((bf16[32,32,128]{2,1,0:T(8,128)(2,1)}), bf16[32,32,128]{2,1,0:T(8,128)(2,1)S(1)}, u32[]{:S(2)}, u32[]{:S(2)}) async-start(bf16[32,32,128]{2,1,0:T(8,128)(2,1)} %bitcast.8), calls=%async_computation | async-start | bytes 524288 | tf_op jit(solution)/shard_map/all_to_all | solution.py:382
  49.8 16.2 %collective-permute-start.7 = (bf16[8,54,384]{2,1,0:T(8,128)(2,1)}, bf16[8,54,384]{2,1,0:T(8,128)(2,1)S(1)}, u32[]{:S(2)}, u32[]{:S(2)}) collective-permute-start(bf16[8,54,384]{2,1,0:T(8,128)(2,1)} %get-tuple-element.51), channel_id=1, source_target_pairs={{0,1},{1,2},{2,3},{3,0},{4,5},{5,6},{6,7},{7,4},{8,9},{9,10},{10,1... | collective-permute-start | bytes 995336 | tf_op jit(solution)/shard_map/ppermute | solution.py:369
  50.4 10.0 %collective-permute-start.8 = (bf16[8,18,384]{2,1,0:T(8,128)(2,1)}, bf16[8,18,384]{2,1,0:T(8,128)(2,1)S(1)}, u32[]{:S(2)}, u32[]{:S(2)}) collective-permute-start(bf16[8,18,384]{2,1,0:T(8,128)(2,1)} %get-tuple-element.52), channel_id=1, source_target_pairs={{0,4},{1,5},{2,6},{3,7},{4,8},{5,9},{6,10},{7,11},{8,12},{9,13},{1... | collective-permute-start | bytes 331784 | tf_op jit(solution)/shard_map/ppermute | solution.py:369
  51.4 14.6 %collective-permute-start.9 = (bf16[8,18,384]{2,1,0:T(8,128)(2,1)}, bf16[8,18,384]{2,1,0:T(8,128)(2,1)S(1)}, u32[]{:S(2)}, u32[]{:S(2)}) collective-permute-start(bf16[8,18,384]{2,1,0:T(8,128)(2,1)} %get-tuple-element.53), channel_id=1, source_target_pairs={{0,5},{1,6},{2,7},{3,4},{4,9},{5,10},{6,11},{7,8},{8,13},{9,14},{1... | collective-permute-start | bytes 331784 | tf_op jit(solution)/shard_map/ppermute | solution.py:369
  56.0 9.9 %collective-permute-start.6 = (f32[32,128]{1,0:T(8,128)S(1)}, f32[32,128]{1,0:T(8,128)S(1)}, u32[]{:S(2)}, u32[]{:S(2)}) collective-permute-start(f32[32,128]{1,0:T(8,128)S(1)} %convert_reduce_fusion), channel_id=1, source_target_pairs={{0,3},{1,0},{2,1},{3,2},{4,7},{5,4},{6,5},{7,6},{8,11},{9,8},{10,9... | collective-permute-start | bytes 49160 | tf_op jit(solution)/shard_map/ppermute | solution.py:391
  59.1 6.8 %collective-permute-start.5 = (f32[32,128]{1,0:T(8,128)S(1)}, f32[32,128]{1,0:T(8,128)S(1)}, u32[]{:S(2)}, u32[]{:S(2)}) collective-permute-start(f32[32,128]{1,0:T(8,128)S(1)} %convert_reduce_fusion), channel_id=1, source_target_pairs={{0,2},{1,3},{2,0},{3,1},{4,6},{5,7},{6,4},{7,5},{8,10},{9,11},{10,... | collective-permute-start | bytes 49160 | tf_op jit(solution)/shard_map/ppermute | solution.py:391
  60.3 5.7 %collective-permute-start.4 = (f32[32,128]{1,0:T(8,128)S(1)}, f32[32,128]{1,0:T(8,128)S(1)}, u32[]{:S(2)}, u32[]{:S(2)}) collective-permute-start(f32[32,128]{1,0:T(8,128)S(1)} %convert_reduce_fusion), channel_id=1, source_target_pairs={{0,1},{1,2},{2,3},{3,0},{4,5},{5,6},{6,7},{7,4},{8,9},{9,10},{10,1... | collective-permute-start | bytes 49160 | tf_op jit(solution)/shard_map/ppermute | solution.py:391
  66.8 17.6 %all-to-all-start.1 = ((bf16[32,32,128]{2,1,0:T(8,128)(2,1)}), bf16[32,32,128]{2,1,0:T(8,128)(2,1)S(1)}, u32[]{:S(2)}, u32[]{:S(2)}) async-start(bf16[32,32,128]{2,1,0:T(8,128)(2,1)} %bitcast.12), calls=%async_computation.1 | async-start | bytes 524288 | tf_op jit(solution)/shard_map/all_to_all | solution.py:398
  74.4 1.1 %copy-start.6 = (bf16[8,144,192]{2,1,0:T(8,128)(2,1)S(1)}, bf16[8,144,192]{2,1,0:T(8,128)(2,1)}, u32[]{:S(2)}) copy-start(bf16[8,144,192]{2,1,0:T(8,128)(2,1)} %get-tuple-element.62.base_ref) | copy-start | bytes 1327108
  75.4 1.1 %copy-start.7 = (bf16[8,144,192]{2,1,0:T(8,128)(2,1)S(1)}, bf16[8,144,192]{2,1,0:T(8,128)(2,1)}, u32[]{:S(2)}) copy-start(bf16[8,144,192]{2,1,0:T(8,128)(2,1)} %get-tuple-element.63.gbase_ref) | copy-start | bytes 1327108
  84.4 5.3 %collective-permute-start.10 = (bf16[1024,128]{1,0:T(8,128)(2,1)S(1)}, bf16[1024,128]{1,0:T(8,128)(2,1)S(1)}, u32[]{:S(2)}, u32[]{:S(2)}) collective-permute-start(bf16[1024,128]{1,0:T(8,128)(2,1)S(1)} %bitcast.21), channel_id=1, source_target_pairs={{0,64},{64,0},{1,65},{65,1},{2,66},{66,2},{3,67},{67,3},{4,68},{68... | collective-permute-start | bytes 786440 | tf_op jit(solution)/shard_map/ppermute | solution.py:373

commit v7 on v6

--- a/solution.py
+++ b/solution.py
@@ -30,6 +30,7 @@
 BROW = WTILES * CH
 GROW = BROW + 3 * BIAS_ROWS
 PIECE = 32
+SPARE = 16
 HTILES = 7
 HLANES = HTILES * LANES
 CHUNK = 3 * LANES
@@ -121,10 +122,10 @@
         for g in range(GROUPS):
             z_i, a_i = divmod(g, WLAT)
             at = SPAN * (((z_i * WLEV + z_j) * WLAT + a_i) * WLAT + a_j)
-            block_s[m, :, g * SPAN : (g + 1) * SPAN] = flat_s[:, at : at + SPAN]
+            block_s[m, :, g * SPAN : (g + 1) * SPAN] = flat_s[:pairs, at : at + SPAN]
         for j in range(3):
             table_s[j, pl.ds(m, pairs, stride=GROUPS), :] = block_s[m, :, j * LANES : (j + 1) * LANES]
-    table = jnp.concatenate([table_s[j] for j in range(3)], axis=1)[:, : GROUPS * SPAN]
+    table = jnp.concatenate([table_s[j, :BIAS_ROWS] for j in range(3)], axis=1)[:, : GROUPS * SPAN]
     high, low = split(table)
     rows = levs * GROUPS
     row_id = lax.broadcasted_iota(jnp.int32, (BIAS_ROWS, TOK), 0)
@@ -270,7 +271,7 @@
     pay_s[GROW + 1 : GROW + 2, : CH - LANES] = g_gain[:, LANES:]
 
     sel_copy.wait()
-    lev_groups = dsum_s.shape[1] // WLON
+    lev_groups = BIAS_ROWS // HEADS
     g_bias = jnp.zeros((BIAS_ROWS, 3 * LANES), F32)
     for xj in range(WLON):
         wide = jnp.concatenate(
@@ -351,7 +352,7 @@
         for g in range(GROUPS):
             z_i, a_i = divmod(g, WLAT)
             to = SPAN * (((z_i * WLEV + z_j) * WLAT + a_i) * WLAT + a_j)
-            table_s[:, to : to + SPAN] = block[:, g * SPAN : (g + 1) * SPAN]
+            table_s[:pairs, to : to + SPAN] = block[:, g * SPAN : (g + 1) * SPAN]
     for h in range(HEADS):
         for lev in range(levs):
             r = h * levs + lev
@@ -452,12 +453,12 @@
     last = (lat_index == lat_count - 1).astype(jnp.int32).reshape(1)
     sel = jnp.asarray(lon_selectors(), BF)
     bias_rows = lev_windows * TOK
-    flat_shape = pltpu.VMEM((pairs, -(-entries // LANES) * LANES), F32)
-    bias_shape = (HTILES, bias_rows, LANES)
+    flat_shape = pltpu.VMEM((pairs + SPARE, -(-entries // LANES) * LANES), F32)
+    bias_shape = (HTILES, bias_rows + SPARE, LANES)
     bias = call(
         expand_kernel,
         sds(bias_shape, F32),
-        scratch=[flat_shape, pltpu.VMEM((GROUPS, pairs, 3 * LANES), F32), pltpu.VMEM((3, BIAS_ROWS, LANES), F32)],
+        scratch=[flat_shape, pltpu.VMEM((GROUPS, pairs, 3 * LANES), F32), pltpu.VMEM((3, BIAS_ROWS + SPARE, LANES), F32)],
         smem=1, count=3, flops=10**9,
     )(last, table, sel)
 

time: 91.7 us -> 91.5 us (level)
  no operation moved by 1% of the time
where the time goes in v7:
time: 91.5 us; the launch traced here: 91.1 us
  starting transfers between devices  40.9 us (45%)
  Pallas kernels  26.5 us (29%)
  waiting for transfers between devices  17.1 us (19%)
  local copies, waits for them, and re-layouts  4.91 us (5%)
    ppermute x6, starting transfers between devices, passed(): return lax.ppermute(value, ('yhi', 'z', 'lat'), pairs)  16.3 us
    pallas_call x1, Pallas kernels, shards(): call(main_kernel, (pltpu.HBM(token_shape.shape, BF), pltpu.HBM(token_shap...  13 us
    all_to_all x1, starting transfers between devices, total_over_devices(): pieces = lax.all_to_all(half, wide, 0, 0, tiled=True)  7.64 us
    all_to_all x1, starting transfers between devices, total_over_devices(): mine = lax.all_to_all(spread, wide, 0, 0, tiled=True)  7.59 us
    ppermute x6, waiting for transfers between devices, passed(): return lax.ppermute(value, ('yhi', 'z', 'lat'), pairs)  6.48 us
    ppermute x2, starting transfers between devices, swapped(): return lax.ppermute(value, 'core', [(0, 1), (1, 0)])  5.92 us
    all_to_all x1, waiting for transfers between devices, total_over_devices(): mine = lax.all_to_all(spread, wide, 0, 0, tiled=True)  5.73 us
    pallas_call x1, Pallas kernels, give_back(): call(return_kernel, (plane_shape, plane_shape, lat_shape, edge_shape, edg...  4.07 us
  transfers between devices with their start and end apart: 13, of which 6 were waited for; matrix products, arithmetic and copies ran while one was open for 2% of the time, Pallas kernels for 10%

profile of v7, /device:TPU:1, one launch (start us, length us, event | category | flops | bytes accessed | tf_op | source)
XLA Modules:
  0.0 91.1 jit_solution(4877206759284972651)
XLA Ops:
  0.6 0.0 copy-start.8
  0.6 0.0 copy-start
  0.7 0.0 copy-start.1
  0.7 2.9 %shard_map.118 = (bf16[8,54,384]{2,1,0:T(8,128)(2,1)}, bf16[8,18,384]{2,1,0:T(8,128)(2,1)}, bf16[8,18,384]{2,1,0:T(8,128)(2,1)}) custom-call(bf16[8,144,192]{2,1,0:T(8,128)(2,1)} %bitcast.23, bf16[8,144,192]{2,1,0:T(8,128)(2,1)} %bitcast.26), custom_call_target="tpu_custom_call" | custom-call | flops 1000000000 | bytes 2000000 | tf_op jit(solution)/shard_map/pallas_call | solution.py:441
  3.6 3.4 %collective-permute-start = (bf16[8,54,384]{2,1,0:T(8,128)(2,1)}, bf16[8,54,384]{2,1,0:T(8,128)(2,1)S(1)}, u32[]{:S(2)}, u32[]{:S(2)}) collective-permute-start(bf16[8,54,384]{2,1,0:T(8,128)(2,1)} %get-tuple-element.41), channel_id=1, source_target_pairs={{0,3},{1,0},{2,1},{3,2},{4,7},{5,4},{6,5},{7,6},{8,11},{9,8},{10,9... | collective-permute-start | bytes 995336 | tf_op jit(solution)/shard_map/ppermute | solution.py:370
  6.9 8.2 %collective-permute-start.1 = (bf16[8,18,384]{2,1,0:T(8,128)(2,1)}, bf16[8,18,384]{2,1,0:T(8,128)(2,1)S(1)}, u32[]{:S(2)}, u32[]{:S(2)}) collective-permute-start(bf16[8,18,384]{2,1,0:T(8,128)(2,1)} %get-tuple-element.42), channel_id=1, source_target_pairs={{0,60},{1,61},{2,62},{3,63},{4,0},{5,1},{6,2},{7,3},{8,4},{9,5},{1... | collective-permute-start | bytes 331784 | tf_op jit(solution)/shard_map/ppermute | solution.py:370
  15.1 1.0 %collective-permute-start.2 = (bf16[8,18,384]{2,1,0:T(8,128)(2,1)}, bf16[8,18,384]{2,1,0:T(8,128)(2,1)}, u32[]{:S(2)}, u32[]{:S(2)}) collective-permute-start(bf16[8,18,384]{2,1,0:T(8,128)(2,1)} %get-tuple-element.43), channel_id=1, source_target_pairs={{0,63},{1,60},{2,61},{3,62},{4,3},{5,0},{6,1},{7,2},{8,7},{9,4},{1... | collective-permute-start | bytes 331784 | tf_op jit(solution)/shard_map/ppermute | solution.py:370
  16.1 0.0 copy-done.8
  16.1 0.9 copy.13
  17.0 1.1 %copy.14 = bf16[192,3,192]{2,0,1:T(8,128)(2,1)S(1)} copy(bf16[192,3,192]{0,2,1:T(8,128)(2,1)} %bitcast.30) | data formatting | bytes 442368 | tf_op jit(solution)/shard_map/reshape | solution.py:465
  18.2 0.0 copy-done
  18.2 0.0 copy-done.1
  18.2 0.0 copy-start.2
  18.2 0.0 copy-start.3
  18.2 0.0 copy-start.4
  18.2 0.0 copy-start.5
  18.2 2.8 %shard_map.119.bias_hbm = f32[7,592,128]{2,1,0:T(8,128)S(1)} custom-call(s32[1]{0:T(128)} %bitcast.6.last_ref, f32[24,1,3312]{2,1,0:T(1,128)S(1)} %bitcast.19, bf16[12,384,256]{2,1,0:T(8,128)(2,1)S(1)} %copy-done), custom_call_target="tpu_custom_call" | custom-call | flops 1000000000 | bytes 2000000 | tf_op jit(solution)/shard_map/pallas_call | solution.py:458
  21.0 0.0 collective-permute-done.1.lon_in
  21.1 0.0 collective-permute-done.2.diag_in
  21.1 0.0 collective-permute-done.lat_in
  21.1 13.0 %shard_map.120 = (bf16[1152,192]{1,0:T(8,128)(2,1)}, bf16[1152,192]{1,0:T(8,128)(2,1)}, bf16[1024,128]{1,0:T(8,128)(2,1)S(1)}, bf16[1024,128]{1,0:T(8,128)(2,1)S(1)}) custom-call(s32[1]{0:T(128)} %bitcast.core_ref, bf16[8,144,192]{2,1,0:T(8,128)(2,1)S(1)} %bitcast.25, bf16[8,144,192]{2,1,0:T(8,128)(2,1)S(1)} %bitcast.28, ...), custom_call_target="tpu_custom_call" | custom-call | flops 10000000000 | bytes 20000000 | tf_op jit(solution)/shard_map/pallas_call | solution.py:473
  34.2 1.7 %collective-permute-start.3 = (bf16[1024,128]{1,0:T(8,128)(2,1)S(1)}, bf16[1024,128]{1,0:T(8,128)(2,1)S(1)}, u32[]{:S(2)}, u32[]{:S(2)}) collective-permute-start(bf16[1024,128]{1,0:T(8,128)(2,1)S(1)} %get-tuple-element.45), channel_id=1, source_target_pairs={{0,64},{64,0},{1,65},{65,1},{2,66},{66,2},{3,67},{67,3},{4,68},{68... | collective-permute-start | bytes 786440 | tf_op jit(solution)/shard_map/ppermute | solution.py:374
  35.9 1.2 %collective-permute-done.3 = bf16[1024,128]{1,0:T(8,128)(2,1)S(1)} collective-permute-done((bf16[1024,128]{1,0:T(8,128)(2,1)S(1)}, bf16[1024,128]{1,0:T(8,128)(2,1)S(1)}, u32[]{:S(2)}, u32[]{:S(2)}) %collective-permute-start.3) | collective-permute-done | bytes 262176 | tf_op jit(solution)/shard_map/ppermute | solution.py:374
  37.1 0.8 add_convert_fusion
  37.8 7.6 %all-to-all-start = ((bf16[32,32,128]{2,1,0:T(8,128)(2,1)}), bf16[32,32,128]{2,1,0:T(8,128)(2,1)S(1)}, u32[]{:S(2)}, u32[]{:S(2)}) async-start(bf16[32,32,128]{2,1,0:T(8,128)(2,1)} %bitcast.8), calls=%async_computation | async-start | bytes 524288 | tf_op jit(solution)/shard_map/all_to_all | solution.py:383
  45.5 4.1 %shard_map.121 = (bf16[8,144,192]{2,1,0:T(8,128)(2,1)}, bf16[8,144,192]{2,1,0:T(8,128)(2,1)}, bf16[8,54,384]{2,1,0:T(8,128)(2,1)}, bf16[8,18,384]{2,1,0:T(8,128)(2,1)}, bf16[8,18,384]{2,1,0:T(8,128)(2,1)}) custom-call(bf16[8,144,192]{2,1,0:T(8,128)(2,1)} %bitcast.24, bf16[8,144,192]{2,1,0:T(8,128)(2,1)} %bitcast.27, ...), custom_call_target="tpu_custom_call" | custom-call | flops 2000000000 | bytes 4000000 | tf_op jit(solution)/shard_map/pallas_call | solution.py:495
  49.6 0.6 collective-permute-start.7
  50.1 1.0 %collective-permute-start.8 = (bf16[8,18,384]{2,1,0:T(8,128)(2,1)}, bf16[8,18,384]{2,1,0:T(8,128)(2,1)S(1)}, u32[]{:S(2)}, u32[]{:S(2)}) collective-permute-start(bf16[8,18,384]{2,1,0:T(8,128)(2,1)} %get-tuple-element.52), channel_id=1, source_target_pairs={{0,4},{1,5},{2,6},{3,7},{4,8},{5,9},{6,10},{7,11},{8,12},{9,13},{1... | collective-permute-start | bytes 331784 | tf_op jit(solution)/shard_map/ppermute | solution.py:370
  51.1 2.1 %collective-permute-start.9 = (bf16[8,18,384]{2,1,0:T(8,128)(2,1)}, bf16[8,18,384]{2,1,0:T(8,128)(2,1)S(1)}, u32[]{:S(2)}, u32[]{:S(2)}) collective-permute-start(bf16[8,18,384]{2,1,0:T(8,128)(2,1)} %get-tuple-element.53), channel_id=1, source_target_pairs={{0,5},{1,6},{2,7},{3,4},{4,9},{5,10},{6,11},{7,8},{8,13},{9,14},{1... | collective-permute-start | bytes 331784 | tf_op jit(solution)/shard_map/ppermute | solution.py:370
  53.2 2.5 %all-to-all-done = bf16[32,32,128]{2,1,0:T(8,128)(2,1)S(1)} async-done(((bf16[32,32,128]{2,1,0:T(8,128)(2,1)}), bf16[32,32,128]{2,1,0:T(8,128)(2,1)S(1)}, u32[]{:S(2)}, u32[]{:S(2)}) %all-to-all-start) | async-done | bytes 262176 | tf_op jit(solution)/shard_map/all_to_all | solution.py:383
  55.8 3.1 %collective-permute-start.6 = (f32[32,128]{1,0:T(8,128)S(1)}, f32[32,128]{1,0:T(8,128)S(1)}, u32[]{:S(2)}, u32[]{:S(2)}) collective-permute-start(f32[32,128]{1,0:T(8,128)S(1)} %convert_reduce_fusion), channel_id=1, source_target_pairs={{0,3},{1,0},{2,1},{3,2},{4,7},{5,4},{6,5},{7,6},{8,11},{9,8},{10,9... | collective-permute-start | bytes 49160 | tf_op jit(solution)/shard_map/ppermute | solution.py:392
  58.9 0.0 collective-permute-start.5
  58.9 1.2 %collective-permute-done.8.lon_in = bf16[8,18,384]{2,1,0:T(8,128)(2,1)S(1)} collective-permute-done((bf16[8,18,384]{2,1,0:T(8,128)(2,1)}, bf16[8,18,384]{2,1,0:T(8,128)(2,1)S(1)}, u32[]{:S(2)}, u32[]{:S(2)}) %collective-permute-start.8) | collective-permute-done | bytes 110624 | tf_op jit(solution)/shard_map/ppermute | solution.py:370
  60.1 0.4 collective-permute-start.4
  60.5 5.3 %collective-permute-done.9.diag_in = bf16[8,18,384]{2,1,0:T(8,128)(2,1)S(1)} collective-permute-done((bf16[8,18,384]{2,1,0:T(8,128)(2,1)}, bf16[8,18,384]{2,1,0:T(8,128)(2,1)S(1)}, u32[]{:S(2)}, u32[]{:S(2)}) %collective-permute-start.9) | collective-permute-done | bytes 110624 | tf_op jit(solution)/shard_map/ppermute | solution.py:370
  65.7 0.0 collective-permute-done.7.lat_in
  65.8 0.0 collective-permute-done.6
  65.8 0.0 collective-permute-done.5
  65.8 0.0 collective-permute-done.4
  65.8 0.7 broadcast_in_dim.2
  66.5 7.6 %all-to-all-start.1 = ((bf16[32,32,128]{2,1,0:T(8,128)(2,1)}), bf16[32,32,128]{2,1,0:T(8,128)(2,1)S(1)}, u32[]{:S(2)}, u32[]{:S(2)}) async-start(bf16[32,32,128]{2,1,0:T(8,128)(2,1)} %bitcast.12), calls=%async_computation.1 | async-start | bytes 524288 | tf_op jit(solution)/shard_map/all_to_all | solution.py:399
  74.1 1.1 %copy-done.6 = bf16[8,144,192]{2,1,0:T(8,128)(2,1)S(1)} copy-done((bf16[8,144,192]{2,1,0:T(8,128)(2,1)S(1)}, bf16[8,144,192]{2,1,0:T(8,128)(2,1)}, u32[]{:S(2)}) %copy-start.6) | copy-done | bytes 442392
  75.2 1.1 %copy-done.7 = bf16[8,144,192]{2,1,0:T(8,128)(2,1)S(1)} copy-done((bf16[8,144,192]{2,1,0:T(8,128)(2,1)S(1)}, bf16[8,144,192]{2,1,0:T(8,128)(2,1)}, u32[]{:S(2)}) %copy-start.7) | copy-done | bytes 442392
  76.3 2.1 %shard_map.122 = (bf16[8,144,192]{2,1,0:T(8,128)(2,1)}, bf16[8,144,192]{2,1,0:T(8,128)(2,1)}) custom-call(bf16[8,144,192]{2,1,0:T(8,128)(2,1)S(1)} %copy-done.6, bf16[8,144,192]{2,1,0:T(8,128)(2,1)S(1)} %copy-done.7, bf16[8,54,384]{2,1,0:T(8,128)(2,1)S(1)} %collective-permute-done.7.lat_in, bf16[8,18,384]{2,1,0:T(8,128)(2,1)S(1)} %collective-permute-done.8.lon_in, ...), custom_call_target="tpu_custom_call" | custom-call | flops 2000000000 | bytes 4000000 | tf_op jit(solution)/shard_map/pallas_call | solution.py:506
  78.4 5.7 %all-to-all-done.1 = bf16[32,32,128]{2,1,0:T(8,128)(2,1)S(1)} async-done(((bf16[32,32,128]{2,1,0:T(8,128)(2,1)}), bf16[32,32,128]{2,1,0:T(8,128)(2,1)S(1)}, u32[]{:S(2)}, u32[]{:S(2)}) %all-to-all-start.1) | async-done | bytes 262176 | tf_op jit(solution)/shard_map/all_to_all | solution.py:399
  84.1 4.2 %collective-permute-start.10 = (bf16[1024,128]{1,0:T(8,128)(2,1)S(1)}, bf16[1024,128]{1,0:T(8,128)(2,1)S(1)}, u32[]{:S(2)}, u32[]{:S(2)}) collective-permute-start(bf16[1024,128]{1,0:T(8,128)(2,1)S(1)} %bitcast.21), channel_id=1, source_target_pairs={{0,64},{64,0},{1,65},{65,1},{2,66},{66,2},{3,67},{67,3},{4,68},{68... | collective-permute-start | bytes 786440 | tf_op jit(solution)/shard_map/ppermute | solution.py:374
  88.3 1.2 %collective-permute-done.10.other_ref = bf16[1024,128]{1,0:T(8,128)(2,1)S(1)} collective-permute-done((bf16[1024,128]{1,0:T(8,128)(2,1)S(1)}, bf16[1024,128]{1,0:T(8,128)(2,1)S(1)}, u32[]{:S(2)}, u32[]{:S(2)}) %collective-permute-start.10) | collective-permute-done | bytes 262176 | tf_op jit(solution)/shard_map/ppermute | solution.py:374
  89.5 1.6 %shard_map.123 = (f32[192,576]{1,0:T(8,128)}, f32[192,192]{1,0:T(8,128)}, f32[1,192]{1,0:T(1,128)}, f32[24,1,3312]{2,1,0:T(1,128)}) custom-call(s32[1]{0:T(128)} %bitcast.core_ref, bf16[1024,128]{1,0:T(8,128)(2,1)S(1)} %bitcast.22, bf16[1024,128]{1,0:T(8,128)(2,1)S(1)} %collective-permute-done.10.other_ref), custom_call_target="tpu_custom_call" | custom-call | flops 1000000000 | bytes 2000000 | tf_op jit(solution)/shard_map/pallas_call | solution.py:510
  (8 shorter events, 0.1 us)
Async XLA Ops:
  0.6 15.5 %copy-start.8 = (bf16[192,576]{1,0:T(8,128)(2,1)S(1)}, bf16[192,576]{1,0:T(8,128)(2,1)}, u32[]{:S(2)}) copy-start(bf16[192,576]{1,0:T(8,128)(2,1)} %param.10) | copy-start | bytes 663556
  0.6 17.5 %copy-start = (bf16[12,384,256]{2,1,0:T(8,128)(2,1)S(1)}, bf16[12,384,256]{2,1,0:T(8,128)(2,1)}, u32[]{:S(2)}) copy-start(bf16[12,384,256]{2,1,0:T(8,128)(2,1)} %constant.38.clone.sel_ref.sel_hbm) | copy-start | bytes 7077892
  0.7 17.5 %copy-start.1 = (f32[4,1,6,3312]{3,1,2,0:T(1,128)S(1)}, f32[4,1,6,3312]{3,1,2,0:T(1,128)}, u32[]{:S(2)}) copy-start(f32[4,1,6,3312]{3,1,2,0:T(1,128)} %param.12) | copy-start | bytes 953860
  3.6 17.5 %collective-permute-start = (bf16[8,54,384]{2,1,0:T(8,128)(2,1)}, bf16[8,54,384]{2,1,0:T(8,128)(2,1)S(1)}, u32[]{:S(2)}, u32[]{:S(2)}) collective-permute-start(bf16[8,54,384]{2,1,0:T(8,128)(2,1)} %get-tuple-element.41), channel_id=1, source_target_pairs={{0,3},{1,0},{2,1},{3,2},{4,7},{5,4},{6,5},{7,6},{8,11},{9,8},{10,9... | collective-permute-start | bytes 995336 | tf_op jit(solution)/shard_map/ppermute | solution.py:370
  6.9 14.1 %collective-permute-start.1 = (bf16[8,18,384]{2,1,0:T(8,128)(2,1)}, bf16[8,18,384]{2,1,0:T(8,128)(2,1)S(1)}, u32[]{:S(2)}, u32[]{:S(2)}) collective-permute-start(bf16[8,18,384]{2,1,0:T(8,128)(2,1)} %get-tuple-element.42), channel_id=1, source_target_pairs={{0,60},{1,61},{2,62},{3,63},{4,0},{5,1},{6,2},{7,3},{8,4},{9,5},{1... | collective-permute-start | bytes 331784 | tf_op jit(solution)/shard_map/ppermute | solution.py:370
  15.1 5.9 %collective-permute-start.2 = (bf16[8,18,384]{2,1,0:T(8,128)(2,1)}, bf16[8,18,384]{2,1,0:T(8,128)(2,1)}, u32[]{:S(2)}, u32[]{:S(2)}) collective-permute-start(bf16[8,18,384]{2,1,0:T(8,128)(2,1)} %get-tuple-element.43), channel_id=1, source_target_pairs={{0,63},{1,60},{2,61},{3,62},{4,3},{5,0},{6,1},{7,2},{8,7},{9,4},{1... | collective-permute-start | bytes 331784 | tf_op jit(solution)/shard_map/ppermute | solution.py:370
  18.2 2.9 %copy-start.2 = (bf16[1,8,6,24,192]{4,3,2,1,0:T(8,128)(2,1)S(1)}, bf16[1,8,6,24,192]{4,3,2,1,0:T(8,128)(2,1)}, u32[]{:S(2)}) copy-start(bf16[1,8,6,24,192]{4,3,2,1,0:T(8,128)(2,1)} %param.7) | copy-start | bytes 1327108
  18.2 2.9 %copy-start.3 = (bf16[1,8,6,24,192]{4,3,2,1,0:T(8,128)(2,1)S(1)}, bf16[1,8,6,24,192]{4,3,2,1,0:T(8,128)(2,1)}, u32[]{:S(2)}) copy-start(bf16[1,8,6,24,192]{4,3,2,1,0:T(8,128)(2,1)} %param.8) | copy-start | bytes 1327108
  18.2 2.9 %copy-start.4 = (bf16[192,192]{1,0:T(8,128)(2,1)S(1)}, bf16[192,192]{1,0:T(8,128)(2,1)}, u32[]{:S(2)}) copy-start(bf16[192,192]{1,0:T(8,128)(2,1)} %proj_ref.3) | copy-start | bytes 221188
  18.2 2.9 %copy-start.5 = (f32[192]{0:T(256)S(1)}, f32[192]{0:T(256)}, u32[]{:S(2)}) copy-start(f32[192]{0:T(256)} %param.9) | copy-start | bytes 2308
  34.2 2.9 %collective-permute-start.3 = (bf16[1024,128]{1,0:T(8,128)(2,1)S(1)}, bf16[1024,128]{1,0:T(8,128)(2,1)S(1)}, u32[]{:S(2)}, u32[]{:S(2)}) collective-permute-start(bf16[1024,128]{1,0:T(8,128)(2,1)S(1)} %get-tuple-element.45), channel_id=1, source_target_pairs={{0,64},{64,0},{1,65},{65,1},{2,66},{66,2},{3,67},{67,3},{4,68},{68... | collective-permute-start | bytes 786440 | tf_op jit(solution)/shard_map/ppermute | solution.py:374
  37.8 17.9 %all-to-all-start = ((bf16[32,32,128]{2,1,0:T(8,128)(2,1)}), bf16[32,32,128]{2,1,0:T(8,128)(2,1)S(1)}, u32[]{:S(2)}, u32[]{:S(2)}) async-start(bf16[32,32,128]{2,1,0:T(8,128)(2,1)} %bitcast.8), calls=%async_computation | async-start | bytes 524288 | tf_op jit(solution)/shard_map/all_to_all | solution.py:383
  49.6 16.2 %collective-permute-start.7 = (bf16[8,54,384]{2,1,0:T(8,128)(2,1)}, bf16[8,54,384]{2,1,0:T(8,128)(2,1)S(1)}, u32[]{:S(2)}, u32[]{:S(2)}) collective-permute-start(bf16[8,54,384]{2,1,0:T(8,128)(2,1)} %get-tuple-element.51), channel_id=1, source_target_pairs={{0,1},{1,2},{2,3},{3,0},{4,5},{5,6},{6,7},{7,4},{8,9},{9,10},{10,1... | collective-permute-start | bytes 995336 | tf_op jit(solution)/shard_map/ppermute | solution.py:370
  50.1 10.0 %collective-permute-start.8 = (bf16[8,18,384]{2,1,0:T(8,128)(2,1)}, bf16[8,18,384]{2,1,0:T(8,128)(2,1)S(1)}, u32[]{:S(2)}, u32[]{:S(2)}) collective-permute-start(bf16[8,18,384]{2,1,0:T(8,128)(2,1)} %get-tuple-element.52), channel_id=1, source_target_pairs={{0,4},{1,5},{2,6},{3,7},{4,8},{5,9},{6,10},{7,11},{8,12},{9,13},{1... | collective-permute-start | bytes 331784 | tf_op jit(solution)/shard_map/ppermute | solution.py:370
  51.1 14.6 %collective-permute-start.9 = (bf16[8,18,384]{2,1,0:T(8,128)(2,1)}, bf16[8,18,384]{2,1,0:T(8,128)(2,1)S(1)}, u32[]{:S(2)}, u32[]{:S(2)}) collective-permute-start(bf16[8,18,384]{2,1,0:T(8,128)(2,1)} %get-tuple-element.53), channel_id=1, source_target_pairs={{0,5},{1,6},{2,7},{3,4},{4,9},{5,10},{6,11},{7,8},{8,13},{9,14},{1... | collective-permute-start | bytes 331784 | tf_op jit(solution)/shard_map/ppermute | solution.py:370
  55.8 10.0 %collective-permute-start.6 = (f32[32,128]{1,0:T(8,128)S(1)}, f32[32,128]{1,0:T(8,128)S(1)}, u32[]{:S(2)}, u32[]{:S(2)}) collective-permute-start(f32[32,128]{1,0:T(8,128)S(1)} %convert_reduce_fusion), channel_id=1, source_target_pairs={{0,3},{1,0},{2,1},{3,2},{4,7},{5,4},{6,5},{7,6},{8,11},{9,8},{10,9... | collective-permute-start | bytes 49160 | tf_op jit(solution)/shard_map/ppermute | solution.py:392
  58.9 6.8 %collective-permute-start.5 = (f32[32,128]{1,0:T(8,128)S(1)}, f32[32,128]{1,0:T(8,128)S(1)}, u32[]{:S(2)}, u32[]{:S(2)}) collective-permute-start(f32[32,128]{1,0:T(8,128)S(1)} %convert_reduce_fusion), channel_id=1, source_target_pairs={{0,2},{1,3},{2,0},{3,1},{4,6},{5,7},{6,4},{7,5},{8,10},{9,11},{10,... | collective-permute-start | bytes 49160 | tf_op jit(solution)/shard_map/ppermute | solution.py:392
  60.1 5.7 %collective-permute-start.4 = (f32[32,128]{1,0:T(8,128)S(1)}, f32[32,128]{1,0:T(8,128)S(1)}, u32[]{:S(2)}, u32[]{:S(2)}) collective-permute-start(f32[32,128]{1,0:T(8,128)S(1)} %convert_reduce_fusion), channel_id=1, source_target_pairs={{0,1},{1,2},{2,3},{3,0},{4,5},{5,6},{6,7},{7,4},{8,9},{9,10},{10,1... | collective-permute-start | bytes 49160 | tf_op jit(solution)/shard_map/ppermute | solution.py:392
  66.5 17.6 %all-to-all-start.1 = ((bf16[32,32,128]{2,1,0:T(8,128)(2,1)}), bf16[32,32,128]{2,1,0:T(8,128)(2,1)S(1)}, u32[]{:S(2)}, u32[]{:S(2)}) async-start(bf16[32,32,128]{2,1,0:T(8,128)(2,1)} %bitcast.12), calls=%async_computation.1 | async-start | bytes 524288 | tf_op jit(solution)/shard_map/all_to_all | solution.py:399
  74.1 1.1 %copy-start.6 = (bf16[8,144,192]{2,1,0:T(8,128)(2,1)S(1)}, bf16[8,144,192]{2,1,0:T(8,128)(2,1)}, u32[]{:S(2)}) copy-start(bf16[8,144,192]{2,1,0:T(8,128)(2,1)} %get-tuple-element.62.base_ref) | copy-start | bytes 1327108
  75.2 1.1 %copy-start.7 = (bf16[8,144,192]{2,1,0:T(8,128)(2,1)S(1)}, bf16[8,144,192]{2,1,0:T(8,128)(2,1)}, u32[]{:S(2)}) copy-start(bf16[8,144,192]{2,1,0:T(8,128)(2,1)} %get-tuple-element.63.gbase_ref) | copy-start | bytes 1327108
  84.1 5.3 %collective-permute-start.10 = (bf16[1024,128]{1,0:T(8,128)(2,1)S(1)}, bf16[1024,128]{1,0:T(8,128)(2,1)S(1)}, u32[]{:S(2)}, u32[]{:S(2)}) collective-permute-start(bf16[1024,128]{1,0:T(8,128)(2,1)S(1)} %bitcast.21), channel_id=1, source_target_pairs={{0,64},{64,0},{1,65},{65,1},{2,66},{66,2},{3,67},{67,3},{4,68},{68... | collective-permute-start | bytes 786440 | tf_op jit(solution)/shard_map/ppermute | solution.py:374
